TPU v7x, 128 devices: a whole 4x4x4 slice. The times are simulated.
128 devices in a mesh: region: 8 (over y, core), dev: 16 (over z, x).
Axes of the slice: x: 4, y: 4, z: 4, core: 2. Of those that a mesh axis runs over, the one named last changes fastest.
Arguments:
- positions: float32 [3, 8192, 256], P(None, ('region', 'dev')), may hold values from 0 to 1
- velocity: float32 [3, 8192, 256], P(None, ('region', 'dev')), may hold values from -6 to 6
- smoothing: float32 [8192, 256], P(('region', 'dev')), may hold values from 0.25 to 0.5
- masses: float32 [8192, 256], P(('region', 'dev')), may hold values from 0.004 to 0.016
- energy: float32 [8192, 256], P(('region', 'dev')), may hold values from 0.5 to 2
- occupancy: int32 [8192], P(('region', 'dev')), may hold values from 128 to 256
- active: int32 [8192, 256], P(('region', 'dev')), may hold values 0 or 1
- send_cells: int32 [128, 16, 16], P(('region', 'dev')), may hold values from 0 to 63
- send_fill: int32 [128, 16], P(('region', 'dev')), may hold values from 0 to 16, as said below
- pair_cell: int32 [128, 16, 16], P(('region', 'dev')), may hold values from 0 to 63
Outputs:
- density: float32 [8192, 256], P(('region', 'dev'))
- forces: float32 [4, 8192, 256], P(None, ('region', 'dev'))
Inputs may be any that keep to these rules, and one draw needn't show every extreme that they name: `send_fill`: entry [d, j] is how many leading slots of device d's list for the device at index j of its region hold cells; it is 0 for d's own index, and in every region some device receives 16 cells from every other device of the region. Slots beyond it are ignored.
All inputs are finite; a program needn't handle non-finite values. No bound on the sum of `active` on one device may be relied on, other than what follows from the above.
Results may differ from a plain program's by a relative error of at most 0.0003.
Values sent between devices are 32-bit elements; how exact they have to be, the bound alone decides.
No kernel may reach another device: no remote copies, remote signals or barrier semaphores. Data moves between devices by JAX's collectives and lax.ppermute only.
A program may use at most 64 MiB of HBM per device.

v0:
```python
import math

import jax
import jax.numpy as jnp
from jax import lax
from jax.sharding import PartitionSpec as P

FACE = 4


KERNEL_NORM = 21.0 / (2.0 * math.pi)
GAMMA_LESS = 2.0 / 3.0
tile_slots = 4


def extended(block, sides, width):
    for axis, dim in sides:
        count = lax.axis_size(axis)
        forward = [(i, i + 1) for i in range(count - 1)]
        forward.append((count - 1, 0))
        backward = [(target, source) for source, target in forward]
        low = lax.ppermute(
            lax.slice_in_dim(block, block.shape[dim] - width, None, axis=dim), axis, forward
        )
        high = lax.ppermute(lax.slice_in_dim(block, 0, width, axis=dim), axis, backward)
        block = jnp.concatenate([low, block, high], axis=dim)
    return block


def kernel_terms(first_side, second_side):
    offsets = [
        first_side[:, axis_id, :, None] - second_side[:, axis_id, None, :] for axis_id in range(3)
    ]
    distance = jnp.sqrt(offsets[0] * offsets[0] + offsets[1] * offsets[1] + offsets[2] * offsets[2])
    support = 0.5 * (first_side[:, 6, :, None] + second_side[:, 6, None, :])
    scaled = distance / support
    remain = jnp.maximum(1.0 - scaled, 0.0)
    return (offsets, support, scaled, remain)


def density_pair(first_side, second_side):
    offsets, support, scaled, remain = kernel_terms(first_side, second_side)
    weight = KERNEL_NORM / (support * support * support) * remain**4 * (1.0 + 4.0 * scaled)
    to_first = jnp.sum(weight * second_side[:, 7, None, :], axis=2)
    to_second = jnp.sum(weight * first_side[:, 7, :, None], axis=1)
    return (to_first, to_second)


def force_pair(first_side, second_side, first_term, second_term):
    offsets, support, scaled, remain = kernel_terms(first_side, second_side)
    slope = -20.0 * KERNEL_NORM / support**5 * remain**3
    velocity_gap = [
        first_side[:, 3 + axis_id, :, None] - second_side[:, 3 + axis_id, None, :]
        for axis_id in range(3)
    ]
    closing = (
        velocity_gap[0] * offsets[0] + velocity_gap[1] * offsets[1] + velocity_gap[2] * offsets[2]
    )
    pushing = (first_term[:, :, None] + second_term[:, None, :]) * slope
    first_mass = first_side[:, 7, :, None]
    second_mass = second_side[:, 7, None, :]
    push_first = pushing * second_mass
    push_second = pushing * first_mass
    acc_first = jnp.stack(
        [-jnp.sum(push_first * offsets[axis_id], axis=2) for axis_id in range(3)], axis=1
    )
    acc_second = jnp.stack(
        [jnp.sum(push_second * offsets[axis_id], axis=1) for axis_id in range(3)], axis=1
    )
    heating = closing * slope
    heat_first = first_term * jnp.sum(heating * second_mass, axis=2)
    heat_second = second_term * jnp.sum(heating * first_mass, axis=1)
    return (
        jnp.concatenate([acc_first, heat_first[:, None]], axis=1),
        jnp.concatenate([acc_second, heat_second[:, None]], axis=1),
    )


def scatter_cells(index_table, values, cell_count):
    flat_index = index_table.reshape(-1)
    selector = (flat_index[None, :] == jnp.arange(cell_count, dtype=jnp.int32)[:, None]).astype(
        jnp.float32
    )
    flat_values = values.reshape(flat_index.shape[0], -1)
    summed = jnp.dot(selector, flat_values, precision=lax.Precision.HIGHEST)
    return summed.reshape((cell_count,) + values.shape[2:])


def block_counts(slot_live):
    filled = jnp.sum(slot_live, axis=1).astype(jnp.int32)
    return (filled + tile_slots - 1) // tile_slots


def blockwise(pair_fn, operands, counts, trailing):
    slot_count = operands[0].shape[1]
    slot_width = operands[0].shape[-1]

    def per_peer(members):
        pieces = members[:-1]
        blocks = members[-1]
        blank_totals = jnp.zeros((slot_count,) + trailing + (slot_width,), jnp.float32)

        def advance(step_id, totals):
            offset = step_id * tile_slots
            windows = [lax.dynamic_slice_in_dim(member, offset, tile_slots, 0) for member in pieces]
            first_out, second_out = pair_fn(*windows)
            return (
                lax.dynamic_update_slice_in_dim(totals[0], first_out, offset, 0),
                lax.dynamic_update_slice_in_dim(totals[1], second_out, offset, 0),
            )

        return lax.fori_loop(0, blocks, advance, (blank_totals, blank_totals))

    return lax.map(per_peer, tuple(operands) + (counts,))


def neighbour_copies(packed):
    cell_count = packed.shape[0]
    last_cut = (jnp.arange(cell_count) < cell_count - 1).astype(jnp.float32)
    feature_ids = jnp.arange(packed.shape[1])
    mass_cut = jnp.where(feature_ids[None, :, None] == 7, last_cut[:, None, None], 1.0)
    return (packed * mass_cut, jnp.roll(packed, -1, axis=0) * mass_cut)


def grouped_rows(member):
    return member.reshape((member.shape[0] // tile_slots, tile_slots) + member.shape[1:])


def local_density(packed):
    cell_count = packed.shape[0]
    first_copy, second_copy = neighbour_copies(packed)

    def per_group(members):
        own_total = density_pair(members[0], members[0])[0]
        first_out, second_out = density_pair(members[1], members[2])
        return (own_total + first_out, second_out)

    own_sums, second_sums = lax.map(
        per_group, (grouped_rows(packed), grouped_rows(first_copy), grouped_rows(second_copy))
    )
    return own_sums.reshape(cell_count, -1) + jnp.roll(
        second_sums.reshape(cell_count, -1), 1, axis=0
    )


def local_force(packed, pressure_term):
    cell_count = packed.shape[0]
    first_copy, second_copy = neighbour_copies(packed)
    rolled_term = jnp.roll(pressure_term, -1, axis=0)

    def per_group(members):
        own_total = force_pair(members[0], members[0], members[3], members[3])[0]
        first_out, second_out = force_pair(members[1], members[2], members[3], members[4])
        return (own_total + first_out, second_out)

    own_sums, second_sums = lax.map(
        per_group,
        (
            grouped_rows(packed),
            grouped_rows(first_copy),
            grouped_rows(second_copy),
            grouped_rows(pressure_term),
            grouped_rows(rolled_term),
        ),
    )
    shaped = (cell_count,) + own_sums.shape[2:]
    return own_sums.reshape(shaped) + jnp.roll(second_sums.reshape(shaped), 1, axis=0)


def return_density(partials):
    return lax.all_to_all(partials, "dev", split_axis=0, concat_axis=0, tiled=True)


def return_force(partials):
    return lax.all_to_all(partials, "dev", split_axis=0, concat_axis=0, tiled=True)


def face_rows(member, cell_count):
    return jnp.concatenate([member[:FACE], member[cell_count - FACE :]], axis=0)


def rim_rows(member, cell_count):
    return jnp.concatenate([member[:FACE], member[cell_count + FACE :]], axis=0)


def spread_faces(face_sums, cell_count):
    middle = jnp.zeros((cell_count - 2 * FACE,) + face_sums.shape[1:], jnp.float32)
    return jnp.concatenate([face_sums[:FACE], middle, face_sums[FACE:]], axis=0)


def local(
    positions,
    velocity,
    smoothing,
    masses,
    energy,
    occupancy,
    active,
    send_cells,
    send_fill,
    pair_cell,
):
    cell_count = masses.shape[0]
    slot_width = masses.shape[1]
    occupied = (jnp.arange(slot_width, dtype=jnp.int32)[None, :] < occupancy[:, None]).astype(
        jnp.float32
    )
    packed = jnp.concatenate(
        [
            jnp.transpose(positions, (1, 0, 2)),
            jnp.transpose(velocity, (1, 0, 2)),
            smoothing[:, None],
            (masses * occupied)[:, None],
            energy[:, None],
        ],
        axis=1,
    )
    slot_total = send_cells.shape[2]
    slot_live = (jnp.arange(slot_total, dtype=jnp.int32)[None, :] < send_fill[0][:, None]).astype(
        jnp.float32
    )
    feature_ids = jnp.arange(packed.shape[1])
    live_cut = jnp.where(feature_ids[None, None, :, None] == 7, slot_live[:, :, None, None], 1.0)
    outgoing = jnp.take(packed, send_cells[0], axis=0) * live_cut
    partner = jnp.take(packed, pair_cell[0], axis=0)
    arrived, arrived_live = (
        lax.all_to_all(outgoing, "dev", split_axis=0, concat_axis=0, tiled=True),
        lax.all_to_all(slot_live, "dev", split_axis=0, concat_axis=0, tiled=True),
    )
    counts = block_counts(arrived_live)
    mine_sums, their_sums = blockwise(density_pair, (partner, arrived), counts, ())
    returned = return_density(their_sums)
    cross_density = scatter_cells(pair_cell[0], mine_sums, cell_count) + scatter_cells(
        send_cells[0], returned * slot_live[:, :, None], cell_count
    )
    cycle_cells = extended(packed, (("region", 0),), FACE)
    face_own = face_rows(packed, cell_count)
    face_far = rim_rows(cycle_cells, cell_count)
    face_density = spread_faces(density_pair(face_own, face_far)[0], cell_count)
    density = (local_density(packed) + cross_density + face_density) * occupied
    pressure_term = jnp.where(
        occupied > 0.0, GAMMA_LESS * energy / jnp.where(occupied > 0.0, density, 1.0), 0.0
    )
    out_terms = jnp.take(pressure_term, send_cells[0], axis=0)
    partner_terms = jnp.take(pressure_term, pair_cell[0], axis=0)
    arrived_terms = lax.all_to_all(out_terms, "dev", split_axis=0, concat_axis=0, tiled=True)
    mine_force, their_force = blockwise(
        force_pair, (partner, arrived, partner_terms, arrived_terms), counts, (4,)
    )
    returned_force = return_force(their_force)
    cross_force = scatter_cells(pair_cell[0], mine_force, cell_count) + scatter_cells(
        send_cells[0], returned_force * slot_live[:, :, None, None], cell_count
    )
    cycle_terms = extended(pressure_term, (("region", 0),), FACE)
    face_force = force_pair(
        face_own, face_far, face_rows(pressure_term, cell_count), rim_rows(cycle_terms, cell_count)
    )[0]
    forces_total = (
        local_force(packed, pressure_term) + cross_force + spread_faces(face_force, cell_count)
    )
    gate = active.astype(jnp.float32) * occupied
    forces = jnp.transpose(forces_total, (1, 0, 2)) * gate[None]
    return (density, forces)


def solution(mesh):
    in_specs = (
        P(None, ("region", "dev"), None),
        P(None, ("region", "dev"), None),
        P(("region", "dev"), None),
        P(("region", "dev"), None),
        P(("region", "dev"), None),
        P(("region", "dev")),
        P(("region", "dev"), None),
        P(("region", "dev"), None, None),
        P(("region", "dev"), None),
        P(("region", "dev"), None, None),
    )
    out_specs = (P(("region", "dev"), None), P(None, ("region", "dev"), None))
    return jax.shard_map(local, mesh=mesh, in_specs=in_specs, out_specs=out_specs, check_vma=False)
```

profile of v0, /device:TPU:0, one launch (start us, length us, event | category | flops | bytes accessed | tf_op | source)
XLA Modules:
  0.0 827.2 jit_solution(6752008477462333512)
XLA Ops:
  9.8 8.0 all-to-all-start
  25.8 5.4 fusion.84
  32.9 7.2 all-to-all-start.1
  40.1 93.8 %while.72 = (s32[]{:T(128)}, f32[16,4,256]{2,1,0:T(4,128)}, f32[16,4,256]{2,1,0:T(4,128)}, f32[16,4,9,256]{3,1,2,0:T(4,128)}, f32[16,4,9,256]{3,1,2,0:T(4,128)}, /*index=5*/f32[16,4,9,256]{3,1,2,0:T(4,128)}, s32[]{:T(128)}) while((s32[]{:T(128)}, f32[16,4,256]{2,1,0:T(4,128)}, f32[16,4,256]{2,1,0:T(4,128)}, f32[16,4,9,256]{3,1,2,0:T(4,128)}, ...), condition=%wide.region_4.5_spmd, body=%wide.region_0.4_spmd.sunk | while | flops 13105154 | bytes 439381 | solution.py:138
  150.4 5.8 copy_select_fusion.1
  162.2 79.2 %while.74 = (s32[]{:T(128)}, f32[16,16,256]{2,1,0:T(8,128)S(1)}, f32[16,16,256]{2,1,0:T(8,128)}, s32[16]{0:T(128)S(1)}, f32[16,16,9,256]{3,1,2,0:T(8,128)}, /*in...) while((s32[]{:T(128)}, f32[16,16,256]{2,1,0:T(8,128)S(1)}, ...), condition=%wide.region_11.13_spmd, body=%wide.region_6.12_spmd.sunk | while | flops 6813708 | bytes 836656 | solution.py:114
  241.4 110.5 %all-to-all-start.2 = ((f32[16,16,256]{2,1,0:T(8,128)}), f32[16,16,256]{2,1,0:T(8,128)S(1)}, u32[]{:S(2)}, u32[]{:S(2)}) async-start(f32[16,16,256]{2,1,0:T(8,128)} %get-tuple-element.237), calls=%async_computation.2 | async-start | bytes 524288 | tf_op jit(solution)/shard_map/all_to_all | solution.py:171
  353.9 6.7 all-to-all-done.2
  366.7 128.3 %while.75 = (s32[]{:T(128)}, f32[16,4,4,256]{3,1,0,2:T(4,128)S(1)}, f32[16,4,4,256]{3,1,0,2:T(4,128)}, f32[16,4,256]{2,1,0:T(4,128)S(1)}, f32[16,4,9,256]{3,1,2,...) while((s32[]{:T(128)}, f32[16,4,4,256]{3,1,0,2:T(4,128)S(1)}, ...), condition=%wide.region_26.28_spmd, body=%wide.region_13.27_spmd.sunk | while | flops 23368704 | bytes 758389 | solution.py:156
  502.3 6.1 fusion.95
  510.0 117.3 %while.77 = (s32[]{:T(128)}, f32[16,16,4,256]{3,2,1,0:T(4,128)}, f32[16,16,4,256]{3,1,2,0:T(8,128)}, s32[16]{0:T(128)S(1)}, f32[16,16,9,256]{3,1,2,0:T(8,128)}, ...) while((s32[]{:T(128)}, f32[16,16,4,256]{3,2,1,0:T(4,128)}, ...), condition=%wide.region_38.41_spmd, body=%wide.region_27.40_spmd.sunk | while | flops 12866575 | bytes 1419012 | solution.py:114
  515.3 4.6 while.79
  522.9 4.6 while.79
  530.5 4.6 while.79
  538.0 4.6 while.79
  545.6 4.6 while.79
  553.2 4.6 while.79
  560.8 4.6 while.79
  575.9 4.6 while.79
  598.7 4.6 while.79
  613.8 4.6 while.79
  621.4 4.6 while.79
  627.3 182.6 %all-to-all-start.4 = ((f32[16,16,4,256]{3,1,2,0:T(8,128)}), f32[16,16,4,256]{3,1,2,0:T(8,128)S(1)}, u32[]{:S(2)}, u32[]{:S(2)}) async-start(f32[16,16,4,256]{3,1,2,0:T(8,128)} %get-tuple-element.241), calls=%async_computation.4 | async-start | bytes 2097152 | tf_op jit(solution)/shard_map/all_to_all | solution.py:175
  811.3 12.6 %all-to-all-done.4 = f32[16,16,4,256]{3,1,2,0:T(8,128)S(1)} async-done(((f32[16,16,4,256]{3,1,2,0:T(8,128)}), f32[16,16,4,256]{3,1,2,0:T(8,128)S(1)}, u32[]{:S(2)}, u32[]{:S(2)}) %all-to-all-start.4) | async-done | bytes 1048608 | tf_op jit(solution)/shard_map/all_to_all | solution.py:175
  (1119 shorter events, 498.8 us)
Async XLA Ops:
  4.8 14.5 %copy-start.15 = (s32[1,16,16]{2,1,0:T(8,128)S(1)}, s32[1,16,16]{2,1,0:T(8,128)}, u32[]{:S(2)}) copy-start(s32[1,16,16]{2,1,0:T(8,128)} %param.33) | copy-start | bytes 3076
  5.5 15.9 %copy-start.17 = (s32[1,16,16]{2,1,0:T(8,128)S(1)}, s32[1,16,16]{2,1,0:T(8,128)}, u32[]{:S(2)}) copy-start(s32[1,16,16]{2,1,0:T(8,128)} %param.35) | copy-start | bytes 3076
  6.1 151.0 %collective-permute-start = (f32[4,9,256]{2,1,0:T(8,128)}, f32[4,9,256]{2,1,0:T(8,128)}, u32[]{:S(2)}, u32[]{:S(2)}) collective-permute-start(f32[4,9,256]{2,1,0:T(8,128)} %get-tuple-element.489), channel_id=1, source_target_pairs={{0,16},{16,32},{32,48},{48,64},{64,80},{80,96},{96,112},{112,0},{1... | collective-permute-start | bytes 110600 | tf_op jit(solution)/shard_map/ppermute | solution.py:22
  6.1 151.8 %collective-permute-start.1 = (f32[4,9,256]{2,1,0:T(8,128)}, f32[4,9,256]{2,1,0:T(8,128)}, u32[]{:S(2)}, u32[]{:S(2)}) collective-permute-start(f32[4,9,256]{2,1,0:T(8,128)} %get-tuple-element.488), channel_id=1, source_target_pairs={{16,0},{32,16},{48,32},{64,48},{80,64},{96,80},{112,96},{0,112},{1... | collective-permute-start | bytes 110600 | tf_op jit(solution)/shard_map/ppermute | solution.py:25
  9.8 23.1 %all-to-all-start = ((f32[16,1,16]{2,1,0:T(1,128)}), f32[16,1,16]{2,1,0:T(1,128)}, u32[]{:S(2)}, u32[]{:S(2)}) async-start(f32[16,1,16]{2,1,0:T(1,128)} %compare_convert_fusion), calls=%async_computation | async-start | bytes 16384 | tf_op jit(solution)/shard_map/all_to_all | solution.py:228
  32.9 129.2 %all-to-all-start.1 = ((f32[16,16,9,256]{3,1,2,0:T(8,128)}), f32[16,16,9,256]{3,1,2,0:T(8,128)S(1)}, u32[]{:S(2)}, u32[]{:S(2)}) async-start(f32[16,16,9,256]{3,1,2,0:T(8,128)} %fusion.84), calls=%async_computation.1 | async-start | bytes 4718592 | tf_op jit(solution)/shard_map/all_to_all | solution.py:227
  40.0 93.8 %copy-start.18 = (s32[1,16,16]{2,1,0:T(8,128)S(1)}, s32[1,16,16]{2,1,0:T(8,128)}, u32[]{:S(2)}) copy-start(s32[1,16,16]{2,1,0:T(8,128)} %param.35) | copy-start | bytes 3076
  40.1 94.5 %copy-start.16 = (s32[1,16,16]{2,1,0:T(8,128)S(1)}, s32[1,16,16]{2,1,0:T(8,128)}, u32[]{:S(2)}) copy-start(s32[1,16,16]{2,1,0:T(8,128)} %param.33) | copy-start | bytes 3076
  149.7 211.0 %copy-start.53 = (f32[64]{0:T(128)}, f32[64]{0:T(128)S(1)}, u32[]{:S(2)}) copy-start(f32[64]{0:T(128)S(1)} %pad.38.clone) | copy-start | bytes 772
  162.1 191.6 %copy-start.27 = (s32[256]{0:T(256)S(1)}, s32[256]{0:T(256)}, u32[]{:S(2)}) copy-start(s32[256]{0:T(256)} %eq.64) | copy-start | bytes 3076
  162.1 198.6 %copy-start.9 = (f32[64,256]{1,0:T(8,128)S(1)}, f32[64,256]{1,0:T(8,128)}, u32[]{:S(2)}) copy-start(f32[64,256]{1,0:T(8,128)} %reshape.575) | copy-start | bytes 196612
  162.1 198.6 %copy-start.20 = (s32[64,256]{1,0:T(8,128)S(1)}, s32[64,256]{1,0:T(8,128)}, u32[]{:S(2)}) copy-start(s32[64,256]{1,0:T(8,128)} %param.32) | copy-start | bytes 196612
  162.1 198.6 %copy-start.25 = (s32[256]{0:T(256)S(1)}, s32[256]{0:T(256)}, u32[]{:S(2)}) copy-start(s32[256]{0:T(256)} %eq.68) | copy-start | bytes 3076
  162.1 198.6 %copy-start.51 = (s32[64]{0:T(128)S(1)}, s32[64]{0:T(128)}, u32[]{:S(2)}) copy-start(s32[64]{0:T(128)} %param.31) | copy-start | bytes 772
  162.1 198.6 %copy-start.52 = (f32[1,256]{1,0:T(1,128)S(1)}, f32[1,256]{1,0:T(1,128)}, u32[]{:S(2)}) copy-start(f32[1,256]{1,0:T(1,128)} %slice.402) | copy-start | bytes 3076
  241.4 120.3 %copy-start.56 = (s32[16]{0:T(128)}, s32[16]{0:T(128)S(1)}, u32[]{:S(2)}) copy-start(s32[16]{0:T(128)S(1)} %get-tuple-element.1312) | copy-start | bytes 196
  241.4 119.2 %all-to-all-start.2 = ((f32[16,16,256]{2,1,0:T(8,128)}), f32[16,16,256]{2,1,0:T(8,128)S(1)}, u32[]{:S(2)}, u32[]{:S(2)}) async-start(f32[16,16,256]{2,1,0:T(8,128)} %get-tuple-element.237), calls=%async_computation.2 | async-start | bytes 524288 | tf_op jit(solution)/shard_map/all_to_all | solution.py:171
  363.6 137.9 %collective-permute-start.2 = (f32[4,256]{1,0:T(4,128)S(1)}, f32[4,256]{1,0:T(4,128)S(1)}, u32[]{:S(2)}, u32[]{:S(2)}) collective-permute-start(f32[4,256]{1,0:T(4,128)S(1)} %get-tuple-element.511), channel_id=1, source_target_pairs={{0,16},{16,32},{32,48},{48,64},{64,80},{80,96},{96,112},{112,0},{1... | collective-permute-start | bytes 12296 | tf_op jit(solution)/shard_map/ppermute | solution.py:22
  363.7 137.8 %collective-permute-start.3 = (f32[4,256]{1,0:T(4,128)S(1)}, f32[4,256]{1,0:T(4,128)}, u32[]{:S(2)}, u32[]{:S(2)}) collective-permute-start(f32[4,256]{1,0:T(4,128)S(1)} %get-tuple-element.514), channel_id=1, source_target_pairs={{16,0},{32,16},{48,32},{64,48},{80,64},{96,80},{112,96},{0,112},{1... | collective-permute-start | bytes 12296 | tf_op jit(solution)/shard_map/ppermute | solution.py:25
  366.6 130.4 %copy-start.22 = (pred[16,16]{1,0:T(8,128)(4,1)S(1)}, pred[16,16]{1,0:T(8,128)(4,1)}, u32[]{:S(2)}) copy-start(pred[16,16]{1,0:T(8,128)(4,1)} %compare_and_fusion) | copy-start | bytes 772
  495.0 15.0 %copy-start.57 = (s32[16]{0:T(128)S(1)}, s32[16]{0:T(128)}, u32[]{:S(2)}) copy-start(s32[16]{0:T(128)} %copy-done.56) | copy-start | bytes 196
  497.8 12.2 %all-to-all-start.3 = ((f32[16,16,256]{2,1,0:T(8,128)}), f32[16,16,256]{2,1,0:T(8,128)S(1)}, u32[]{:S(2)}, u32[]{:S(2)}) async-start(f32[16,16,256]{2,1,0:T(8,128)} %broadcast_select_fusion), calls=%async_computation.3 | async-start | bytes 524288 | tf_op jit(solution)/shard_map/all_to_all | solution.py:246
  627.3 182.7 %copy-start.5 = (f32[16,16,4,256]{3,2,1,0:T(4,128)S(1)}, f32[16,16,4,256]{3,2,1,0:T(4,128)}, u32[]{:S(2)}) copy-start(f32[16,16,4,256]{3,2,1,0:T(4,128)} %get-tuple-element.240) | copy-start | bytes 3145732
  627.3 196.6 %all-to-all-start.4 = ((f32[16,16,4,256]{3,1,2,0:T(8,128)}), f32[16,16,4,256]{3,1,2,0:T(8,128)S(1)}, u32[]{:S(2)}, u32[]{:S(2)}) async-start(f32[16,16,4,256]{3,1,2,0:T(8,128)} %get-tuple-element.241), calls=%async_computation.4 | async-start | bytes 2097152 | tf_op jit(solution)/shard_map/all_to_all | solution.py:175
  (43 other events, 264.2 us)
where the time goes:
time: 836 us; the launch traced here: 827 us
  starting transfers between devices  318 us (38%)
  other arithmetic  260 us (31%)
  local copies, waits for them, and re-layouts  178 us (21%)
  loops' own time  45.9 us (5%)
  waiting for transfers between devices  20.8 us (2%)
    all_to_all x1, starting transfers between devices, return_force(): lax.all_to_all(partials, 'dev', split_axis=0, concat_axis=0, tiled=True)  183 us
    all_to_all x1, starting transfers between devices, return_density(): lax.all_to_all(partials, 'dev', split_axis=0, concat_axis=0, tiled=True)  110 us
    reduce_sum x31, other arithmetic, force_pair(): jnp.sum(push_second * offsets[axis_id], axis=1)  93.1 us
    squeeze x64, local copies, waits for them, and re-layouts, local_density(): lax.map(per_group, (grouped_rows(packed), grouped_rows(first_copy), group...  50.1 us
    reduce_sum x31, other arithmetic, density_pair(): to_second = jnp.sum(weight * first_side[:, 7, :, None], axis=1)  48.5 us
    reduce_sum x17, other arithmetic, force_pair(): jnp.sum(push_first * offsets[axis_id], axis=2)  48.3 us
    another operation x32, loops' own time, per_peer(): return lax.fori_loop(0, blocks, advance, (blank_totals, blank_totals))  43.4 us
    dynamic_update_slice x64, local copies, waits for them, and re-layouts, blockwise(): return lax.map(per_peer, tuple(operands) + (counts,))  30.6 us
  transfers between devices with their start and end apart: 9, of which 3 were waited for; matrix products, arithmetic and copies ran while one was open for 33% of the time, Pallas kernels for 0%

commit v1 on v0

v1 whole, which is shorter than its diff:
```python
import functools
import math

import jax
import jax.numpy as jnp
from jax import lax
from jax.experimental import pallas as pl
from jax.experimental.pallas import tpu as pltpu
from jax.sharding import PartitionSpec as P

BF = jnp.bfloat16
F32 = jnp.float32
FACE = 4
CELLS = 64
WIDTH = 256
PEERS = 16
SLOTS = 16
LISTED = PEERS * SLOTS
GAMMA_LESS = 2.0 / 3.0
W_SCALE = 84.0 / math.pi
G_SCALE = 6720.0 / math.pi
TINY = 1e-14
EMPTY = 1e8
CHUNK = 32
NN = (((1,), (0,)), ((), ()))
NT = (((1,), (1,)), ((), ()))
VM = pl.BlockSpec(memory_space=pltpu.VMEM)
SM = pl.BlockSpec(memory_space=pltpu.SMEM)
ROWS = 5


def params():
    return pltpu.CompilerParams(vmem_limit_bytes=50 * 2**20)


def split2(x):
    a = x.astype(BF)
    return a, (x - a.astype(F32)).astype(BF)


def split3(x):
    a = x.astype(BF).astype(F32)
    rest = x - a
    b = rest.astype(BF).astype(F32)
    return a, b, rest - b


def rows_of(cell):
    x, y, z, h, m = [cell[k : k + 1] for k in range(5)]
    norm = 4.0 * (x * x + y * y + z * z)
    root = lax.rsqrt(jnp.where(m > 0.0, m, 1.0))
    mu = jnp.where(m > 0.0, root * lax.rsqrt(root), EMPTY)
    return x, y, z, h, norm, mu


def first_rows(cell):
    x, y, z, h, norm, mu = rows_of(cell)
    one = jnp.ones_like(x)
    return jnp.concatenate(
        [-8.0 * x, -8.0 * y, -8.0 * z, norm, one, h * h * mu, 2.0 * h * mu, mu], 0
    )


def second_rows(cell):
    x, y, z, h, norm, mu = rows_of(cell)
    one = jnp.ones_like(x)
    return jnp.concatenate([x, y, z, one, norm, mu, h * mu, h * h * mu], 0)


def first_operand(rows):
    a1, a2, a3 = split3(rows)
    return jnp.concatenate([a1, a1, a2, a2, a1, a3, jnp.zeros((80, WIDTH), F32)], 0).T.astype(BF)


def second_operands(rows, both):
    b1, b2, b3 = split3(rows)
    stacked = jnp.concatenate([b1, b2, b1, b2, b3, b1, jnp.zeros((80, WIDTH), F32)], 0)
    part = lax.broadcasted_iota(jnp.int32, stacked.shape, 0) % 8
    near = jnp.where(part < 5, stacked, 0.0).astype(BF)
    if not both:
        return near
    return near, jnp.where(part >= 5, stacked, 0.0).astype(BF)


def support_columns(row):
    return jnp.broadcast_to(row, (128, WIDTH)).T


def density_weights(left, near, mixed, columns, row, one_sided):
    second = jnp.zeros((8, WIDTH), F32)
    firsts = []
    for start in range(0, WIDTH, CHUNK):
        part = left[start : start + CHUNK]
        s = jnp.dot(part, near, preferred_element_type=F32)
        mix = jnp.dot(part, mixed, preferred_element_type=F32)
        s = jnp.maximum(s, TINY)
        dist = s * lax.rsqrt(s)
        wide = columns[start : start + CHUNK]
        support = jnp.concatenate([wide, wide], 1) + row
        d = jnp.maximum(support - dist, 0.0)
        x = pl.reciprocal(mix, approx=True) * d
        x = x * x
        x = x * x
        w = x * (support + 4.0 * dist)
        for k in range(CHUNK // 8):
            second = second + w[8 * k : 8 * k + 8]
        if not one_sided:
            firsts.append(w[:, :128] + w[:, 128:])
    if one_sided:
        return second
    turned = jnp.concatenate(firsts, 0).T
    first = turned[:8]
    for k in range(1, 16):
        first = first + turned[8 * k : 8 * k + 8]
    return second, first


def inverse_mass(m):
    return jnp.where(m > 0.0, W_SCALE / jnp.where(m > 0.0, m, 1.0), 0.0)


def prepare_kernel(occ, pair, pos, vel, smooth, mass, own, out):
    lane = lax.broadcasted_iota(jnp.int32, (1, WIDTH), 1)

    def cell_step(c, _):
        one = pl.ds(c, 1)
        rows = [pos[k, one, :] - 0.5 for k in range(3)]
        rows.append(smooth[one, :])
        rows.append(jnp.where(lane < occ[c], mass[one, :], 0.0))
        rows += [vel[k, one, :] for k in range(3)]
        own[c] = jnp.concatenate(rows, 0)
        return 0

    lax.fori_loop(0, CELLS, cell_step, 0)

    def slot_step(p, _):
        out[p] = own[pair[p], 0:ROWS]
        return 0

    lax.fori_loop(0, LISTED, slot_step, 0)


def prepare(occ, pair, pos, vel, smooth, mass):
    return pl.pallas_call(
        prepare_kernel,
        in_specs=[SM, SM, VM, VM, VM, VM],
        out_specs=[VM, VM],
        out_shape=[
            jax.ShapeDtypeStruct((CELLS, 8, WIDTH), F32),
            jax.ShapeDtypeStruct((LISTED, ROWS, WIDTH), F32),
        ],
        compiler_params=params(),
    )(occ, pair, pos, vel, smooth, mass)


def local_density_kernel(own, rho, second, total):
    def cell_step(c, _):
        second[c] = second_rows(own[c])
        return 0

    lax.fori_loop(0, CELLS, cell_step, 0)
    empty = jnp.concatenate([jnp.zeros((4, WIDTH), F32)] + [jnp.ones((1, WIDTH), F32)], 0)
    second[CELLS] = second_rows(empty * jnp.zeros((ROWS, WIDTH), F32))
    total[...] = jnp.zeros_like(total)

    def pairs(c):
        cell = own[c]
        left = first_operand(first_rows(cell))
        columns = support_columns(cell[3:4])
        row_self = cell[3:4]
        near, mixed = second_operands(second[c], True)
        own_sum = density_weights(left, near, mixed, columns, row_self, True)
        after = jnp.minimum(c + 1, CELLS - 1)
        near, mixed = second_operands(second[c + 1], True)
        to_second, to_first = density_weights(left, near, mixed, columns, own[after, 3:4], False)
        return own_sum + to_first, to_second

    def step(i, _):
        here0, next0 = pairs(2 * i)
        here1, next1 = pairs(2 * i + 1)
        total[2 * i] += here0
        total[2 * i + 1] += here1 + next0
        total[2 * i + 2] += next1
        return 0

    lax.fori_loop(0, CELLS // 2, step, 0)

    def finish(c, _):
        rho[c] = jnp.sum(total[c], axis=0, keepdims=True) * inverse_mass(own[c, 4:5])
        return 0

    lax.fori_loop(0, CELLS, finish, 0)


def local_density(own):
    return pl.pallas_call(
        local_density_kernel,
        in_specs=[VM],
        out_specs=VM,
        out_shape=jax.ShapeDtypeStruct((CELLS, 1, WIDTH), F32),
        scratch_shapes=[
            pltpu.VMEM((CELLS + 1, 8, WIDTH), F32),
            pltpu.VMEM((CELLS + 2, 8, WIDTH), F32),
        ],
        cost_estimate=pl.CostEstimate(
            flops=127 * 65536 * 60, bytes_accessed=2 * 2**20, transcendentals=0
        ),
        compiler_params=params(),
    )(own)


def list_pairs(fill, cells, slot_of, cell_of):
    def peer_step(e, count):
        def slot_step(s, count):
            slot_of[count] = e * SLOTS + s
            cell_of[count] = cells[e * SLOTS + s]
            return count + 1

        return lax.fori_loop(0, fill[e], slot_step, count)

    count = lax.fori_loop(0, PEERS, peer_step, 0)
    for f in range(FACE):
        slot_of[count + f] = LISTED + f
        cell_of[count + f] = f
        slot_of[count + FACE + f] = LISTED + FACE + f
        cell_of[count + FACE + f] = CELLS - FACE + f
    for f in range(3):
        slot_of[count + 2 * FACE + f] = LISTED + 2 * FACE
        cell_of[count + 2 * FACE + f] = 0
    return (count + 2 * FACE + 3) // 4


def arrived_cell(slot, listed, faces):
    is_listed = slot < LISTED
    inner = listed[jnp.minimum(slot, LISTED - 1)]
    face = slot - LISTED
    outer = faces[jnp.clip(face, 0, 2 * FACE - 1), 0:ROWS]
    cell = jnp.where(is_listed, inner, outer)
    return jnp.where(face < 2 * FACE, cell, 0.0)


def cross_density_kernel(fill, cells, own, listed, faces, rho, back, total, slot_of, cell_of):
    total[...] = jnp.zeros_like(total)
    back[...] = jnp.zeros_like(back)
    trips = list_pairs(fill, cells, slot_of, cell_of)

    def pair(n):
        slot = slot_of[n]
        mine = own[cell_of[n]]
        other = arrived_cell(slot, listed, faces)
        left = first_operand(first_rows(mine))
        near, mixed = second_operands(second_rows(other), True)
        to_second, to_first = density_weights(
            left, near, mixed, support_columns(mine[3:4]), other[3:4], False
        )
        sent = jnp.sum(to_second, axis=0, keepdims=True) * inverse_mass(other[4:5])
        return slot, cell_of[n], to_first, sent

    def step(i, _):
        results = [pair(4 * i + k) for k in range(4)]
        for slot, cell, to_first, sent in results:
            total[cell] += to_first
            back[pl.ds(slot, 1), :] = sent
        return 0

    lax.fori_loop(0, trips, step, 0)

    def finish(c, _):
        rho[c] = jnp.sum(total[c], axis=0, keepdims=True) * inverse_mass(own[c, 4:5])
        return 0

    lax.fori_loop(0, CELLS, finish, 0)


def cross_density(fill, cells, own, listed, faces):
    return pl.pallas_call(
        cross_density_kernel,
        in_specs=[SM, SM, VM, VM, VM],
        out_specs=[VM, VM],
        out_shape=[
            jax.ShapeDtypeStruct((CELLS, 1, WIDTH), F32),
            jax.ShapeDtypeStruct((LISTED + 16, WIDTH), F32),
        ],
        scratch_shapes=[
            pltpu.VMEM((CELLS, 8, WIDTH), F32),
            pltpu.SMEM((LISTED + 16,), jnp.int32),
            pltpu.SMEM((LISTED + 16,), jnp.int32),
        ],
        cost_estimate=pl.CostEstimate(
            flops=80 * 65536 * 60, bytes_accessed=2 * 2**20, transcendentals=0
        ),
        compiler_params=params(),
    )(fill, cells, own, listed, faces)


def pressure_kernel(occ, pair, near, cross, returned, energy, own, density, term, out):
    lane = lax.broadcasted_iota(jnp.int32, (1, WIDTH), 1)
    term[...] = near[...] + cross[...]

    def slot_step(p, _):
        term[pair[p]] += returned[pl.ds(p, 1), :]
        return 0

    lax.fori_loop(0, LISTED, slot_step, 0)

    def cell_step(c, _):
        one = pl.ds(c, 1)
        full = lane < occ[c]
        rho = jnp.where(full, term[c], 0.0)
        density[one, :] = rho
        term[c] = jnp.where(full, GAMMA_LESS * energy[one, :] / jnp.where(full, rho, 1.0), 0.0)
        return 0

    lax.fori_loop(0, CELLS, cell_step, 0)

    def send_step(p, _):
        c = pair[p]
        out[p] = jnp.concatenate([own[c, 5:8], term[c]], 0)
        return 0

    lax.fori_loop(0, LISTED, send_step, 0)


def pressure(occ, pair, near, cross, returned, energy, own):
    return pl.pallas_call(
        pressure_kernel,
        in_specs=[SM, SM, VM, VM, VM, VM, VM],
        out_specs=[VM, VM, VM],
        out_shape=[
            jax.ShapeDtypeStruct((CELLS, WIDTH), F32),
            jax.ShapeDtypeStruct((CELLS, 1, WIDTH), F32),
            jax.ShapeDtypeStruct((LISTED, 4, WIDTH), F32),
        ],
        compiler_params=params(),
    )(occ, pair, near, cross, returned, energy, own)


def force_rows(cell, velocity, term):
    x, y, z, _, m = [cell[k : k + 1] for k in range(5)]
    u, v, w = [velocity[k : k + 1] for k in range(3)]
    mp = m * term
    blank = jnp.zeros_like(m)
    rows = jnp.concatenate(
        [m, m * x, m * y, m * z, mp, mp * x, mp * y, mp * z]
        + [m * u, m * v, m * w, m * (u * x + v * y + w * z)]
        + [blank] * 4,
        0,
    )
    high, low = split2(rows)
    return jnp.concatenate([high, low], 0)


def force_of(sums, cell, velocity, term):
    sums = sums[:16] + sums[16:]
    one, p_one = sums[0:1], sums[4:5]
    place, speed = cell[0:3], velocity
    acc = term * (place * one - sums[1:4]) + (place * p_one - sums[5:8])
    mixed = jnp.sum(
        speed * (place * one - sums[1:4]) - place * sums[8:11], axis=0, keepdims=True
    )
    rate = -term * (mixed + sums[11:12])
    return G_SCALE * jnp.concatenate([acc, rate], 0)


def slopes(left, near, columns, row, high, low):
    for start in range(0, WIDTH, CHUNK):
        s = jnp.dot(left[start : start + CHUNK], near, preferred_element_type=F32)
        s = jnp.maximum(s, TINY)
        dist = s * lax.rsqrt(s)
        wide = columns[start : start + CHUNK]
        support = jnp.concatenate([wide, wide], 1) + row
        d = jnp.maximum(support - dist, 0.0)
        e = pl.reciprocal(support * support, approx=True)
        x = e * d
        g = (x * x) * (x * e)
        top = g.astype(BF)
        high[start : start + CHUNK] = top
        low[start : start + CHUNK] = (g - top.astype(F32)).astype(BF)


def slope_sums(rows, high, low, dims):
    top = lax.dot_general(rows, high[...], dims, preferred_element_type=F32)
    return top + lax.dot_general(rows, low[...], dims, preferred_element_type=F32)


def local_force_kernel(start, stop, own, term, out, second, rows, total, *slots):
    def cell_step(c, _):
        cell = own[c]
        second[c] = second_rows(cell)
        rows[c] = force_rows(cell, cell[5:8], term[c])
        return 0

    lax.fori_loop(0, CELLS, cell_step, 0)
    second[CELLS] = second_rows(jnp.zeros((ROWS, WIDTH), F32))
    rows[CELLS] = jnp.zeros((32, WIDTH), BF)
    total[...] = jnp.zeros_like(total)

    def make(c, held):
        cell = own[c]
        left = first_operand(first_rows(cell))
        columns = support_columns(cell[3:4])
        slopes(left, second_operands(second[c], False), columns, cell[3:4], held[0], held[1])
        after = jnp.minimum(c + 1, CELLS - 1)
        slopes(
            left, second_operands(second[c + 1], False), columns, own[after, 3:4], held[2], held[3]
        )

    def use(c, held):
        mine, other = rows[c], rows[c + 1]
        total[c] += slope_sums(mine, held[0], held[1], NN) + slope_sums(other, held[2], held[3], NT)
        total[c + 1] += slope_sums(mine, held[2], held[3], NN)

    def step(i, _):
        make(2 * i, slots[:4])
        make(2 * i + 1, slots[4:])
        use(2 * i, slots[:4])
        use(2 * i + 1, slots[4:])
        return 0

    lax.fori_loop(start // 2, stop // 2, step, 0)

    def finish(c, _):
        cell = own[c]
        out[c] = force_of(total[c], cell, cell[5:8], term[c])
        return 0

    lax.fori_loop(0, CELLS, finish, 0)


def local_force(own, term, start, stop):
    return pl.pallas_call(
        functools.partial(local_force_kernel, start, stop),
        in_specs=[VM, VM],
        out_specs=VM,
        out_shape=jax.ShapeDtypeStruct((CELLS, 4, WIDTH), F32),
        scratch_shapes=[
            pltpu.VMEM((CELLS + 1, 8, WIDTH), F32),
            pltpu.VMEM((CELLS + 1, 32, WIDTH), BF),
            pltpu.VMEM((CELLS + 1, 32, WIDTH), F32),
        ]
        + [pltpu.VMEM((WIDTH, WIDTH), BF)] * 8,
        cost_estimate=pl.CostEstimate(
            flops=2 * (stop - start) * 65536 * 80, bytes_accessed=2 * 2**20, transcendentals=0
        ),
        compiler_params=params(),
    )(own, term)


def cross_force_kernel(
    fill, cells, own, term, listed, second_part, faces, face_terms, out, back,
    rows, total, slot_of, cell_of, *slots
):
    def cell_step(c, _):
        cell = own[c]
        rows[c] = force_rows(cell, cell[5:8], term[c])
        return 0

    lax.fori_loop(0, CELLS, cell_step, 0)
    total[...] = jnp.zeros_like(total)
    back[...] = jnp.zeros_like(back)
    trips = list_pairs(fill, cells, slot_of, cell_of)

    def make(n, held):
        slot = slot_of[n]
        mine = own[cell_of[n]]
        other = arrived_cell(slot, listed, faces)
        is_listed = slot < LISTED
        inner = second_part[jnp.minimum(slot, LISTED - 1)]
        face = jnp.clip(slot - LISTED, 0, 2 * FACE - 1)
        outer = jnp.concatenate([faces[face, 5:8], face_terms[face]], 0)
        moving = jnp.where(is_listed, inner, outer)
        left = first_operand(first_rows(mine))
        slopes(
            left, second_operands(second_rows(other), False), support_columns(mine[3:4]),
            other[3:4], held[0], held[1],
        )
        return slot, cell_of[n], other, moving

    def use(made, held):
        slot, cell, other, moving = made
        sums = slope_sums(rows[cell], held[0], held[1], NN)
        back[slot] = force_of(sums, other, moving[0:3], moving[3:4])
        theirs = force_rows(other, moving[0:3], moving[3:4])
        total[cell] += slope_sums(theirs, held[0], held[1], NT)

    def step(i, _):
        made = [make(4 * i + k, slots[2 * k : 2 * k + 2]) for k in range(4)]
        for k in range(4):
            use(made[k], slots[2 * k : 2 * k + 2])
        return 0

    lax.fori_loop(0, trips, step, 0)

    def finish(c, _):
        cell = own[c]
        out[c] = force_of(total[c], cell, cell[5:8], term[c])
        return 0

    lax.fori_loop(0, CELLS, finish, 0)


def cross_force(fill, cells, own, term, listed, second_part, faces, face_terms):
    return pl.pallas_call(
        cross_force_kernel,
        in_specs=[SM, SM] + [VM] * 6,
        out_specs=[VM, VM],
        out_shape=[
            jax.ShapeDtypeStruct((CELLS, 4, WIDTH), F32),
            jax.ShapeDtypeStruct((LISTED + 16, 4, WIDTH), F32),
        ],
        scratch_shapes=[
            pltpu.VMEM((CELLS, 32, WIDTH), BF),
            pltpu.VMEM((CELLS, 32, WIDTH), F32),
            pltpu.SMEM((LISTED + 16,), jnp.int32),
            pltpu.SMEM((LISTED + 16,), jnp.int32),
        ]
        + [pltpu.VMEM((WIDTH, WIDTH), BF)] * 8,
        cost_estimate=pl.CostEstimate(
            flops=80 * 65536 * 80, bytes_accessed=2 * 2**20, transcendentals=0
        ),
        compiler_params=params(),
    )(fill, cells, own, term, listed, second_part, faces, face_terms)


def finish_kernel(occ, pair, early, late, cross, returned, active, out, total):
    lane = lax.broadcasted_iota(jnp.int32, (1, WIDTH), 1)
    total[...] = early[...] + late[...] + cross[...]

    def slot_step(p, _):
        total[pair[p]] += returned[p]
        return 0

    lax.fori_loop(0, LISTED, slot_step, 0)

    def cell_step(c, _):
        one = pl.ds(c, 1)
        gate = jnp.where(lane < occ[c], active[one, :].astype(F32), 0.0)
        gated = total[c] * gate
        for k in range(4):
            out[k, one, :] = gated[k : k + 1]
        return 0

    lax.fori_loop(0, CELLS, cell_step, 0)


def finish(occ, pair, early, late, cross, returned, active):
    return pl.pallas_call(
        finish_kernel,
        in_specs=[SM, SM] + [VM] * 5,
        out_specs=VM,
        out_shape=jax.ShapeDtypeStruct((4, CELLS, WIDTH), F32),
        scratch_shapes=[pltpu.VMEM((CELLS, 4, WIDTH), F32)],
        compiler_params=params(),
    )(occ, pair, early, late, cross, returned, active)


def to_peers(block):
    flat = block.reshape((PEERS, -1, WIDTH))
    moved = lax.all_to_all(flat, "dev", split_axis=0, concat_axis=0, tiled=True)
    return moved.reshape(block.shape)


def with_neighbours(block):
    count = lax.axis_size("region")
    up = [(i, (i + 1) % count) for i in range(count)]
    down = [(i, (i - 1) % count) for i in range(count)]
    return jnp.concatenate(
        [
            lax.ppermute(block[CELLS - FACE :], "region", up),
            lax.ppermute(block[:FACE], "region", down),
        ],
        0,
    )


def local(
    positions, velocity, smoothing, masses, energy, occupancy, active, send_cells, send_fill,
    pair_cell,
):
    pair = pair_cell.reshape(-1)
    cells = send_cells.reshape(-1)
    fill = send_fill.reshape(-1)
    own, listed = prepare(occupancy, pair, positions, velocity, smoothing, masses)
    arrived = to_peers(listed)
    faces = with_neighbours(own)
    near_rho = local_density(own)
    cross_rho, back = cross_density(fill, cells, own, arrived, faces)
    returned = to_peers(back[:LISTED])
    density, term, moving = pressure(
        occupancy, pair, near_rho, cross_rho, returned, energy, own
    )
    arrived_moving = to_peers(moving)
    face_terms = with_neighbours(term)
    early = local_force(own, term, 0, CELLS // 2)
    cross, force_back = cross_force(
        fill, cells, own, term, arrived, arrived_moving, faces, face_terms
    )
    returned_force = to_peers(force_back[:LISTED])
    late = local_force(own, term, CELLS // 2, CELLS)
    forces = finish(occupancy, pair, early, late, cross, returned_force, active)
    return (density, forces)


def solution(mesh):
    cells = P(("region", "dev"), None)
    vectors = P(None, ("region", "dev"), None)
    lists = P(("region", "dev"), None, None)
    in_specs = (
        vectors, vectors, cells, cells, cells, P(("region", "dev")), cells, lists, cells, lists,
    )
    return jax.shard_map(
        local, mesh=mesh, in_specs=in_specs, out_specs=(cells, vectors), check_vma=False
    )
```

time: 836 us -> 209 us (0.25)
  starting transfers between devices: 318 us -> 28.5 us
  other arithmetic: 260 us -> 0.01 us
  local copies, waits for them, and re-layouts: 178 us -> 12.5 us
  Pallas kernels: 0 us -> 132 us
  loops' own time: 45.9 us -> 0 us
  waiting for transfers between devices: 20.8 us -> 31.2 us
    all_to_all x5 -> x4, starting transfers between devices: 312 us -> 22.6 us  [to_peers(): moved = lax.all_to_all(flat, 'dev', split_axis=0, concat_axis=0, tiled=True)]
    reduce_sum x97 -> x0, other arithmetic: 218 us -> none  [the longest x31 93.1 us: force_pair(): jnp.sum(push_second * offsets[axis_id], axis=1)]
    pallas_call x0 -> x8, Pallas kernels: none -> 132 us  [the longest x2 41.7 us: local_force(): pl.pallas_call(functools.partial(local_force_kernel, start, stop), in_spe...]
    squeeze x112 -> x0, local copies, waits for them, and re-layouts: 80 us -> none  [the longest x64 50.1 us: local_density(): lax.map(per_group, (grouped_rows(packed), grouped_rows(first_copy), group...]
    another operation x36 -> x0, loops' own time: 45.9 us -> none  [the longest x32 43.4 us: per_peer(): return lax.fori_loop(0, blocks, advance, (blank_totals, blank_totals))]
    dynamic_update_slice x110 -> x0, local copies, waits for them, and re-layouts: 40.6 us -> none  [the longest x64 30.6 us: blockwise(): return lax.map(per_peer, tuple(operands) + (counts,))]
    dynamic_slice x62 -> x0, local copies, waits for them, and re-layouts: 20.5 us -> none  [the longest x32 20.2 us: blockwise(): return lax.map(per_peer, tuple(operands) + (counts,))]
    dynamic_update_slice x63 -> x0, other arithmetic: 20.2 us -> none  [the longest x32 10.1 us: local_force(): lax.map(per_group, (grouped_rows(packed), grouped_rows(first_copy), group...]
  transfers between devices with their start and end apart: 9 -> 8, of which waited for: 3 -> 4; matrix products, arithmetic and copies ran while one was open for 33% -> 0% of each run, Pallas kernels for 0% -> 35%
where the time goes in v1:
time: 209 us; the launch traced here: 205 us
  Pallas kernels  132 us (63%)
  waiting for transfers between devices  31.2 us (15%)
  starting transfers between devices  28.5 us (14%)
  local copies, waits for them, and re-layouts  12.5 us (6%)
    pallas_call x2, Pallas kernels, local_force(): pl.pallas_call(functools.partial(local_force_kernel, start, stop), in_spe...  41.7 us
    pallas_call x1, Pallas kernels, local_density(): pl.pallas_call(local_density_kernel, in_specs=[VM], out_specs=VM, out_sha...  29.2 us
    pallas_call x1, Pallas kernels, cross_force(): pl.pallas_call(cross_force_kernel, in_specs=[SM, SM] + [VM] * 6, out_spec...  28.8 us
    all_to_all x4, waiting for transfers between devices, to_peers(): moved = lax.all_to_all(flat, 'dev', split_axis=0, concat_axis=0, tiled=True)  28.4 us
    all_to_all x4, starting transfers between devices, to_peers(): moved = lax.all_to_all(flat, 'dev', split_axis=0, concat_axis=0, tiled=True)  22.6 us
    pallas_call x1, Pallas kernels, cross_density(): pl.pallas_call(cross_density_kernel, in_specs=[SM, SM, VM, VM, VM], out_s...  19.3 us
    pallas_call x1, Pallas kernels, pressure(): pl.pallas_call(pressure_kernel, in_specs=[SM, SM, VM, VM, VM, VM, VM], ou...  6.52 us
    ppermute x2, starting transfers between devices, with_neighbours(): lax.ppermute(block[:FACE], 'region', down)  5.89 us
  transfers between devices with their start and end apart: 8, of which 4 were waited for; matrix products, arithmetic and copies ran while one was open for 0% of the time, Pallas kernels for 35%

profile of v1, /device:TPU:0, one launch (start us, length us, event | category | flops | bytes accessed | tf_op | source)
XLA Modules:
  0.0 205.1 jit_solution(3315846807798426197)
XLA Ops:
  1.4 0.9 copy-done.1
  2.3 0.9 copy-done.2
  5.6 2.7 %shard_map.113 = (f32[64,8,256]{2,1,0:T(8,128)S(1)}, f32[256,5,256]{2,1,0:T(8,128)S(1)}) custom-call(s32[64]{0:T(128)S(1)} %copy-done.7, s32[256]{0:T(256)S(1)} %reshape.37.pair, f32[3,64,256]{2,1,0:T(8,128)S(1)} %copy-done.1, f32[3,64,256]{2,1,0:T(8,128)S(1)} %copy-done.2, f32[64,256]{1,0:T(8,128)S(1)} %copy-done.3, f32[64,256]{1,0:T(8,128)S(1)} %copy-done.4), custom_call_target="tpu_custom_call" | custom-call | tf_op jit(solution)/shard_map/pallas_call | solution.py:144
  8.3 1.3 reshape.40
  9.6 8.1 %all-to-all-start = ((f32[16,80,256]{2,1,0:T(8,128)}), f32[16,80,256]{2,1,0:T(8,128)}, u32[]{:S(2)}, u32[]{:S(2)}) async-start(f32[16,80,256]{2,1,0:T(8,128)} %reshape.40), calls=%async_computation | async-start | bytes 2621440 | tf_op jit(solution)/shard_map/all_to_all | solution.py:559
  17.8 2.9 %collective-permute-start.1 = (f32[4,8,256]{2,1,0:T(8,128)S(1)}, f32[4,8,256]{2,1,0:T(8,128)S(1)}, u32[]{:S(2)}, u32[]{:S(2)}) collective-permute-start(f32[4,8,256]{2,1,0:T(8,128)S(1)} %get-tuple-element.20), channel_id=1, source_target_pairs={{0,112},{16,0},{32,16},{48,32},{64,48},{80,64},{96,80},{112,96},{1... | collective-permute-start | bytes 98312 | tf_op jit(solution)/shard_map/ppermute | solution.py:570
  20.9 1.5 collective-permute-done
  22.4 16.3 %all-to-all-done = f32[16,80,256]{2,1,0:T(8,128)} async-done(((f32[16,80,256]{2,1,0:T(8,128)}), f32[16,80,256]{2,1,0:T(8,128)}, u32[]{:S(2)}, u32[]{:S(2)}) %all-to-all-start) | async-done | bytes 1310752 | tf_op jit(solution)/shard_map/all_to_all | solution.py:559
  38.7 1.4 reshape.41.listed
  40.1 19.3 %shard_map.115 = (f32[64,1,256]{2,1,0:T(1,128)S(1)}, f32[272,256]{1,0:T(8,128)S(1)}) custom-call(s32[16]{0:T(128)S(1)} %bitcast.4, s32[256]{0:T(256)S(1)} %reshape.39.cells, f32[64,8,256]{2,1,0:T(8,128)S(1)} %get-tuple-element.11.own, f32[256,5,256]{2,1,0:T(8,128)S(1)} %reshape.41.listed, f32[8,8,256]{2,1,0:T(8,128)S(1)} %constant_dynamic-update-slice_fusion.faces), custom_call_target="tpu_custom_call" | custom-call | flops 314572800 | bytes 2097152 | tf_op jit(solution)/shard_map/pallas_call | solution.py:276
  60.1 3.7 %all-to-all-start.1 = ((f32[16,16,256]{2,1,0:T(8,128)}), f32[16,16,256]{2,1,0:T(8,128)S(1)}, u32[]{:S(2)}, u32[]{:S(2)}) async-start(f32[16,16,256]{2,1,0:T(8,128)} %bitcast.1), calls=%async_computation.1 | async-start | bytes 524288 | tf_op jit(solution)/shard_map/all_to_all | solution.py:559
  63.8 29.2 %shard_map.114.near = f32[64,1,256]{2,1,0:T(1,128)S(1)} custom-call(f32[64,8,256]{2,1,0:T(8,128)S(1)} %get-tuple-element.11.own), custom_call_target="tpu_custom_call" | custom-call | flops 499384320 | bytes 2097152 | tf_op jit(solution)/shard_map/pallas_call | solution.py:196
  93.0 6.5 %shard_map.116 = (f32[64,256]{1,0:T(8,128)}, f32[64,1,256]{2,1,0:T(1,128)S(1)}, f32[256,4,256]{2,1,0:T(4,128)S(1)}) custom-call(s32[64]{0:T(128)S(1)} %copy-done.8, s32[256]{0:T(256)S(1)} %reshape.37.pair, f32[64,1,256]{2,1,0:T(1,128)S(1)} %shard_map.114.near, f32[64,1,256]{2,1,0:T(1,128)S(1)} %get-tuple-element.13.cross, f32[256,256]{1,0:T(8,128)S(1)} %bitcast.3, ...), custom_call_target="tpu_custom_call" | custom-call | tf_op jit(solution)/shard_map/pallas_call | solution.py:325
  99.5 1.3 reshape.44
  100.9 7.2 %all-to-all-start.2 = ((f32[16,64,256]{2,1,0:T(8,128)}), f32[16,64,256]{2,1,0:T(8,128)S(1)}, u32[]{:S(2)}, u32[]{:S(2)}) async-start(f32[16,64,256]{2,1,0:T(8,128)} %reshape.44), calls=%async_computation.2 | async-start | bytes 2097152 | tf_op jit(solution)/shard_map/all_to_all | solution.py:559
  108.1 2.9 %collective-permute-start.3 = (f32[4,1,256]{2,1,0:T(1,128)S(1)}, f32[4,1,256]{2,1,0:T(1,128)S(1)}, u32[]{:S(2)}, u32[]{:S(2)}) collective-permute-start(f32[4,1,256]{2,1,0:T(1,128)S(1)} %get-tuple-element.23), channel_id=1, source_target_pairs={{0,112},{16,0},{32,16},{48,32},{64,48},{80,64},{96,80},{112,96},{1... | collective-permute-start | bytes 12296 | tf_op jit(solution)/shard_map/ppermute | solution.py:570
  111.0 1.3 collective-permute-done.2
  112.4 12.1 %all-to-all-done.2 = f32[16,64,256]{2,1,0:T(8,128)S(1)} async-done(((f32[16,64,256]{2,1,0:T(8,128)}), f32[16,64,256]{2,1,0:T(8,128)S(1)}, u32[]{:S(2)}, u32[]{:S(2)}) %all-to-all-start.2) | async-done | bytes 1048608 | tf_op jit(solution)/shard_map/all_to_all | solution.py:559
  124.8 28.8 %shard_map.119 = (f32[64,4,256]{2,1,0:T(4,128)S(1)}, f32[272,4,256]{2,1,0:T(4,128)S(1)}) custom-call(s32[16]{0:T(128)S(1)} %bitcast.5, s32[256]{0:T(256)S(1)} %reshape.39.cells, f32[64,8,256]{2,1,0:T(8,128)S(1)} %get-tuple-element.11.own, f32[64,1,256]{2,1,0:T(1,128)S(1)} %get-tuple-element.16.term, f32[256,5,256]{2,1,0:T(8,128)} %copy-done, ...), custom_call_target="tpu_custom_call" | custom-call | flops 419430400 | bytes 2097152 | tf_op jit(solution)/shard_map/pallas_call | solution.py:503
  153.8 1.4 reshape.46
  155.1 3.7 %all-to-all-start.3 = ((f32[16,64,256]{2,1,0:T(8,128)}), f32[16,64,256]{2,1,0:T(8,128)S(1)}, u32[]{:S(2)}, u32[]{:S(2)}) async-start(f32[16,64,256]{2,1,0:T(8,128)} %reshape.46), calls=%async_computation.3 | async-start | bytes 2097152 | tf_op jit(solution)/shard_map/all_to_all | solution.py:559
  158.8 20.8 %shard_map.118.late = f32[64,4,256]{2,1,0:T(4,128)S(1)} custom-call(f32[64,8,256]{2,1,0:T(8,128)S(1)} %get-tuple-element.11.own, f32[64,1,256]{2,1,0:T(1,128)S(1)} %get-tuple-element.16.term), custom_call_target="tpu_custom_call" | custom-call | flops 335544320 | bytes 2097152 | tf_op jit(solution)/shard_map/pallas_call | solution.py:431
  179.6 20.9 %shard_map.117.early = f32[64,4,256]{2,1,0:T(4,128)S(1)} custom-call(f32[64,8,256]{2,1,0:T(8,128)S(1)} %get-tuple-element.11.own, f32[64,1,256]{2,1,0:T(1,128)S(1)} %get-tuple-element.16.term), custom_call_target="tpu_custom_call" | custom-call | flops 335544320 | bytes 2097152 | tf_op jit(solution)/shard_map/pallas_call | solution.py:431
  201.3 3.8 %shard_map.120 = f32[4,64,256]{2,1,0:T(8,128)} custom-call(s32[64]{0:T(128)S(1)} %copy-done.8, s32[256]{0:T(256)S(1)} %reshape.37.pair, f32[64,4,256]{2,1,0:T(4,128)S(1)} %shard_map.117.early, f32[64,4,256]{2,1,0:T(4,128)S(1)} %shard_map.118.late, f32[64,4,256]{2,1,0:T(4,128)S(1)} %get-tuple-element.18.cross, f32[256,4,256]{2,1,0:T(4,128)S(1)} %reshape.47.returned, ...), custom_call_target="tpu_custom_call" | custom-call | tf_op jit(solution)/shard_map/pallas_call | solution.py:547
  (37 shorter events, 5.3 us)
Async XLA Ops:
  1.4 0.9 copy-start.1
  2.3 0.9 copy-start.2
  3.3 0.8 copy-start.3
  4.1 0.8 copy-start.4
  4.9 0.7 copy-start.7
  9.6 11.1 %copy-start.10 = (s32[1,16,16]{2,1,0:T(8,128)S(1)}, s32[1,16,16]{2,1,0:T(8,128)}, u32[]{:S(2)}) copy-start(s32[1,16,16]{2,1,0:T(8,128)} %param.17) | copy-start | bytes 3076
  9.6 29.0 %all-to-all-start = ((f32[16,80,256]{2,1,0:T(8,128)}), f32[16,80,256]{2,1,0:T(8,128)}, u32[]{:S(2)}, u32[]{:S(2)}) async-start(f32[16,80,256]{2,1,0:T(8,128)} %reshape.40), calls=%async_computation | async-start | bytes 2621440 | tf_op jit(solution)/shard_map/all_to_all | solution.py:559
  17.8 4.6 %collective-permute-start = (f32[4,8,256]{2,1,0:T(8,128)S(1)}, f32[4,8,256]{2,1,0:T(8,128)S(1)}, u32[]{:S(2)}, u32[]{:S(2)}) collective-permute-start(f32[4,8,256]{2,1,0:T(8,128)S(1)} %get-tuple-element.21), channel_id=1, source_target_pairs={{0,16},{16,32},{32,48},{48,64},{64,80},{80,96},{96,112},{112,0},{1... | collective-permute-start | bytes 98312 | tf_op jit(solution)/shard_map/ppermute | solution.py:569
  17.8 4.5 %collective-permute-start.1 = (f32[4,8,256]{2,1,0:T(8,128)S(1)}, f32[4,8,256]{2,1,0:T(8,128)S(1)}, u32[]{:S(2)}, u32[]{:S(2)}) collective-permute-start(f32[4,8,256]{2,1,0:T(8,128)S(1)} %get-tuple-element.20), channel_id=1, source_target_pairs={{0,112},{16,0},{32,16},{48,32},{64,48},{80,64},{96,80},{112,96},{1... | collective-permute-start | bytes 98312 | tf_op jit(solution)/shard_map/ppermute | solution.py:570
  22.4 17.7 %copy-start.9 = (s32[1,16]{1,0:T(1,128)S(1)}, s32[1,16]{1,0:T(1,128)}, u32[]{:S(2)}) copy-start(s32[1,16]{1,0:T(1,128)} %param.18) | copy-start | bytes 196
  40.1 19.3 %copy-start = (f32[256,5,256]{2,1,0:T(8,128)}, f32[256,5,256]{2,1,0:T(8,128)S(1)}, u32[]{:S(2)}) copy-start(f32[256,5,256]{2,1,0:T(8,128)S(1)} %reshape.41.listed) | copy-start | bytes 3932164
  60.1 32.9 %copy-start.5 = (f32[64,256]{1,0:T(8,128)S(1)}, f32[64,256]{1,0:T(8,128)}, u32[]{:S(2)}) copy-start(f32[64,256]{1,0:T(8,128)} %energy.1) | copy-start | bytes 196612
  60.1 32.9 %copy-start.8 = (s32[64]{0:T(128)S(1)}, s32[64]{0:T(128)}, u32[]{:S(2)}) copy-start(s32[64]{0:T(128)} %occ.5) | copy-start | bytes 772
  60.1 32.9 %all-to-all-start.1 = ((f32[16,16,256]{2,1,0:T(8,128)}), f32[16,16,256]{2,1,0:T(8,128)S(1)}, u32[]{:S(2)}, u32[]{:S(2)}) async-start(f32[16,16,256]{2,1,0:T(8,128)} %bitcast.1), calls=%async_computation.1 | async-start | bytes 524288 | tf_op jit(solution)/shard_map/all_to_all | solution.py:559
  100.9 23.6 %all-to-all-start.2 = ((f32[16,64,256]{2,1,0:T(8,128)}), f32[16,64,256]{2,1,0:T(8,128)S(1)}, u32[]{:S(2)}, u32[]{:S(2)}) async-start(f32[16,64,256]{2,1,0:T(8,128)} %reshape.44), calls=%async_computation.2 | async-start | bytes 2097152 | tf_op jit(solution)/shard_map/all_to_all | solution.py:559
  108.1 4.3 %collective-permute-start.2 = (f32[4,1,256]{2,1,0:T(1,128)S(1)}, f32[4,1,256]{2,1,0:T(1,128)S(1)}, u32[]{:S(2)}, u32[]{:S(2)}) collective-permute-start(f32[4,1,256]{2,1,0:T(1,128)S(1)} %get-tuple-element.22), channel_id=1, source_target_pairs={{0,16},{16,32},{32,48},{48,64},{64,80},{80,96},{96,112},{112,0},{1... | collective-permute-start | bytes 12296 | tf_op jit(solution)/shard_map/ppermute | solution.py:569
  108.1 4.3 %collective-permute-start.3 = (f32[4,1,256]{2,1,0:T(1,128)S(1)}, f32[4,1,256]{2,1,0:T(1,128)S(1)}, u32[]{:S(2)}, u32[]{:S(2)}) collective-permute-start(f32[4,1,256]{2,1,0:T(1,128)S(1)} %get-tuple-element.23), channel_id=1, source_target_pairs={{0,112},{16,0},{32,16},{48,32},{64,48},{80,64},{96,80},{112,96},{1... | collective-permute-start | bytes 12296 | tf_op jit(solution)/shard_map/ppermute | solution.py:570
  155.1 45.4 %all-to-all-start.3 = ((f32[16,64,256]{2,1,0:T(8,128)}), f32[16,64,256]{2,1,0:T(8,128)S(1)}, u32[]{:S(2)}, u32[]{:S(2)}) async-start(f32[16,64,256]{2,1,0:T(8,128)} %reshape.46), calls=%async_computation.3 | async-start | bytes 2097152 | tf_op jit(solution)/shard_map/all_to_all | solution.py:559
  200.5 0.8 copy-start.6

commit v2 on v1

v2 whole, which is shorter than its diff:
```python
import functools
import math

import jax
import jax.numpy as jnp
from jax import lax
from jax.experimental import pallas as pl
from jax.experimental.pallas import tpu as pltpu
from jax.sharding import PartitionSpec as P

BF = jnp.bfloat16
F32 = jnp.float32
FACE = 4
CELLS = 64
WIDTH = 256
PEERS = 16
SLOTS = 16
LISTED = PEERS * SLOTS
GAMMA_LESS = 2.0 / 3.0
W_SCALE = 84.0 / math.pi
G_SCALE = 6720.0 / math.pi
TINY = 1e-14
EMPTY = 1e8
CHUNK = 32
NN = (((1,), (0,)), ((), ()))
NT = (((1,), (1,)), ((), ()))
VM = pl.BlockSpec(memory_space=pltpu.VMEM)
SM = pl.BlockSpec(memory_space=pltpu.SMEM)
ROWS = 5
MOVING = 4
SPLIT = 40
LOCAL_ROWS = (160, 192, 224, 256)
CROSS_ROWS = (192, 256)
UNIT = 4
LOCAL_AT = 16
LOCAL_LIST = 72
CROSS_AT = LOCAL_AT + 2 * len(LOCAL_ROWS) * LOCAL_LIST
CROSS_LIST = LISTED + 16
PLAN = CROSS_AT + 2 * len(CROSS_ROWS) * CROSS_LIST
ANYWHERE = pl.BlockSpec(memory_space=pl.ANY)


def params():
    return pltpu.CompilerParams(vmem_limit_bytes=50 * 2**20)


def split2(x):
    a = x.astype(BF)
    return a, (x - a.astype(F32)).astype(BF)


def split3(x):
    a = x.astype(BF).astype(F32)
    rest = x - a
    b = rest.astype(BF).astype(F32)
    return a, b, rest - b


def rows_of(cell):
    x, y, z, h, m = [cell[k : k + 1] for k in range(5)]
    norm = 4.0 * (x * x + y * y + z * z)
    root = lax.rsqrt(jnp.where(m > 0.0, m, 1.0))
    mu = jnp.where(m > 0.0, root * lax.rsqrt(root), EMPTY)
    return x, y, z, h, norm, mu


def first_rows(cell):
    x, y, z, h, norm, mu = rows_of(cell)
    one = jnp.ones_like(x)
    return jnp.concatenate(
        [-8.0 * x, -8.0 * y, -8.0 * z, norm, one, h * h * mu, 2.0 * h * mu, mu], 0
    )


def second_rows(cell):
    x, y, z, h, norm, mu = rows_of(cell)
    one = jnp.ones_like(x)
    return jnp.concatenate([x, y, z, one, norm, mu, h * mu, h * h * mu], 0)


def first_operand(rows):
    a1, a2, a3 = split3(rows)
    return jnp.concatenate([a1, a1, a2, a2, a1, a3, jnp.zeros((80, WIDTH), F32)], 0).T.astype(BF)


def second_operands(rows, both):
    b1, b2, b3 = split3(rows)
    stacked = jnp.concatenate([b1, b2, b1, b2, b3, b1, jnp.zeros((80, WIDTH), F32)], 0)
    part = lax.broadcasted_iota(jnp.int32, stacked.shape, 0) % 8
    near = jnp.where(part < 5, stacked, 0.0).astype(BF)
    if not both:
        return near
    return near, jnp.where(part >= 5, stacked, 0.0).astype(BF)


def support_columns(row):
    return jnp.broadcast_to(row, (128, WIDTH)).T


def density_products(left, operands, count, s_ref, mix_ref):
    part = left[:count]
    s_ref[0:count] = jnp.dot(part, operands[0], preferred_element_type=F32)
    mix_ref[0:count] = jnp.dot(part, operands[1], preferred_element_type=F32)


def density_weights(count, s_ref, mix_ref, columns, row, one_sided):
    second = jnp.zeros((8, WIDTH), F32)
    firsts = []
    for start in range(0, count, CHUNK):
        s = jnp.maximum(s_ref[start : start + CHUNK], TINY)
        dist = s * lax.rsqrt(s)
        wide = columns[start : start + CHUNK]
        support = jnp.concatenate([wide, wide], 1) + row
        d = jnp.maximum(support - dist, 0.0)
        x = pl.reciprocal(mix_ref[start : start + CHUNK], approx=True) * d
        x = x * x
        x = x * x
        w = x * (support + 4.0 * dist)
        for k in range(CHUNK // 8):
            second = second + w[8 * k : 8 * k + 8]
        if not one_sided:
            firsts.append(w[:, :128] + w[:, 128:])
    if one_sided:
        return second
    if count < WIDTH:
        firsts.append(jnp.zeros((WIDTH - count, 128), F32))
    turned = jnp.concatenate(firsts, 0).T
    first = turned[:8]
    for k in range(1, 16):
        first = first + turned[8 * k : 8 * k + 8]
    return second, first


def inverse_mass(m):
    return jnp.where(m > 0.0, W_SCALE / jnp.where(m > 0.0, m, 1.0), 0.0)


def make_plan(occ, fill, cells, plan):
    for k in range(LOCAL_AT):
        plan[k] = 0
    classes = len(LOCAL_ROWS)

    def local_step(c, _):
        size = occ[c]
        kind = sum((size > rows).astype(jnp.int32) for rows in LOCAL_ROWS[:-1])
        kind = kind + jnp.where(c >= SPLIT, classes, 0)
        count = plan[kind]
        plan[LOCAL_AT + kind * LOCAL_LIST + count] = c
        plan[kind] = count + 1
        return 0

    lax.fori_loop(0, CELLS, local_step, 0)
    for kind in range(2 * classes):
        count = plan[kind]
        plan[LOCAL_AT + kind * LOCAL_LIST + count] = CELLS
        plan[kind] = (count + 1) // 2

    base = 2 * classes

    unused = jnp.int32(0)
    for e in range(PEERS):
        unused = jnp.where(fill[0, e] == 0, e * SLOTS, unused)
    for kind in range(len(CROSS_ROWS)):
        at = CROSS_AT + 2 * kind * CROSS_LIST
        for k in range(UNIT - 1):
            plan[at + k] = unused
            plan[at + CROSS_LIST + k] = CELLS

    def peer_step(e, counts):
        def slot_step(s, counts):
            cell = cells[e, s]
            wide = (occ[cell] > CROSS_ROWS[0]).astype(jnp.int32)
            at = CROSS_AT + 2 * wide * CROSS_LIST + jnp.where(wide > 0, counts[1], counts[0])
            plan[at + UNIT - 1] = e * SLOTS + s
            plan[at + CROSS_LIST + UNIT - 1] = cell
            return (counts[0] + 1 - wide, counts[1] + wide)

        return lax.fori_loop(0, fill[0, e], slot_step, counts)

    counts = lax.fori_loop(0, PEERS, peer_step, (jnp.int32(0), jnp.int32(0)))
    for kind in range(len(CROSS_ROWS)):
        trips = (counts[kind] + UNIT - 1) // UNIT
        plan[base + 2 * kind] = trips
        plan[base + 2 * kind + 1] = UNIT - 1 + counts[kind] - UNIT * trips


def fetch(pairs, sem):
    copies = [
        pltpu.make_async_copy(source, target, sem.at[k])
        for k, (source, target) in enumerate(pairs)
    ]
    for copy in copies:
        copy.start()
    return copies


def prepare_kernel(
    occ, fill, cells, pair, pos_in, vel_in, smooth_in, mass_in, own, out, plan,
    pos, vel, smooth, mass, sem,
):
    copies = fetch(
        [(pos_in, pos), (vel_in, vel), (smooth_in, smooth), (mass_in, mass)], sem
    )
    lane = lax.broadcasted_iota(jnp.int32, (1, WIDTH), 1)
    for copy in copies:
        copy.wait()

    def cell_step(c, _):
        one = pl.ds(c, 1)
        rows = [pos[k, one, :] - 0.5 for k in range(3)]
        rows.append(smooth[one, :])
        rows.append(jnp.where(lane < occ[c], mass[one, :], 0.0))
        rows += [vel[k, one, :] for k in range(3)]
        own[c] = jnp.concatenate(rows, 0)
        return 0

    lax.fori_loop(0, CELLS, cell_step, 0, unroll=8)
    own[CELLS] = jnp.zeros((8, WIDTH), F32)

    def peer_step(e, _):
        for s in range(SLOTS):
            out[e, s * ROWS : (s + 1) * ROWS] = own[pair[e, s], 0:ROWS]
        return 0

    lax.fori_loop(0, PEERS, peer_step, 0)
    make_plan(occ, fill, cells, plan)


def prepare(occ, fill, cells, pair, pos, vel, smooth, mass):
    return pl.pallas_call(
        prepare_kernel,
        in_specs=[SM] * 4 + [ANYWHERE] * 4,
        out_specs=[VM, VM, SM],
        out_shape=[
            jax.ShapeDtypeStruct((CELLS + 1, 8, WIDTH), F32),
            jax.ShapeDtypeStruct((PEERS, SLOTS * ROWS, WIDTH), F32),
            jax.ShapeDtypeStruct((PLAN,), jnp.int32),
        ],
        scratch_shapes=[
            pltpu.VMEM((3, CELLS, WIDTH), F32),
            pltpu.VMEM((3, CELLS, WIDTH), F32),
            pltpu.VMEM((CELLS, WIDTH), F32),
            pltpu.VMEM((CELLS, WIDTH), F32),
            pltpu.SemaphoreType.DMA((4,)),
        ],
        compiler_params=params(),
    )(occ, fill, cells, pair, pos, vel, smooth, mass)


def fold(total, own, cells, out, carried):
    def cell_step(c, _):
        mine = jnp.sum(total[c], axis=0, keepdims=True) * inverse_mass(own[c, 4:5])
        one = pl.ds(c, 1)
        out[one, :] = mine if carried is None else carried[one, :] + mine
        return 0

    lax.fori_loop(0, cells, cell_step, 0, unroll=8)


def local_density_kernel(part, plan, own, *rest):
    if part:
        faces, carried, rho, second, total, *slots = rest
    else:
        faces = carried = None
        rho, second, total, *slots = rest

    def cell_step(c, _):
        second[c] = second_rows(own[c])
        return 0

    lax.fori_loop(0, CELLS + 1, cell_step, 0, unroll=5)
    total[...] = jnp.zeros_like(total)

    def unit(count, places):
        plans = []
        for k, c in enumerate(places):
            after = jnp.minimum(c + 1, CELLS)
            left = first_operand(first_rows(own[c]))
            one, two = slots[4 * k : 4 * k + 2], slots[4 * k + 2 : 4 * k + 4]
            density_products(left, second_operands(second[c], True), count, *one)
            density_products(left, second_operands(second[after], True), count, *two)
            plans.append((c, after, one, two))
        sums = []
        for c, after, one, two in plans:
            row = own[c, 3:4]
            columns = support_columns(row)
            own_sum = density_weights(count, *one, columns, row, True)
            to_second, to_first = density_weights(
                count, *two, columns, own[after, 3:4], False
            )
            sums.append((c, after, own_sum + to_first, to_second))
        for c, after, here, there in sums:
            total[c] += here
            total[after] += there

    for kind, count in enumerate(LOCAL_ROWS):
        at = kind + part * len(LOCAL_ROWS)
        start = LOCAL_AT + at * LOCAL_LIST

        def step(i, _):
            unit(count, [plan[start + 2 * i], plan[start + 2 * i + 1]])
            return 0

        lax.fori_loop(0, plan[at], step, 0)

    if part:

        def face_step(i, _):
            made = []
            for k in range(FACE):
                cell = faces[i * FACE + k]
                c = i * (CELLS - FACE) + k
                held = slots[2 * k : 2 * k + 2]
                left = first_operand(first_rows(cell))
                density_products(left, second_operands(second[c], True), WIDTH, *held)
                made.append((cell, c, held))
            for cell, c, held in made:
                total[c] += density_weights(
                    WIDTH, *held, support_columns(cell[3:4]), own[c, 3:4], True
                )
            return 0

        lax.fori_loop(0, 2, face_step, 0)

    fold(total, own, CELLS, rho, carried)


def local_density(part, plan, own, *rest):
    return pl.pallas_call(
        functools.partial(local_density_kernel, part),
        in_specs=[SM] + [VM] * (1 + len(rest)),
        out_specs=VM,
        out_shape=jax.ShapeDtypeStruct((CELLS, WIDTH), F32),
        scratch_shapes=[
            pltpu.VMEM((CELLS + 1, 8, WIDTH), F32),
            pltpu.VMEM((CELLS + 1, 8, WIDTH), F32),
        ]
        + [pltpu.VMEM((WIDTH, WIDTH), F32)] * 8,
        cost_estimate=pl.CostEstimate(
            flops=64 * 65536 * 60, bytes_accessed=2 * 2**20, transcendentals=0
        ),
        compiler_params=params(),
    )(plan, own, *rest)


def listed_rows(slot, block, count):
    return [block[slot // SLOTS, pl.ds((slot % SLOTS) * count + k, 1), :] for k in range(count)]


def listed_cell(slot, listed):
    return jnp.concatenate(listed_rows(slot, listed, ROWS), 0)


def over_pairs(plan, unit):
    for kind, count in enumerate(CROSS_ROWS):
        base = 2 * len(LOCAL_ROWS) + 2 * kind
        at = CROSS_AT + 2 * kind * CROSS_LIST + plan[base + 1]

        def step(i, _):
            unit(
                count,
                [
                    (plan[at + UNIT * i + k], plan[at + CROSS_LIST + UNIT * i + k])
                    for k in range(UNIT)
                ],
            )
            return 0

        lax.fori_loop(0, plan[base], step, 0)


def cross_density_kernel(plan, own, listed, carried, rho, back, total, *slots):
    total[...] = jnp.zeros_like(total)
    back[...] = jnp.zeros_like(back)

    def unit(count, pairs):
        made = []
        for k, (slot, c) in enumerate(pairs):
            other = listed_cell(slot, listed)
            held = slots[2 * k : 2 * k + 2]
            left = first_operand(first_rows(own[c]))
            density_products(left, second_operands(second_rows(other), True), count, *held)
            made.append((slot, c, other, held))
        sums = []
        for slot, c, other, held in made:
            to_second, to_first = density_weights(
                count, *held, support_columns(own[c, 3:4]), other[3:4], False
            )
            sent = jnp.sum(to_second, axis=0, keepdims=True) * inverse_mass(other[4:5])
            sums.append((slot, c, to_first, sent))
        for slot, c, to_first, sent in sums:
            total[c] += to_first
            back[slot // SLOTS, pl.ds(slot % SLOTS, 1), :] = sent

    over_pairs(plan, unit)
    fold(total, own, CELLS, rho, carried)


def cross_density(plan, own, listed, carried):
    return pl.pallas_call(
        cross_density_kernel,
        in_specs=[SM, VM, VM, VM],
        out_specs=[VM, VM],
        out_shape=[
            jax.ShapeDtypeStruct((CELLS, WIDTH), F32),
            jax.ShapeDtypeStruct((PEERS, SLOTS, WIDTH), F32),
        ],
        scratch_shapes=[pltpu.VMEM((CELLS + 1, 8, WIDTH), F32)]
        + [pltpu.VMEM((WIDTH, WIDTH), F32)] * 8,
        cost_estimate=pl.CostEstimate(
            flops=80 * 65536 * 60, bytes_accessed=2 * 2**20, transcendentals=0
        ),
        compiler_params=params(),
    )(plan, own, listed, carried)


def pressure_kernel(
    occ, pair, near, returned, energy_in, own, density, moving, out, energy, sum_of, sem
):
    copies = fetch([(energy_in, energy)], sem)
    lane = lax.broadcasted_iota(jnp.int32, (1, WIDTH), 1)

    def read_step(c, _):
        sum_of[c] = near[pl.ds(c, 1), :]
        return 0

    lax.fori_loop(0, CELLS, read_step, 0, unroll=8)

    def peer_step(e, _):
        for s in range(SLOTS):
            sum_of[pair[e, s]] += returned[e, s : s + 1]
        return 0

    lax.fori_loop(0, PEERS, peer_step, 0)
    copies[0].wait()

    def cell_step(c, _):
        one = pl.ds(c, 1)
        full = lane < occ[c]
        rho = jnp.where(full, sum_of[c], 0.0)
        density[one, :] = rho
        term = jnp.where(full, GAMMA_LESS * energy[one, :] / jnp.where(full, rho, 1.0), 0.0)
        moving[c] = jnp.concatenate([own[c, 5:8], term], 0)
        return 0

    lax.fori_loop(0, CELLS, cell_step, 0, unroll=8)
    moving[CELLS] = jnp.zeros((MOVING, WIDTH), F32)

    def send_step(e, _):
        for s in range(SLOTS):
            out[e, s * MOVING : (s + 1) * MOVING] = moving[pair[e, s]]
        return 0

    lax.fori_loop(0, PEERS, send_step, 0)


def pressure(occ, pair, near, returned, energy, own):
    return pl.pallas_call(
        pressure_kernel,
        in_specs=[SM, SM, VM, VM, ANYWHERE, VM],
        out_specs=[VM, VM, VM],
        out_shape=[
            jax.ShapeDtypeStruct((CELLS, WIDTH), F32),
            jax.ShapeDtypeStruct((CELLS + 1, MOVING, WIDTH), F32),
            jax.ShapeDtypeStruct((PEERS, SLOTS * MOVING, WIDTH), F32),
        ],
        scratch_shapes=[
            pltpu.VMEM((CELLS, WIDTH), F32),
            pltpu.VMEM((CELLS, 1, WIDTH), F32),
            pltpu.SemaphoreType.DMA((1,)),
        ],
        compiler_params=params(),
    )(occ, pair, near, returned, energy, own)


def force_rows(cell, moving):
    x, y, z, _, m = [cell[k : k + 1] for k in range(5)]
    u, v, w, term = [moving[k : k + 1] for k in range(4)]
    mp = m * term
    blank = jnp.zeros_like(m)
    rows = jnp.concatenate(
        [m, m * x, m * y, m * z, mp, mp * x, mp * y, mp * z]
        + [m * u, m * v, m * w, m * (u * x + v * y + w * z)]
        + [blank] * 4,
        0,
    )
    high, low = split2(rows)
    return jnp.concatenate([high, low], 0)


def force_of(sums, cell, moving):
    sums = sums[:16] + sums[16:]
    one, p_one = sums[0:1], sums[4:5]
    place, speed, term = cell[0:3], moving[0:3], moving[3:4]
    lean = place * one - sums[1:4]
    acc = term * lean + (place * p_one - sums[5:8])
    mixed = jnp.sum(speed * lean - place * sums[8:11], axis=0, keepdims=True)
    rate = -term * (mixed + sums[11:12])
    return G_SCALE * jnp.concatenate([acc, rate], 0)


def slopes(left, near, columns, row, count, s_ref, high, low):
    s_ref[0:count] = jnp.dot(left[:count], near, preferred_element_type=F32)
    for start in range(0, count, CHUNK):
        s = jnp.maximum(s_ref[start : start + CHUNK], TINY)
        dist = s * lax.rsqrt(s)
        wide = columns[start : start + CHUNK]
        support = jnp.concatenate([wide, wide], 1) + row
        d = jnp.maximum(support - dist, 0.0)
        e = pl.reciprocal(support * support, approx=True)
        x = e * d
        g = (x * x) * (x * e)
        top = g.astype(BF)
        high[start : start + CHUNK] = top
        low[start : start + CHUNK] = (g - top.astype(F32)).astype(BF)


def to_seconds(rows, count, high, low):
    part = rows[:, :count]
    top = lax.dot_general(part, high[0:count], NN, preferred_element_type=F32)
    return top + lax.dot_general(part, low[0:count], NN, preferred_element_type=F32)


def to_firsts(rows, count, high, low):
    top = lax.dot_general(rows, high[0:count], NT, preferred_element_type=F32)
    return top + lax.dot_general(rows, low[0:count], NT, preferred_element_type=F32)


def add_forces(total, own, moving, out, carried):
    def cell_step(c, _):
        mine = force_of(total[c], own[c], moving[c])
        out[c] = mine if carried is None else carried[c] + mine
        return 0

    lax.fori_loop(0, CELLS, cell_step, 0, unroll=4)


def local_force_kernel(part, plan, own, moving, *rest):
    if part:
        faces, face_terms, carried, out, second, rows, total, *slots = rest
    else:
        faces = face_terms = carried = None
        out, second, rows, total, *slots = rest

    def cell_step(c, _):
        cell = own[c]
        second[c] = second_rows(cell)
        rows[c] = force_rows(cell, moving[c])
        return 0

    lax.fori_loop(0, CELLS + 1, cell_step, 0, unroll=5)
    total[...] = jnp.zeros_like(total)

    def unit(count, places):
        made = []
        for k, c in enumerate(places):
            after = jnp.minimum(c + 1, CELLS)
            one, two = slots[6 * k : 6 * k + 3], slots[6 * k + 3 : 6 * k + 6]
            row = own[c, 3:4]
            left = first_operand(first_rows(own[c]))
            columns = support_columns(row)
            slopes(left, second_operands(second[c], False), columns, row, count, *one)
            slopes(
                left, second_operands(second[after], False), columns, own[after, 3:4], count, *two
            )
            made.append((c, after, one[1:], two[1:]))
        for c, after, one, two in made:
            mine, other = rows[c], rows[after]
            total[c] += to_seconds(mine, count, *one)
            total[c, :, 0:count] += to_firsts(other, count, *two)
            total[after] += to_seconds(mine, count, *two)

    for kind, count in enumerate(LOCAL_ROWS):
        at = kind + part * len(LOCAL_ROWS)
        start = LOCAL_AT + at * LOCAL_LIST

        def step(i, _):
            unit(count, [plan[start + 2 * i], plan[start + 2 * i + 1]])
            return 0

        lax.fori_loop(0, plan[at], step, 0)

    if part:

        def face_step(i, _):
            made = []
            for k in range(FACE):
                cell = faces[i * FACE + k]
                c = i * (CELLS - FACE) + k
                held = slots[3 * k : 3 * k + 3]
                left = first_operand(first_rows(cell))
                slopes(
                    left, second_operands(second[c], False), support_columns(cell[3:4]),
                    own[c, 3:4], WIDTH, *held,
                )
                theirs = jnp.concatenate([cell[5:8], face_terms[i * FACE + k, 3:4]], 0)
                made.append((force_rows(cell, theirs), c, held[1:]))
            for theirs, c, held in made:
                total[c] += to_seconds(theirs, WIDTH, *held)
            return 0

        lax.fori_loop(0, 2, face_step, 0)

    add_forces(total, own, moving, out, carried)


PAIR_SLOT = [
    pltpu.VMEM((WIDTH, WIDTH), F32),
    pltpu.VMEM((WIDTH, WIDTH), BF),
    pltpu.VMEM((WIDTH, WIDTH), BF),
]


def local_force(part, plan, own, moving, *rest):
    return pl.pallas_call(
        functools.partial(local_force_kernel, part),
        in_specs=[SM] + [VM] * (2 + len(rest)),
        out_specs=VM,
        out_shape=jax.ShapeDtypeStruct((CELLS, 4, WIDTH), F32),
        scratch_shapes=[
            pltpu.VMEM((CELLS + 1, 8, WIDTH), F32),
            pltpu.VMEM((CELLS + 1, 32, WIDTH), BF),
            pltpu.VMEM((CELLS + 1, 32, WIDTH), F32),
        ]
        + PAIR_SLOT * 4,
        cost_estimate=pl.CostEstimate(
            flops=64 * 65536 * 80, bytes_accessed=2 * 2**20, transcendentals=0
        ),
        compiler_params=params(),
    )(plan, own, moving, *rest)


def cross_force_kernel(
    plan, own, moving, listed, arrived, carried, out, back, rows, total, *slots
):
    def cell_step(c, _):
        rows[c] = force_rows(own[c], moving[c])
        return 0

    lax.fori_loop(0, CELLS + 1, cell_step, 0, unroll=5)
    total[...] = jnp.zeros_like(total)
    back[...] = jnp.zeros_like(back)

    def unit(count, pairs):
        made = []
        for k, (slot, c) in enumerate(pairs):
            other = listed_cell(slot, listed)
            held = slots[3 * k : 3 * k + 3]
            left = first_operand(first_rows(own[c]))
            slopes(
                left, second_operands(second_rows(other), False), support_columns(own[c, 3:4]),
                other[3:4], count, *held,
            )
            made.append((slot, c, other, held[1:]))
        for slot, c, other, held in made:
            theirs = jnp.concatenate(listed_rows(slot, arrived, MOVING), 0)
            sums = to_seconds(rows[c], count, *held)
            sent = force_of(sums, other, theirs)
            for k in range(MOVING):
                at = pl.ds((slot % SLOTS) * MOVING + k, 1)
                back[slot // SLOTS, at, :] = sent[k : k + 1]
            total[c, :, 0:count] += to_firsts(force_rows(other, theirs), count, *held)

    over_pairs(plan, unit)
    add_forces(total, own, moving, out, carried)


def cross_force(plan, own, moving, listed, arrived, carried):
    return pl.pallas_call(
        cross_force_kernel,
        in_specs=[SM] + [VM] * 5,
        out_specs=[VM, VM],
        out_shape=[
            jax.ShapeDtypeStruct((CELLS, 4, WIDTH), F32),
            jax.ShapeDtypeStruct((PEERS, SLOTS * MOVING, WIDTH), F32),
        ],
        scratch_shapes=[
            pltpu.VMEM((CELLS + 1, 32, WIDTH), BF),
            pltpu.VMEM((CELLS + 1, 32, WIDTH), F32),
        ]
        + PAIR_SLOT * 4,
        cost_estimate=pl.CostEstimate(
            flops=80 * 65536 * 80, bytes_accessed=2 * 2**20, transcendentals=0
        ),
        compiler_params=params(),
    )(plan, own, moving, listed, arrived, carried)


def finish_kernel(occ, pair, near, returned, active_in, out, total, active, sem):
    copies = fetch([(active_in, active)], sem)
    lane = lax.broadcasted_iota(jnp.int32, (1, WIDTH), 1)
    total[...] = near[...]

    def peer_step(e, _):
        for s in range(SLOTS):
            total[pair[e, s]] += returned[e, s * MOVING : (s + 1) * MOVING]
        return 0

    lax.fori_loop(0, PEERS, peer_step, 0)
    copies[0].wait()

    def cell_step(c, _):
        one = pl.ds(c, 1)
        gate = jnp.where(lane < occ[c], active[one, :].astype(F32), 0.0)
        gated = total[c] * gate
        for k in range(4):
            out[k, one, :] = gated[k : k + 1]
        return 0

    lax.fori_loop(0, CELLS, cell_step, 0, unroll=8)


def finish(occ, pair, near, returned, active):
    return pl.pallas_call(
        finish_kernel,
        in_specs=[SM, SM, VM, VM, ANYWHERE],
        out_specs=VM,
        out_shape=jax.ShapeDtypeStruct((4, CELLS, WIDTH), F32),
        scratch_shapes=[
            pltpu.VMEM((CELLS, 4, WIDTH), F32),
            pltpu.VMEM((CELLS, WIDTH), jnp.int32),
            pltpu.SemaphoreType.DMA((1,)),
        ],
        compiler_params=params(),
    )(occ, pair, near, returned, active)


def to_peers(block):
    return lax.all_to_all(block, "dev", split_axis=0, concat_axis=0, tiled=True)


def with_neighbours(block):
    count = lax.axis_size("region")
    up = [(i, (i + 1) % count) for i in range(count)]
    down = [(i, (i - 1) % count) for i in range(count)]
    return jnp.concatenate(
        [
            lax.ppermute(block[CELLS - FACE : CELLS], "region", up),
            lax.ppermute(block[:FACE], "region", down),
        ],
        0,
    )


def local(
    positions, velocity, smoothing, masses, energy, occupancy, active, send_cells, send_fill,
    pair_cell,
):
    pair = pair_cell[0]
    own, listed, plan = prepare(
        occupancy, send_fill, send_cells[0], pair, positions, velocity, smoothing, masses
    )
    arrived = to_peers(listed)
    faces = with_neighbours(own)
    rho = local_density(0, plan, own)
    rho, back = cross_density(plan, own, arrived, rho)
    returned = to_peers(back)
    rho = local_density(1, plan, own, faces, rho)
    density, moving, leaving = pressure(occupancy, pair, rho, returned, energy, own)
    arrived_moving = to_peers(leaving)
    face_terms = with_neighbours(moving)
    sums = local_force(0, plan, own, moving)
    sums, force_back = cross_force(plan, own, moving, arrived, arrived_moving, sums)
    returned_force = to_peers(force_back)
    sums = local_force(1, plan, own, moving, faces, face_terms, sums)
    forces = finish(occupancy, pair, sums, returned_force, active)
    return (density, forces)


def solution(mesh):
    cells = P(("region", "dev"), None)
    vectors = P(None, ("region", "dev"), None)
    lists = P(("region", "dev"), None, None)
    in_specs = (
        vectors, vectors, cells, cells, cells, P(("region", "dev")), cells, lists, cells, lists,
    )
    return jax.shard_map(
        local, mesh=mesh, in_specs=in_specs, out_specs=(cells, vectors), check_vma=False
    )
```

time: 209 us -> 169 us (0.81)
  the two profiles are of different devices: /device:TPU:0 before, /device:TPU:57 now
where the time goes in v2:
time: 169 us; the launch traced here: 167 us
  Pallas kernels  119 us (70%)
  starting transfers between devices  35.7 us (21%)
  local copies, waits for them, and re-layouts  6.27 us (4%)
  waiting for transfers between devices  4.75 us (3%)
    pallas_call x2, Pallas kernels, local_force(): pl.pallas_call(functools.partial(local_force_kernel, part), in_specs=[SM]...  39.6 us
    all_to_all x4, starting transfers between devices, to_peers(): return lax.all_to_all(block, 'dev', split_axis=0, concat_axis=0, tiled=True)  32.3 us
    pallas_call x2, Pallas kernels, local_density(): pl.pallas_call(functools.partial(local_density_kernel, part), in_specs=[S...  29.4 us
    pallas_call x1, Pallas kernels, cross_force(): pl.pallas_call(cross_force_kernel, in_specs=[SM] + [VM] * 5, out_specs=[V...  22.5 us
    pallas_call x1, Pallas kernels, cross_density(): pl.pallas_call(cross_density_kernel, in_specs=[SM, VM, VM, VM], out_specs...  15.4 us
    unnamed x27, local copies, waits for them, and re-layouts  6.26 us
    pallas_call x1, Pallas kernels, prepare(): pl.pallas_call(prepare_kernel, in_specs=[SM] * 4 + [ANYWHERE] * 4, out_sp...  5.86 us
    ppermute x2, waiting for transfers between devices, with_neighbours(): lax.ppermute(block[:FACE], 'region', down)  3.8 us
  transfers between devices with their start and end apart: 8, of which 3 were waited for; matrix products, arithmetic and copies ran while one was open for 0% of the time, Pallas kernels for 51%

profile of v2, /device:TPU:57, one launch (start us, length us, event | category | flops | bytes accessed | tf_op | source)
XLA Modules:
  0.0 166.5 jit_solution(8319530868835790771)
XLA Ops:
  0.6 0.9 copy-done.1
  1.6 0.9 copy-done.2
  2.5 0.7 copy-done.3
  3.2 0.8 copy-done.5
  4.0 0.8 copy-done.6
  4.9 0.7 copy-done.9
  5.6 0.7 copy-done.10
  6.9 5.9 %shard_map.113 = (f32[65,8,256]{2,1,0:T(8,128)S(1)}, f32[16,80,256]{2,1,0:T(8,128)}, s32[1680]{0:T(1024)S(1)}) custom-call(s32[64]{0:T(128)S(1)} %copy-done.10, s32[1,16]{1,0:T(1,128)S(1)} %copy-done.12, s32[16,16]{1,0:T(8,128)S(1)} %bitcast.5, s32[16,16]{1,0:T(8,128)S(1)} %bitcast.2, f32[3,64,256]{2,1,0:T(8,128)S(1)} %copy-done.1, ...), custom_call_target="tpu_custom_call" | custom-call | tf_op jit(solution)/shard_map/pallas_call | solution.py:230
  12.7 7.5 %all-to-all-start = ((f32[16,80,256]{2,1,0:T(8,128)}), f32[16,80,256]{2,1,0:T(8,128)S(1)}, u32[]{:S(2)}, u32[]{:S(2)}) async-start(f32[16,80,256]{2,1,0:T(8,128)} %get-tuple-element.14), calls=%async_computation | async-start | bytes 2621440 | tf_op jit(solution)/shard_map/all_to_all | solution.py:729
  20.2 0.9 collective-permute-start
  21.3 16.1 %shard_map.114.carried = f32[64,256]{1,0:T(8,128)S(1)} custom-call(s32[1680]{0:T(1024)S(1)} %get-tuple-element.12.plan, f32[65,8,256]{2,1,0:T(8,128)S(1)} %get-tuple-element.13.own), custom_call_target="tpu_custom_call" | custom-call | flops 251658240 | bytes 2097152 | tf_op jit(solution)/shard_map/pallas_call | solution.py:329
  37.5 15.4 %shard_map.115 = (f32[64,256]{1,0:T(8,128)S(1)}, f32[16,16,256]{2,1,0:T(8,128)}) custom-call(s32[1680]{0:T(1024)S(1)} %get-tuple-element.12.plan, f32[65,8,256]{2,1,0:T(8,128)S(1)} %get-tuple-element.13.own, f32[16,80,256]{2,1,0:T(8,128)S(1)} %all-to-all-done.listed, f32[64,256]{1,0:T(8,128)S(1)} %shard_map.114.carried), custom_call_target="tpu_custom_call" | custom-call | flops 314572800 | bytes 2097152 | tf_op jit(solution)/shard_map/pallas_call | solution.py:400
  52.9 8.6 %all-to-all-start.1 = ((f32[16,16,256]{2,1,0:T(8,128)}), f32[16,16,256]{2,1,0:T(8,128)S(1)}, u32[]{:S(2)}, u32[]{:S(2)}) async-start(f32[16,16,256]{2,1,0:T(8,128)} %get-tuple-element.16), calls=%async_computation.1 | async-start | bytes 524288 | tf_op jit(solution)/shard_map/all_to_all | solution.py:729
  61.5 13.2 %shard_map.116.near = f32[64,256]{1,0:T(8,128)S(1)} custom-call(s32[1680]{0:T(1024)S(1)} %get-tuple-element.12.plan, f32[65,8,256]{2,1,0:T(8,128)S(1)} %get-tuple-element.13.own, f32[8,8,256]{2,1,0:T(8,128)S(1)} %constant_dynamic-update-slice_fusion.rest_0_, f32[64,256]{1,0:T(8,128)S(1)} %get-tuple-element.15.rest_1_), custom_call_target="tpu_custom_call" | custom-call | flops 251658240 | bytes 2097152 | tf_op jit(solution)/shard_map/pallas_call | solution.py:329
  74.8 3.6 %shard_map.117 = (f32[64,256]{1,0:T(8,128)}, f32[65,4,256]{2,1,0:T(4,128)S(1)}, f32[16,64,256]{2,1,0:T(8,128)}) custom-call(s32[64]{0:T(128)S(1)} %copy-done.11, s32[16,16]{1,0:T(8,128)S(1)} %bitcast.3, f32[64,256]{1,0:T(8,128)S(1)} %shard_map.116.near, f32[16,16,256]{2,1,0:T(8,128)S(1)} %all-to-all-done.1.returned, f32[64,256]{1,0:T(8,128)S(1)} %copy-done.7, ...), custom_call_target="tpu_custom_call" | custom-call | tf_op jit(solution)/shard_map/pallas_call | solution.py:458
  78.4 6.3 %all-to-all-start.2 = ((f32[16,64,256]{2,1,0:T(8,128)}), f32[16,64,256]{2,1,0:T(8,128)S(1)}, u32[]{:S(2)}, u32[]{:S(2)}) async-start(f32[16,64,256]{2,1,0:T(8,128)} %get-tuple-element.19), calls=%async_computation.2 | async-start | bytes 2097152 | tf_op jit(solution)/shard_map/all_to_all | solution.py:729
  84.7 21.8 %shard_map.118.carried = f32[64,4,256]{2,1,0:T(4,128)S(1)} custom-call(s32[1680]{0:T(1024)S(1)} %get-tuple-element.12.plan, f32[65,8,256]{2,1,0:T(8,128)S(1)} %get-tuple-element.13.own, f32[65,4,256]{2,1,0:T(4,128)S(1)} %get-tuple-element.18.moving), custom_call_target="tpu_custom_call" | custom-call | flops 335544320 | bytes 2097152 | tf_op jit(solution)/shard_map/pallas_call | solution.py:615
  106.5 22.5 %shard_map.119 = (f32[64,4,256]{2,1,0:T(4,128)S(1)}, f32[16,64,256]{2,1,0:T(8,128)}) custom-call(s32[1680]{0:T(1024)S(1)} %get-tuple-element.12.plan, f32[65,8,256]{2,1,0:T(8,128)S(1)} %get-tuple-element.13.own, f32[65,4,256]{2,1,0:T(4,128)S(1)} %get-tuple-element.18.moving, f32[16,80,256]{2,1,0:T(8,128)} %copy-done, ...), custom_call_target="tpu_custom_call" | custom-call | flops 419430400 | bytes 2097152 | tf_op jit(solution)/shard_map/pallas_call | solution.py:669
  129.1 10.0 %all-to-all-start.3 = ((f32[16,64,256]{2,1,0:T(8,128)}), f32[16,64,256]{2,1,0:T(8,128)S(1)}, u32[]{:S(2)}, u32[]{:S(2)}) async-start(f32[16,64,256]{2,1,0:T(8,128)} %get-tuple-element.21), calls=%async_computation.3 | async-start | bytes 2097152 | tf_op jit(solution)/shard_map/all_to_all | solution.py:729
  139.1 2.4 %collective-permute-start.2 = (f32[4,4,256]{2,1,0:T(4,128)S(1)}, f32[4,4,256]{2,1,0:T(4,128)S(1)}, u32[]{:S(2)}, u32[]{:S(2)}) collective-permute-start(f32[4,4,256]{2,1,0:T(4,128)S(1)} %get-tuple-element.24), channel_id=1, source_target_pairs={{0,16},{16,32},{32,48},{48,64},{64,80},{80,96},{96,112},{112,0},{1... | collective-permute-start | bytes 49160 | tf_op jit(solution)/shard_map/ppermute | solution.py:738
  141.4 0.9 collective-permute-done.2
  142.3 3.8 %collective-permute-done.3 = f32[4,4,256]{2,1,0:T(4,128)S(1)} collective-permute-done((f32[4,4,256]{2,1,0:T(4,128)S(1)}, f32[4,4,256]{2,1,0:T(4,128)S(1)}, u32[]{:S(2)}, u32[]{:S(2)}) %collective-permute-start.3) | collective-permute-done | bytes 16416 | tf_op jit(solution)/shard_map/ppermute | solution.py:739
  146.1 17.8 %shard_map.120.near = f32[64,4,256]{2,1,0:T(4,128)S(1)} custom-call(s32[1680]{0:T(1024)S(1)} %get-tuple-element.12.plan, f32[65,8,256]{2,1,0:T(8,128)S(1)} %get-tuple-element.13.own, f32[65,4,256]{2,1,0:T(4,128)S(1)} %get-tuple-element.18.moving, f32[8,8,256]{2,1,0:T(8,128)S(1)} %constant_dynamic-update-slice_fusion.rest_0_, ...), custom_call_target="tpu_custom_call" | custom-call | flops 335544320 | bytes 2097152 | tf_op jit(solution)/shard_map/pallas_call | solution.py:615
  163.9 2.5 %shard_map.121 = f32[4,64,256]{2,1,0:T(8,128)} custom-call(s32[64]{0:T(128)S(1)} %copy-done.11, s32[16,16]{1,0:T(8,128)S(1)} %bitcast.4, f32[64,4,256]{2,1,0:T(4,128)S(1)} %shard_map.120.near, f32[16,64,256]{2,1,0:T(8,128)S(1)} %all-to-all-done.3.returned, s32[64,256]{1,0:T(8,128)S(1)} %copy-done.8), custom_call_target="tpu_custom_call" | custom-call | tf_op jit(solution)/shard_map/pallas_call | solution.py:714
  (32 shorter events, 0.9 us)
Async XLA Ops:
  0.6 0.9 copy-start.1
  1.6 0.9 copy-start.2
  2.5 0.7 copy-start.3
  3.2 0.8 copy-start.5
  4.0 0.8 copy-start.6
  4.9 0.7 copy-start.9
  5.6 0.7 copy-start.10
  6.2 0.7 copy-start.12
  12.7 24.8 %all-to-all-start = ((f32[16,80,256]{2,1,0:T(8,128)}), f32[16,80,256]{2,1,0:T(8,128)S(1)}, u32[]{:S(2)}, u32[]{:S(2)}) async-start(f32[16,80,256]{2,1,0:T(8,128)} %get-tuple-element.14), calls=%async_computation | async-start | bytes 2621440 | tf_op jit(solution)/shard_map/all_to_all | solution.py:729
  20.2 41.3 %collective-permute-start = (f32[4,8,256]{2,1,0:T(8,128)S(1)}, f32[4,8,256]{2,1,0:T(8,128)S(1)}, u32[]{:S(2)}, u32[]{:S(2)}) collective-permute-start(f32[4,8,256]{2,1,0:T(8,128)S(1)} %get-tuple-element.23), channel_id=1, source_target_pairs={{0,16},{16,32},{32,48},{48,64},{64,80},{80,96},{96,112},{112,0},{1... | collective-permute-start | bytes 98312 | tf_op jit(solution)/shard_map/ppermute | solution.py:738
  21.2 40.4 %collective-permute-start.1 = (f32[4,8,256]{2,1,0:T(8,128)S(1)}, f32[4,8,256]{2,1,0:T(8,128)S(1)}, u32[]{:S(2)}, u32[]{:S(2)}) collective-permute-start(f32[4,8,256]{2,1,0:T(8,128)S(1)} %get-tuple-element.22), channel_id=1, source_target_pairs={{0,112},{16,0},{32,16},{48,32},{64,48},{80,64},{96,80},{112,96},{1... | collective-permute-start | bytes 98312 | tf_op jit(solution)/shard_map/ppermute | solution.py:739
  37.4 37.4 %copy-start.4 = (s32[1,16,16]{2,1,0:T(8,128)S(1)}, s32[1,16,16]{2,1,0:T(8,128)}, u32[]{:S(2)}) copy-start(s32[1,16,16]{2,1,0:T(8,128)} %param.19) | copy-start | bytes 3076
  37.4 37.4 %copy-start.7 = (f32[64,256]{1,0:T(8,128)S(1)}, f32[64,256]{1,0:T(8,128)}, u32[]{:S(2)}) copy-start(f32[64,256]{1,0:T(8,128)} %energy_in.1) | copy-start | bytes 196612
  37.5 37.4 %copy-start.11 = (s32[64]{0:T(128)S(1)}, s32[64]{0:T(128)}, u32[]{:S(2)}) copy-start(s32[64]{0:T(128)} %occ.5) | copy-start | bytes 772
  37.5 37.3 %copy-start = (f32[16,80,256]{2,1,0:T(8,128)}, f32[16,80,256]{2,1,0:T(8,128)S(1)}, u32[]{:S(2)}) copy-start(f32[16,80,256]{2,1,0:T(8,128)S(1)} %all-to-all-done.listed) | copy-start | bytes 3932164
  52.9 21.9 %all-to-all-start.1 = ((f32[16,16,256]{2,1,0:T(8,128)}), f32[16,16,256]{2,1,0:T(8,128)S(1)}, u32[]{:S(2)}, u32[]{:S(2)}) async-start(f32[16,16,256]{2,1,0:T(8,128)} %get-tuple-element.16), calls=%async_computation.1 | async-start | bytes 524288 | tf_op jit(solution)/shard_map/all_to_all | solution.py:729
  78.4 28.1 %all-to-all-start.2 = ((f32[16,64,256]{2,1,0:T(8,128)}), f32[16,64,256]{2,1,0:T(8,128)S(1)}, u32[]{:S(2)}, u32[]{:S(2)}) async-start(f32[16,64,256]{2,1,0:T(8,128)} %get-tuple-element.19), calls=%async_computation.2 | async-start | bytes 2097152 | tf_op jit(solution)/shard_map/all_to_all | solution.py:729
  129.1 34.8 %copy-start.8 = (s32[64,256]{1,0:T(8,128)S(1)}, s32[64,256]{1,0:T(8,128)}, u32[]{:S(2)}) copy-start(s32[64,256]{1,0:T(8,128)} %active_in.1) | copy-start | bytes 196612
  129.1 34.8 %all-to-all-start.3 = ((f32[16,64,256]{2,1,0:T(8,128)}), f32[16,64,256]{2,1,0:T(8,128)S(1)}, u32[]{:S(2)}, u32[]{:S(2)}) async-start(f32[16,64,256]{2,1,0:T(8,128)} %get-tuple-element.21), calls=%async_computation.3 | async-start | bytes 2097152 | tf_op jit(solution)/shard_map/all_to_all | solution.py:729
  139.1 3.2 %collective-permute-start.2 = (f32[4,4,256]{2,1,0:T(4,128)S(1)}, f32[4,4,256]{2,1,0:T(4,128)S(1)}, u32[]{:S(2)}, u32[]{:S(2)}) collective-permute-start(f32[4,4,256]{2,1,0:T(4,128)S(1)} %get-tuple-element.24), channel_id=1, source_target_pairs={{0,16},{16,32},{32,48},{48,64},{64,80},{80,96},{96,112},{112,0},{1... | collective-permute-start | bytes 49160 | tf_op jit(solution)/shard_map/ppermute | solution.py:738
  141.4 4.7 %collective-permute-start.3 = (f32[4,4,256]{2,1,0:T(4,128)S(1)}, f32[4,4,256]{2,1,0:T(4,128)S(1)}, u32[]{:S(2)}, u32[]{:S(2)}) collective-permute-start(f32[4,4,256]{2,1,0:T(4,128)S(1)} %get-tuple-element.25), channel_id=1, source_target_pairs={{0,112},{16,0},{32,16},{48,32},{64,48},{80,64},{96,80},{112,96},{1... | collective-permute-start | bytes 49160 | tf_op jit(solution)/shard_map/ppermute | solution.py:739

commit v3 on v2

v3 whole, which is shorter than its diff:
```python
import functools
import math

import jax
import jax.numpy as jnp
from jax import lax
from jax.experimental import pallas as pl
from jax.experimental.pallas import tpu as pltpu
from jax.sharding import PartitionSpec as P

BF = jnp.bfloat16
F32 = jnp.float32
FACE = 4
CELLS = 64
WIDTH = 256
PEERS = 16
SLOTS = 16
LISTED = PEERS * SLOTS
GAMMA_LESS = 2.0 / 3.0
W_SCALE = 84.0 / math.pi
G_SCALE = 6720.0 / math.pi
TINY = 1e-14
EMPTY = 1e8
CHUNK = 32
CELL = 8
SUMS = 16
NN = (((1,), (0,)), ((), ()))
NT = (((1,), (1,)), ((), ()))
VM = pl.BlockSpec(memory_space=pltpu.VMEM)
SM = pl.BlockSpec(memory_space=pltpu.SMEM)
ROWS = 5
MOVING = 4
SPLIT = 40
LOCAL_ROWS = (192, 224, 256)
CROSS_ROWS = (192, 256)
UNIT = 4
LOCAL_AT = 16
LOCAL_LIST = 72
LEAD = UNIT + 3
CROSS_AT = LOCAL_AT + 2 * len(LOCAL_ROWS) * LOCAL_LIST
CROSS_LIST = LISTED + 16
PLAN = CROSS_AT + 2 * len(CROSS_ROWS) * CROSS_LIST
ANYWHERE = pl.BlockSpec(memory_space=pl.ANY)


def params():
    return pltpu.CompilerParams(vmem_limit_bytes=50 * 2**20)


def split2(x):
    a = x.astype(BF)
    return a, (x - a.astype(F32)).astype(BF)


def split3(x):
    a = x.astype(BF).astype(F32)
    rest = x - a
    b = rest.astype(BF).astype(F32)
    return a, b, rest - b


def pair_terms(x, y, z, h, m):
    norm = 4.0 * (x * x + y * y + z * z)
    root = lax.rsqrt(jnp.where(m > 0.0, m, 1.0))
    mu = jnp.where(m > 0.0, root * lax.rsqrt(root), EMPTY)
    one = jnp.ones_like(x)
    first = [-8.0 * x, -8.0 * y, -8.0 * z, norm, one, h * h * mu, 2.0 * h * mu, mu]
    second = [x, y, z, one, norm, mu, h * mu, h * h * mu]
    return first, second


def both(read):
    return jnp.concatenate([read(0), read(1)], -1)


def half(value, h):
    return value[..., 128 * h : 128 * (h + 1)]


def put(ref, planes, start, count, stride):
    for k, plane in enumerate(planes):
        for h in range(2):
            ref[h, pl.ds(start + k, count, stride=stride), :] = half(plane, h)


def planes_of(ref, ids, start, count, stride):
    return [both(lambda h: ref[h, pl.ds(start + k, count, stride=stride), :]) for k in ids]


def rows_at(index, size):
    return pl.ds(pl.multiple_of(index * size, size), size)


def block(ref, index, size):
    return both(lambda h: ref[h, rows_at(index, size), :])


def set_block(ref, index, size, value):
    for h in range(2):
        ref[h, rows_at(index, size), :] = half(value, h)


def add_block(ref, index, size, value):
    for h in range(2):
        ref[h, rows_at(index, size), :] += half(value, h)


def line(ref, index, size, k):
    return both(lambda h: ref[h, pl.ds(index * size + k, 1), :])


def listed_planes(listed, e, ids, size):
    step = SLOTS * size
    return [
        both(lambda h: listed[e, pl.ds(h * step + k, SLOTS, stride=size), :]) for k in ids
    ]


def listed_support(listed, slot):
    at = (slot % SLOTS) * ROWS + 3
    return both(lambda h: listed[slot // SLOTS, pl.ds(h * SLOTS * ROWS + at, 1), :])


def first_operand(rows):
    a1, a2, a3 = split3(rows)
    return jnp.concatenate([a1, a1, a2, a2, a1, a3, jnp.zeros((80, WIDTH), F32)], 0).T.astype(BF)


def second_operands(rows, both):
    b1, b2, b3 = split3(rows)
    stacked = jnp.concatenate([b1, b2, b1, b2, b3, b1, jnp.zeros((80, WIDTH), F32)], 0)
    part = lax.broadcasted_iota(jnp.int32, stacked.shape, 0) % 8
    near = jnp.where(part < 5, stacked, 0.0).astype(BF)
    if not both:
        return near
    return near, jnp.where(part >= 5, stacked, 0.0).astype(BF)


def support_columns(row):
    return jnp.broadcast_to(row, (128, WIDTH)).T


def density_products(left, operands, count, s_ref, mix_ref):
    part = left[:count]
    s_ref[0:count] = jnp.dot(part, operands[0], preferred_element_type=F32)
    mix_ref[0:count] = jnp.dot(part, operands[1], preferred_element_type=F32)


def density_weights(count, s_ref, mix_ref, columns, row, one_sided):
    second = jnp.zeros((8, WIDTH), F32)
    firsts = []
    for start in range(0, count, CHUNK):
        s = jnp.maximum(s_ref[start : start + CHUNK], TINY)
        dist = s * lax.rsqrt(s)
        wide = columns[start : start + CHUNK]
        support = jnp.concatenate([wide, wide], 1) + row
        d = jnp.maximum(support - dist, 0.0)
        x = pl.reciprocal(mix_ref[start : start + CHUNK], approx=True) * d
        x = x * x
        x = x * x
        w = x * (support + 4.0 * dist)
        for k in range(CHUNK // 8):
            second = second + w[8 * k : 8 * k + 8]
        if not one_sided:
            firsts.append(w[:, :128] + w[:, 128:])
    if one_sided:
        return second
    if count < WIDTH:
        firsts.append(jnp.zeros((WIDTH - count, 128), F32))
    turned = jnp.concatenate(firsts, 0).T
    first = turned[:8]
    for k in range(1, 16):
        first = first + turned[8 * k : 8 * k + 8]
    return second, first


def inverse_mass(m):
    return jnp.where(m > 0.0, W_SCALE / jnp.where(m > 0.0, m, 1.0), 0.0)


def plan_kernel(occ, fill, cells, _, plan):
    classes = len(LOCAL_ROWS)
    for kind in range(2 * classes):
        plan[kind] = 0
        for k in range(2):
            plan[LOCAL_AT + kind * LOCAL_LIST + k] = CELLS

    def local_step(c, _):
        size = occ[c]
        kind = sum((size > rows).astype(jnp.int32) for rows in LOCAL_ROWS[:-1])
        kind = kind + jnp.where(c >= SPLIT, classes, 0)
        count = plan[kind]
        plan[LOCAL_AT + kind * LOCAL_LIST + 2 + count] = c
        plan[kind] = count + 1
        return 0

    lax.fori_loop(0, CELLS, local_step, 0)
    for kind in range(2 * classes):
        count = plan[kind]
        for k in range(2):
            plan[LOCAL_AT + kind * LOCAL_LIST + 2 + count + k] = CELLS
        plan[kind] = (count + 1) // 2

    base = 2 * classes

    unused = jnp.int32(0)
    for e in range(PEERS):
        unused = jnp.where(fill[0, e] == 0, e * SLOTS, unused)

    def blank(at):
        plan[at] = unused
        plan[at + CROSS_LIST] = CELLS

    for kind in range(len(CROSS_ROWS)):
        for k in range(LEAD):
            blank(CROSS_AT + 2 * kind * CROSS_LIST + k)

    def peer_step(e, counts):
        def slot_step(s, counts):
            cell = cells[e, s]
            wide = (occ[cell] > CROSS_ROWS[0]).astype(jnp.int32)
            at = CROSS_AT + LEAD + jnp.where(
                wide > 0, 2 * CROSS_LIST + counts[1], counts[0]
            )
            plan[at] = e * SLOTS + s
            plan[at + CROSS_LIST] = cell
            return (counts[0] + 1 - wide, counts[1] + wide)

        return lax.fori_loop(0, fill[0, e], slot_step, counts)

    counts = lax.fori_loop(0, PEERS, peer_step, (jnp.int32(0), jnp.int32(0)))
    for kind in range(len(CROSS_ROWS)):
        trips = (counts[kind] + UNIT - 1) // UNIT
        plan[base + 2 * kind] = trips
        plan[base + 2 * kind + 1] = LEAD + counts[kind] - UNIT * trips
        for k in range(2):
            blank(CROSS_AT + 2 * kind * CROSS_LIST + LEAD + counts[kind] + k)


def make_plan(occ, fill, cells, own):
    return pl.pallas_call(
        plan_kernel,
        in_specs=[SM] * 3 + [ANYWHERE],
        out_specs=SM,
        out_shape=jax.ShapeDtypeStruct((PLAN,), jnp.int32),
    )(occ, fill, cells, own)


def fetch(pairs, sem):
    copies = [
        pltpu.make_async_copy(source, target, sem.at[k])
        for k, (source, target) in enumerate(pairs)
    ]
    for copy in copies:
        copy.start()
    return copies


def prepare_kernel(
    occ, pair, pos_in, vel_in, smooth_in, mass_in, own, first, second, out,
    pos, vel, smooth, mass, full, cells, sem,
):
    copies = fetch(
        [(pos_in, pos), (vel_in, vel), (smooth_in, smooth), (mass_in, mass)], sem
    )
    lane = lax.broadcasted_iota(jnp.int32, (1, WIDTH), 1)
    for c in range(CELLS):
        full[c : c + 1, :] = (lane < occ[c]).astype(F32)
    for copy in copies:
        copy.wait()
    place = [pos[k] - 0.5 for k in range(3)]
    m = jnp.where(full[...] > 0.0, mass[...], 0.0)
    h = smooth[...]
    put(own, place + [h, m] + [vel[k] for k in range(3)], 0, CELLS, CELL)
    blank = jnp.zeros((CELL, WIDTH), F32)
    wide = jnp.full((1, WIDTH), 0.5, F32)
    set_block(own, CELLS, CELL, jnp.concatenate([blank[:3], wide, blank[:4]], 0))
    before, after = pair_terms(*place, h, m)
    put(first, before, 0, CELLS, CELL)
    put(second, after, 0, CELLS, CELL)
    before, after = pair_terms(*[blank[:1]] * 3, wide, blank[:1])
    set_block(first, CELLS, CELL, jnp.concatenate(before, 0))
    set_block(second, CELLS, CELL, jnp.concatenate(after, 0))

    def cell_step(c, _):
        cells[c] = block(own, c, CELL)
        return 0

    lax.fori_loop(0, CELLS, cell_step, 0, unroll=8)

    def peer_step(e, _):
        for s in range(SLOTS):
            cell = cells[pair[e, s], 0:ROWS]
            for h in range(2):
                at = (h * SLOTS + s) * ROWS
                out[e, at : at + ROWS] = half(cell, h)
        return 0

    lax.fori_loop(0, PEERS, peer_step, 0)


def prepare(occ, pair, pos, vel, smooth, mass):
    rows = jax.ShapeDtypeStruct((2, (CELLS + 1) * CELL, 128), F32)
    plane = pltpu.VMEM((CELLS, WIDTH), F32)
    return pl.pallas_call(
        prepare_kernel,
        in_specs=[SM] * 2 + [ANYWHERE] * 4,
        out_specs=[VM] * 4,
        out_shape=[rows] * 3 + [jax.ShapeDtypeStruct((PEERS, 2 * SLOTS * ROWS, 128), F32)],
        scratch_shapes=[
            pltpu.VMEM((3, CELLS, WIDTH), F32),
            pltpu.VMEM((3, CELLS, WIDTH), F32),
            plane,
            plane,
            plane,
            pltpu.VMEM((CELLS, CELL, WIDTH), F32),
            pltpu.SemaphoreType.DMA((4,)),
        ],
        compiler_params=pltpu.CompilerParams(vmem_limit_bytes=60 * 2**20),
    )(occ, pair, pos, vel, smooth, mass)


def fold(total, own, out, carried):
    mine = sum(planes_of(total, range(CELL), 0, CELLS, CELL))
    mass = planes_of(own, [4], 0, CELLS, CELL)[0]
    mine = mine * inverse_mass(mass)
    out[...] = mine if carried is None else carried[...] + mine


def make_face_first(faces, face_first):
    planes = planes_of(faces, range(ROWS), 0, 2 * FACE, CELL)
    put(face_first, pair_terms(*planes)[0], 0, 2 * FACE, CELL)


def face_cell(n):
    return jnp.where(n < FACE, n, CELLS - 2 * FACE + n)


def in_turns(trips, item, last, products, weights, slot_a, slot_b):
    products(item(0), slot_a)

    def step(i, _):
        products(item(2 * i + 1), slot_b)
        weights(item(2 * i), slot_a)
        after = 2 * i + 2
        products(item(after if last is None else jnp.minimum(after, last - 1)), slot_a)
        weights(item(2 * i + 1), slot_b)
        return 0

    lax.fori_loop(0, trips, step, 0)


def cell_list(plan, part, kind):
    at = kind + part * len(LOCAL_ROWS)
    start = LOCAL_AT + at * LOCAL_LIST + 2
    return plan[at], lambda n: plan[start + n]


def local_density_kernel(part, plan, own, first, second, *rest):
    if part:
        faces, carried, rho, total, face_first, *slots = rest
    else:
        carried = None
        rho, total, *slots = rest
    slot_a, slot_b = slots[:6], slots[6:]
    total[...] = jnp.zeros_like(total)

    def products(count, c, held):
        left = first_operand(block(first, c, CELL))
        after = jnp.minimum(c + 1, CELLS)
        held[4][...] = support_columns(line(own, c, CELL, 3))
        density_products(left, second_operands(block(second, c, CELL), True), count, *held[0:2])
        density_products(
            left, second_operands(block(second, after, CELL), True), count, *held[2:4]
        )

    def weights(count, c, held):
        after = jnp.minimum(c + 1, CELLS)
        row, other = line(own, c, CELL, 3), line(own, after, CELL, 3)
        own_sum = density_weights(count, *held[0:2], held[4], row, True)
        there, here = density_weights(count, *held[2:4], held[4], other, False)
        add_block(total, c, CELL, own_sum + here)
        add_block(total, after, CELL, there)

    for kind, count in enumerate(LOCAL_ROWS):
        trips, item = cell_list(plan, part, kind)
        in_turns(
            trips, item, None, functools.partial(products, count),
            functools.partial(weights, count), slot_a, slot_b,
        )

    if part:
        make_face_first(faces, face_first)

        def face_products(i, held):
            for k in range(2):
                n = 2 * i + k
                left = first_operand(block(face_first, n, CELL))
                operands = second_operands(block(second, face_cell(n), CELL), True)
                held[4 + k][...] = support_columns(line(faces, n, CELL, 3))
                density_products(left, operands, WIDTH, *held[2 * k : 2 * k + 2])

        def face_weights(i, held):
            for k in range(2):
                c = face_cell(2 * i + k)
                added = density_weights(
                    WIDTH, *held[2 * k : 2 * k + 2], held[4 + k], line(own, c, CELL, 3), True
                )
                add_block(total, c, CELL, added)

        in_turns(FACE // 2, lambda i: i, FACE, face_products, face_weights, slot_a, slot_b)

    fold(total, own, rho, carried)


DENSITY_SLOT = [pltpu.VMEM((WIDTH, WIDTH), F32)] * 4 + [pltpu.VMEM((WIDTH, 128), F32)] * 2


def local_density(part, plan, own, first, second, *rest):
    return pl.pallas_call(
        functools.partial(local_density_kernel, part),
        in_specs=[SM] + [VM] * (3 + len(rest)),
        out_specs=VM,
        out_shape=jax.ShapeDtypeStruct((CELLS, WIDTH), F32),
        scratch_shapes=[pltpu.VMEM((2, (CELLS + 1) * CELL, 128), F32)]
        + [pltpu.VMEM((2, 2 * FACE * CELL, 128), F32)] * part
        + DENSITY_SLOT * 2,
        cost_estimate=pl.CostEstimate(
            flops=64 * 65536 * 60, bytes_accessed=2 * 2**20, transcendentals=0
        ),
        compiler_params=params(),
    )(plan, own, first, second, *rest)


def pair_list(plan, kind):
    base = 2 * len(LOCAL_ROWS) + 2 * kind
    at = CROSS_AT + 2 * kind * CROSS_LIST + plan[base + 1]

    def item(n):
        return [(plan[at + 2 * n + k], plan[at + CROSS_LIST + 2 * n + k]) for k in range(2)]

    return plan[base], item


def live_rows(fill, e):
    row = lax.broadcasted_iota(jnp.int32, (SLOTS, WIDTH), 0)
    return row < fill[0, e]


def cross_density_kernel(
    fill, plan, own, first, listed, carried, rho, back, total, theirs, there_of, *slots
):
    slot_a, slot_b = slots[:6], slots[6:]
    total[...] = jnp.zeros_like(total)

    def peer_step(e, _):
        after = pair_terms(*listed_planes(listed, e, range(ROWS), ROWS))[1]
        put(theirs, after, e * SLOTS * CELL, SLOTS, CELL)
        return 0

    lax.fori_loop(0, PEERS, peer_step, 0, unroll=2)

    def products(count, pairs, held):
        for k, (slot, c) in enumerate(pairs):
            left = first_operand(block(first, c, CELL))
            held[4 + k][...] = support_columns(line(own, c, CELL, 3))
            operands = second_operands(block(theirs, slot, CELL), True)
            density_products(left, operands, count, *held[2 * k : 2 * k + 2])

    def weights(count, pairs, held):
        for k, (slot, c) in enumerate(pairs):
            support = listed_support(listed, slot)
            there, here = density_weights(
                count, *held[2 * k : 2 * k + 2], held[4 + k], support, False
            )
            add_block(total, c, CELL, here)
            set_block(there_of, slot, CELL, there)

    for kind, count in enumerate(CROSS_ROWS):
        trips, item = pair_list(plan, kind)
        in_turns(
            trips, item, None, functools.partial(products, count),
            functools.partial(weights, count), slot_a, slot_b,
        )

    def back_step(e, _):
        summed = sum(planes_of(there_of, range(CELL), e * SLOTS * CELL, SLOTS, CELL))
        mass = listed_planes(listed, e, [4], ROWS)[0]
        back[e] = jnp.where(live_rows(fill, e), summed * inverse_mass(mass), 0.0)
        return 0

    lax.fori_loop(0, PEERS, back_step, 0, unroll=2)
    fold(total, own, rho, carried)


def cross_density(fill, plan, own, first, listed, carried):
    return pl.pallas_call(
        cross_density_kernel,
        in_specs=[SM, SM] + [VM] * 4,
        out_specs=[VM, VM],
        out_shape=[
            jax.ShapeDtypeStruct((CELLS, WIDTH), F32),
            jax.ShapeDtypeStruct((PEERS, SLOTS, WIDTH), F32),
        ],
        scratch_shapes=[
            pltpu.VMEM((2, (CELLS + 1) * CELL, 128), F32),
            pltpu.VMEM((2, LISTED * CELL, 128), F32),
            pltpu.VMEM((2, LISTED * CELL, 128), F32),
        ]
        + DENSITY_SLOT * 2,
        cost_estimate=pl.CostEstimate(
            flops=80 * 65536 * 60, bytes_accessed=2 * 2**20, transcendentals=0
        ),
        compiler_params=params(),
    )(fill, plan, own, first, listed, carried)


def pressure_kernel(
    pair, near, returned, energy_in, own, density, term, out, energy, sum_of, moving, sem
):
    copies = fetch([(energy_in, energy)], sem)
    sum_of[...] = near[...]

    def peer_step(e, _):
        for s in range(SLOTS):
            sum_of[pl.ds(pair[e, s], 1), :] += returned[e, s : s + 1]
        return 0

    lax.fori_loop(0, PEERS, peer_step, 0)
    copies[0].wait()
    full = planes_of(own, [4], 0, CELLS, CELL)[0] > 0.0
    rho = jnp.where(full, sum_of[...], 0.0)
    density[...] = rho
    term[...] = jnp.where(full, GAMMA_LESS * energy[...] / jnp.where(full, rho, 1.0), 0.0)

    def cell_step(c, _):
        moving[c] = jnp.concatenate(
            [line(own, c, CELL, k) for k in (5, 6, 7)] + [term[pl.ds(c, 1), :]], 0
        )
        return 0

    lax.fori_loop(0, CELLS, cell_step, 0, unroll=8)

    def send_step(e, _):
        for s in range(SLOTS):
            cell = moving[pair[e, s]]
            for h in range(2):
                at = (h * SLOTS + s) * MOVING
                out[e, at : at + MOVING] = half(cell, h)
        return 0

    lax.fori_loop(0, PEERS, send_step, 0)


def pressure(pair, near, returned, energy, own):
    plane = jax.ShapeDtypeStruct((CELLS, WIDTH), F32)
    return pl.pallas_call(
        pressure_kernel,
        in_specs=[SM, VM, VM, ANYWHERE, VM],
        out_specs=[VM, VM, VM],
        out_shape=[
            plane,
            plane,
            jax.ShapeDtypeStruct((PEERS, 2 * SLOTS * MOVING, 128), F32),
        ],
        scratch_shapes=[
            pltpu.VMEM((CELLS, WIDTH), F32),
            pltpu.VMEM((CELLS, WIDTH), F32),
            pltpu.VMEM((CELLS, MOVING, WIDTH), F32),
            pltpu.SemaphoreType.DMA((1,)),
        ],
        compiler_params=params(),
    )(pair, near, returned, energy, own)


def force_terms(place, m, speed, term):
    mp = m * term
    turned = sum(a * b for a, b in zip(place, speed))
    return (
        [m] + [m * a for a in place] + [mp] + [mp * a for a in place]
        + [m * a for a in speed] + [m * turned]
    )


def forces_of(sums, place, speed, term):
    lean = [a * sums[0] - b for a, b in zip(place, sums[1:4])]
    acc = [term * a + (b * sums[4] - c) for a, b, c in zip(lean, place, sums[5:8])]
    mixed = sum(a * b - c * d for a, b, c, d in zip(speed, lean, place, sums[8:11]))
    return [G_SCALE * a for a in acc] + [-G_SCALE * term * (mixed + sums[11])]


def force_operand(ref, index):
    high, low = split2(block(ref, index, SUMS))
    return jnp.concatenate([high, low], 0)


def own_terms(own, term, rows):
    planes = planes_of(own, range(CELL), 0, CELLS, CELL)
    terms = force_terms(planes[0:3], planes[4], planes[5:8], term[...])
    put(rows, terms, 0, CELLS, SUMS)
    put(rows, [jnp.zeros((CELLS, WIDTH), F32)] * 4, 12, CELLS, SUMS)
    set_block(rows, CELLS, SUMS, jnp.zeros((SUMS, WIDTH), F32))


def slopes(s_ref, high, low, columns, row, count):
    for start in range(0, count, CHUNK):
        s = jnp.maximum(s_ref[start : start + CHUNK], TINY)
        dist = s * lax.rsqrt(s)
        wide = columns[start : start + CHUNK]
        support = jnp.concatenate([wide, wide], 1) + row
        d = jnp.maximum(support - dist, 0.0)
        e = pl.reciprocal(support * support, approx=True)
        x = e * d
        g = (x * x) * (x * e)
        top = g.astype(BF)
        high[start : start + CHUNK] = top
        low[start : start + CHUNK] = (g - top.astype(F32)).astype(BF)


def distances(left, rows, count, s_ref):
    s_ref[0:count] = jnp.dot(
        left[:count], second_operands(rows, False), preferred_element_type=F32
    )


def to_seconds(rows, count, high, low):
    part = rows[:, :count]
    top = lax.dot_general(part, high[0:count], NN, preferred_element_type=F32)
    both = top + lax.dot_general(part, low[0:count], NN, preferred_element_type=F32)
    return both[:SUMS] + both[SUMS:]


def to_firsts(rows, count, high, low):
    top = lax.dot_general(rows, high[0:count], NT, preferred_element_type=F32)
    both = top + lax.dot_general(rows, low[0:count], NT, preferred_element_type=F32)
    return both[:SUMS] + both[SUMS:]


def in_three_turns(trips, item, last, products, tiles, sums, slot_a, slot_b):
    products(item(0), slot_a)

    def step(i, _):
        products(item(2 * i + 1), slot_b)
        sums(item(2 * i - 2), slot_a)
        tiles(item(2 * i), slot_a)
        after = 2 * i + 2
        products(item(after if last is None else jnp.minimum(after, last - 1)), slot_a)
        sums(item(2 * i - 1), slot_b)
        tiles(item(2 * i + 1), slot_b)
        return 0

    lax.fori_loop(0, trips, step, 0)
    sums(item(2 * trips - 2), slot_a)
    sums(item(2 * trips - 1), slot_b)


def clear(slots):
    for held in slots:
        held[...] = jnp.zeros_like(held)


def add_forces(total, own, term, out, carried):
    planes = planes_of(own, range(CELL), 0, CELLS, CELL)
    sums = planes_of(total, range(12), 0, CELLS, SUMS)
    for k, force in enumerate(forces_of(sums, planes[0:3], planes[5:8], term[...])):
        out[k] = force if carried is None else carried[k] + force


def local_force_kernel(part, plan, own, first, second, term, *rest):
    if part:
        faces, face_terms, carried, out, rows, total, face_rows, face_first, *slots = rest
    else:
        carried = None
        out, rows, total, *slots = rest
    slot_a, slot_b = slots[:7], slots[7:]
    own_terms(own, term, rows)
    total[...] = jnp.zeros_like(total)
    clear([held[k] for held in (slot_a, slot_b) for k in (2, 3, 5, 6)])

    def products(count, c, held):
        left = first_operand(block(first, c, CELL))
        held[0][...] = support_columns(line(own, c, CELL, 3))
        distances(left, block(second, c, CELL), count, held[1])
        distances(left, block(second, jnp.minimum(c + 1, CELLS), CELL), count, held[4])

    def tiles(count, c, held):
        other = line(own, jnp.minimum(c + 1, CELLS), CELL, 3)
        slopes(*held[1:4], held[0], line(own, c, CELL, 3), count)
        slopes(*held[4:7], held[0], other, count)

    def sums(count, c, held):
        after = jnp.minimum(c + 1, CELLS)
        mine, other = force_operand(rows, c), force_operand(rows, after)
        added = to_firsts(other, count, *held[5:7])
        if count < WIDTH:
            added = jnp.concatenate([added, jnp.zeros((SUMS, WIDTH - count), F32)], 1)
        add_block(total, c, SUMS, to_seconds(mine, count, *held[2:4]) + added)
        add_block(total, after, SUMS, to_seconds(mine, count, *held[5:7]))

    for kind, count in enumerate(LOCAL_ROWS):
        trips, item = cell_list(plan, part, kind)
        in_three_turns(
            trips, item, None, functools.partial(products, count),
            functools.partial(tiles, count), functools.partial(sums, count), slot_a, slot_b,
        )

    if part:
        make_face_first(faces, face_first)
        planes = planes_of(faces, range(CELL), 0, 2 * FACE, CELL)
        terms = force_terms(planes[0:3], planes[4], planes[5:8], face_terms[...])
        blank = jnp.zeros((2 * FACE, WIDTH), F32)
        put(face_rows, terms + [blank] * 4, 0, 2 * FACE, SUMS)

        def face_products(i, held):
            for k in range(2):
                n = 2 * i + k
                left = first_operand(block(face_first, n, CELL))
                distances(left, block(second, face_cell(n), CELL), WIDTH, held[1 + 3 * k])

        def face_tiles(i, held):
            for k in range(2):
                n = 2 * i + k
                columns = support_columns(line(faces, n, CELL, 3))
                slopes(
                    *held[1 + 3 * k : 4 + 3 * k], columns, line(own, face_cell(n), CELL, 3), WIDTH
                )

        def face_sums(i, held):
            for k in range(2):
                n = jnp.maximum(2 * i, 0) + k
                c = jnp.where(i < 0, CELLS, face_cell(n))
                theirs = force_operand(face_rows, n)
                add_block(
                    total, c, SUMS, to_seconds(theirs, WIDTH, *held[2 + 3 * k : 4 + 3 * k])
                )

        in_three_turns(
            FACE // 2, lambda i: i, FACE, face_products, face_tiles, face_sums, slot_a, slot_b
        )

    add_forces(total, own, term, out, carried)


FORCE_PAIR = [
    pltpu.VMEM((WIDTH, WIDTH), F32),
    pltpu.VMEM((WIDTH, WIDTH), BF),
    pltpu.VMEM((WIDTH, WIDTH), BF),
]
FORCE_SLOT = [pltpu.VMEM((WIDTH, 128), F32)] + FORCE_PAIR * 2


def local_force(part, plan, own, first, second, term, *rest):
    scratch = [
        pltpu.VMEM((2, (CELLS + 1) * SUMS, 128), F32),
        pltpu.VMEM((2, (CELLS + 1) * SUMS, 128), F32),
    ]
    if part:
        scratch.append(pltpu.VMEM((2, 2 * FACE * SUMS, 128), F32))
        scratch.append(pltpu.VMEM((2, 2 * FACE * CELL, 128), F32))
    return pl.pallas_call(
        functools.partial(local_force_kernel, part),
        in_specs=[SM] + [VM] * (4 + len(rest)),
        out_specs=VM,
        out_shape=jax.ShapeDtypeStruct((4, CELLS, WIDTH), F32),
        scratch_shapes=scratch + FORCE_SLOT * 2,
        cost_estimate=pl.CostEstimate(
            flops=64 * 65536 * 80, bytes_accessed=2 * 2**20, transcendentals=0
        ),
        compiler_params=params(),
    )(plan, own, first, second, term, *rest)


def cross_force_kernel(
    fill, plan, own, first, term, listed, arrived, carried, out, back,
    rows, total, theirs, their_rows, sums_of, *slots
):
    slot_a, slot_b = slots[:8], slots[8:]
    own_terms(own, term, rows)
    total[...] = jnp.zeros_like(total)
    clear([held[k] for held in (slot_a, slot_b) for k in (3, 4, 6, 7)])

    def peer_step(e, _):
        planes = listed_planes(listed, e, range(ROWS), ROWS)
        put(theirs, pair_terms(*planes)[1], e * SLOTS * CELL, SLOTS, CELL)
        *speed, pressed = listed_planes(arrived, e, range(MOVING), MOVING)
        terms = force_terms(planes[0:3], planes[4], speed, pressed)
        blank = jnp.zeros((SLOTS, WIDTH), F32)
        put(their_rows, terms + [blank] * 4, e * SLOTS * SUMS, SLOTS, SUMS)
        return 0

    lax.fori_loop(0, PEERS, peer_step, 0)

    def products(count, pairs, held):
        for k, (slot, c) in enumerate(pairs):
            held[k][...] = support_columns(line(own, c, CELL, 3))
            left = first_operand(block(first, c, CELL))
            distances(left, block(theirs, slot, CELL), count, held[2 + 3 * k])

    def tiles(count, pairs, held):
        for k, (slot, c) in enumerate(pairs):
            support = listed_support(listed, slot)
            slopes(*held[2 + 3 * k : 5 + 3 * k], held[k], support, count)

    def sums(count, pairs, held):
        for k, (slot, c) in enumerate(pairs):
            tile = held[3 + 3 * k : 5 + 3 * k]
            set_block(sums_of, slot, SUMS, to_seconds(force_operand(rows, c), count, *tile))
            added = to_firsts(force_operand(their_rows, slot), count, *tile)
            if count < WIDTH:
                added = jnp.concatenate([added, jnp.zeros((SUMS, WIDTH - count), F32)], 1)
            add_block(total, c, SUMS, added)

    for kind, count in enumerate(CROSS_ROWS):
        trips, item = pair_list(plan, kind)
        in_three_turns(
            trips, item, None, functools.partial(products, count),
            functools.partial(tiles, count), functools.partial(sums, count), slot_a, slot_b,
        )

    def back_step(e, _):
        planes = listed_planes(listed, e, range(3), ROWS)
        *speed, pressed = listed_planes(arrived, e, range(MOVING), MOVING)
        summed = planes_of(sums_of, range(12), e * SLOTS * SUMS, SLOTS, SUMS)
        live = live_rows(fill, e)
        for k, force in enumerate(forces_of(summed, planes, speed, pressed)):
            force = jnp.where(live, force, 0.0)
            for h in range(2):
                at = pl.ds(h * SLOTS * MOVING + k, SLOTS, stride=MOVING)
                back[e, at, :] = half(force, h)
        return 0

    lax.fori_loop(0, PEERS, back_step, 0)
    add_forces(total, own, term, out, carried)


def cross_force(fill, plan, own, first, term, listed, arrived, carried):
    return pl.pallas_call(
        cross_force_kernel,
        in_specs=[SM, SM] + [VM] * 6,
        out_specs=[VM, VM],
        out_shape=[
            jax.ShapeDtypeStruct((4, CELLS, WIDTH), F32),
            jax.ShapeDtypeStruct((PEERS, 2 * SLOTS * MOVING, 128), F32),
        ],
        scratch_shapes=[
            pltpu.VMEM((2, (CELLS + 1) * SUMS, 128), F32),
            pltpu.VMEM((2, (CELLS + 1) * SUMS, 128), F32),
            pltpu.VMEM((2, LISTED * CELL, 128), F32),
            pltpu.VMEM((2, LISTED * SUMS, 128), F32),
            pltpu.VMEM((2, LISTED * SUMS, 128), F32),
        ]
        + (FORCE_SLOT[:1] * 2 + FORCE_PAIR * 2) * 2,
        cost_estimate=pl.CostEstimate(
            flops=80 * 65536 * 80, bytes_accessed=2 * 2**20, transcendentals=0
        ),
        compiler_params=params(),
    )(fill, plan, own, first, term, listed, arrived, carried)


def finish_kernel(pair, near, returned, active_in, own, out, total, active, gate, sem):
    copies = fetch([(active_in, active)], sem)
    total[...] = jnp.zeros_like(total)

    def peer_step(e, _):
        for s in range(SLOTS):
            at = s * MOVING
            total[pair[e, s]] += both(
                lambda h: returned[
                    e, h * SLOTS * MOVING + at : h * SLOTS * MOVING + at + MOVING
                ]
            )
        return 0

    lax.fori_loop(0, PEERS, peer_step, 0)
    copies[0].wait()
    full = planes_of(own, [4], 0, CELLS, CELL)[0] > 0.0
    gate[...] = jnp.where(full, active[...].astype(F32), 0.0)

    def cell_step(c, _):
        one = pl.ds(c, 1)
        open_to = gate[one, :]
        for k in range(4):
            out[k, one, :] = (near[k, one, :] + total[c, k : k + 1]) * open_to
        return 0

    lax.fori_loop(0, CELLS, cell_step, 0, unroll=8)


def finish(pair, near, returned, active, own):
    return pl.pallas_call(
        finish_kernel,
        in_specs=[SM, VM, VM, ANYWHERE, VM],
        out_specs=VM,
        out_shape=jax.ShapeDtypeStruct((4, CELLS, WIDTH), F32),
        scratch_shapes=[
            pltpu.VMEM((CELLS, 4, WIDTH), F32),
            pltpu.VMEM((CELLS, WIDTH), jnp.int32),
            pltpu.VMEM((CELLS, WIDTH), F32),
            pltpu.SemaphoreType.DMA((1,)),
        ],
        compiler_params=params(),
    )(pair, near, returned, active, own)


def to_peers(block):
    return lax.all_to_all(block, "dev", split_axis=0, concat_axis=0, tiled=True)


def with_neighbours(rows, size):
    count = lax.axis_size("region")
    up = [(i, (i + 1) % count) for i in range(count)]
    down = [(i, (i - 1) % count) for i in range(count)]
    return jnp.concatenate(
        [
            lax.ppermute(rows[..., (CELLS - FACE) * size : CELLS * size, :], "region", up),
            lax.ppermute(rows[..., : FACE * size, :], "region", down),
        ],
        -2,
    )


def local(
    positions, velocity, smoothing, masses, energy, occupancy, active, send_cells, send_fill,
    pair_cell,
):
    pair = pair_cell[0]
    own, first, second, listed = prepare(
        occupancy, pair, positions, velocity, smoothing, masses
    )
    arrived = to_peers(listed)
    plan = make_plan(occupancy, send_fill, send_cells[0], own)
    faces = with_neighbours(own, CELL)
    rho = local_density(0, plan, own, first, second)
    rho, back = cross_density(send_fill, plan, own, first, arrived, rho)
    returned = to_peers(back)
    rho = local_density(1, plan, own, first, second, faces, rho)
    density, term, leaving = pressure(pair, rho, returned, energy, own)
    arrived_moving = to_peers(leaving)
    face_terms = with_neighbours(term, 1)
    sums = local_force(0, plan, own, first, second, term)
    sums, force_back = cross_force(
        send_fill, plan, own, first, term, arrived, arrived_moving, sums
    )
    returned_force = to_peers(force_back)
    sums = local_force(1, plan, own, first, second, term, faces, face_terms, sums)
    forces = finish(pair, sums, returned_force, active, own)
    return (density, forces)


def solution(mesh):
    cells = P(("region", "dev"), None)
    vectors = P(None, ("region", "dev"), None)
    lists = P(("region", "dev"), None, None)
    in_specs = (
        vectors, vectors, cells, cells, cells, P(("region", "dev")), cells, lists, cells, lists,
    )
    return jax.shard_map(
        local, mesh=mesh, in_specs=in_specs, out_specs=(cells, vectors), check_vma=False
    )
```

time: 169 us -> 153 us (0.905)
  the two profiles are of different devices: /device:TPU:57 before, /device:TPU:0 now
where the time goes in v3:
time: 153 us; the launch traced here: 152 us
  Pallas kernels  107 us (70%)
  starting transfers between devices  38.5 us (25%)
  local copies, waits for them, and re-layouts  3.49 us (2%)
    pallas_call x2, Pallas kernels, local_force(): pl.pallas_call(functools.partial(local_force_kernel, part), in_specs=[SM]...  33.9 us
    all_to_all x4, starting transfers between devices, to_peers(): return lax.all_to_all(block, 'dev', split_axis=0, concat_axis=0, tiled=True)  32.6 us
    pallas_call x2, Pallas kernels, local_density(): pl.pallas_call(functools.partial(local_density_kernel, part), in_specs=[S...  26.9 us
    pallas_call x1, Pallas kernels, cross_force(): pl.pallas_call(cross_force_kernel, in_specs=[SM, SM] + [VM] * 6, out_spec...  19.4 us
    pallas_call x1, Pallas kernels, cross_density(): pl.pallas_call(cross_density_kernel, in_specs=[SM, SM] + [VM] * 4, out_sp...  13.6 us
    ppermute x2, starting transfers between devices, with_neighbours(): lax.ppermute(rows[..., :FACE * size, :], 'region', down)  5.89 us
    pallas_call x1, Pallas kernels, prepare(): pl.pallas_call(prepare_kernel, in_specs=[SM] * 2 + [ANYWHERE] * 4, out_sp...  4.27 us
    pallas_call x1, Pallas kernels, make_plan(): pl.pallas_call(plan_kernel, in_specs=[SM] * 3 + [ANYWHERE], out_specs=SM,...  3.61 us
  transfers between devices with their start and end apart: 8, of which 1 were waited for; matrix products, arithmetic and copies ran while one was open for 1% of the time, Pallas kernels for 51%

profile of v3, /device:TPU:0, one launch (start us, length us, event | category | flops | bytes accessed | tf_op | source)
XLA Modules:
  0.0 151.6 jit_solution(218332358160224132)
XLA Ops:
  0.6 4.3 %shard_map.113 = (f32[2,520,128]{2,1,0:T(8,128)}, f32[2,520,128]{2,1,0:T(8,128)}, f32[2,520,128]{2,1,0:T(8,128)}, f32[16,160,128]{2,1,0:T(8,128)}) custom-call(s32[64]{0:T(128)} %occ.3, s32[16,16]{1,0:T(8,128)} %bitcast.2, f32[3,64,256]{2,1,0:T(8,128)} %pos_in.1, f32[3,64,256]{2,1,0:T(8,128)} %vel_in.1, f32[64,256]{1,0:T(8,128)} %smooth_in.1, f32[64,256]{1,0:T(8,128)} %mass_in.1), custom_call_target="tpu_custom_call" | custom-call | tf_op jit(solution)/shard_map/pallas_call | solution.py:305
  4.9 8.1 %all-to-all-start = ((f32[16,160,128]{2,1,0:T(8,128)}), f32[16,160,128]{2,1,0:T(8,128)S(1)}, u32[]{:S(2)}, u32[]{:S(2)}) async-start(f32[16,160,128]{2,1,0:T(8,128)} %get-tuple-element.16), calls=%async_computation | async-start | bytes 2621440 | tf_op jit(solution)/shard_map/all_to_all | solution.py:906
  13.1 0.8 fusion
  13.9 3.0 %collective-permute-start.1 = (f32[2,32,128]{2,1,0:T(8,128)S(1)}, f32[2,32,128]{2,1,0:T(8,128)S(1)}, u32[]{:S(2)}, u32[]{:S(2)}) collective-permute-start(f32[2,32,128]{2,1,0:T(8,128)S(1)} %get-tuple-element.24), channel_id=1, source_target_pairs={{0,112},{16,0},{32,16},{48,32},{64,48},{80,64},{96,80},{112,96},{1... | collective-permute-start | bytes 98312 | tf_op jit(solution)/shard_map/ppermute | solution.py:916
  16.8 3.6 %shard_map.114.plan = s32[1536]{0:T(1024)} custom-call(s32[64]{0:T(128)} %occ.3, s32[1,16]{1,0:T(1,128)} %fill.5, s32[16,16]{1,0:T(8,128)} %bitcast.5, f32[2,520,128]{2,1,0:T(8,128)} %get-tuple-element.13._.own), custom_call_target="tpu_custom_call" | custom-call | tf_op jit(solution)/shard_map/pallas_call | solution.py:241
  20.5 0.7 copy-done.6
  21.2 14.9 %shard_map.115.carried = f32[64,256]{1,0:T(8,128)S(1)} custom-call(s32[1536]{0:T(1024)S(1)} %copy-done.6, f32[2,520,128]{2,1,0:T(8,128)S(1)} %copy-done, f32[2,520,128]{2,1,0:T(8,128)S(1)} %copy-done.1, f32[2,520,128]{2,1,0:T(8,128)S(1)} %copy-done.3), custom_call_target="tpu_custom_call" | custom-call | flops 251658240 | bytes 2097152 | tf_op jit(solution)/shard_map/pallas_call | solution.py:420
  36.1 13.6 %shard_map.116 = (f32[64,256]{1,0:T(8,128)S(1)}, f32[16,16,256]{2,1,0:T(8,128)}) custom-call(s32[1,16]{1,0:T(1,128)S(1)} %copy-done.11, s32[1536]{0:T(1024)S(1)} %copy-done.7, f32[2,520,128]{2,1,0:T(8,128)S(1)} %copy-done, f32[2,520,128]{2,1,0:T(8,128)S(1)} %copy-done.1, f32[16,160,128]{2,1,0:T(8,128)S(1)} %all-to-all-done.listed, ...), custom_call_target="tpu_custom_call" | custom-call | flops 314572800 | bytes 2097152 | tf_op jit(solution)/shard_map/pallas_call | solution.py:497
  49.7 8.6 %all-to-all-start.1 = ((f32[16,16,256]{2,1,0:T(8,128)}), f32[16,16,256]{2,1,0:T(8,128)S(1)}, u32[]{:S(2)}, u32[]{:S(2)}) async-start(f32[16,16,256]{2,1,0:T(8,128)} %get-tuple-element.18), calls=%async_computation.1 | async-start | bytes 524288 | tf_op jit(solution)/shard_map/all_to_all | solution.py:906
  58.4 12.0 %shard_map.117.near = f32[64,256]{1,0:T(8,128)S(1)} custom-call(s32[1536]{0:T(1024)S(1)} %copy-done.7, f32[2,520,128]{2,1,0:T(8,128)S(1)} %copy-done, f32[2,520,128]{2,1,0:T(8,128)S(1)} %copy-done.1, f32[2,520,128]{2,1,0:T(8,128)S(1)} %copy-done.3, f32[2,64,128]{2,1,0:T(8,128)S(1)} %constant_dynamic-update-slice_fusion.rest_0_, ...), custom_call_target="tpu_custom_call" | custom-call | flops 251658240 | bytes 2097152 | tf_op jit(solution)/shard_map/pallas_call | solution.py:420
  70.4 3.0 %shard_map.118 = (f32[64,256]{1,0:T(8,128)}, f32[64,256]{1,0:T(8,128)S(1)}, f32[16,128,128]{2,1,0:T(8,128)S(1)}) custom-call(s32[16,16]{1,0:T(8,128)S(1)} %bitcast.3, f32[64,256]{1,0:T(8,128)S(1)} %shard_map.117.near, f32[16,16,256]{2,1,0:T(8,128)S(1)} %all-to-all-done.1.returned, f32[64,256]{1,0:T(8,128)S(1)} %copy-done.9, f32[2,520,128]{2,1,0:T(8,128)S(1)} %copy-done), custom_call_target="tpu_custom_call" | custom-call | tf_op jit(solution)/shard_map/pallas_call | solution.py:557
  73.4 1.0 copy-done.5
  74.4 7.1 %all-to-all-start.2 = ((f32[16,128,128]{2,1,0:T(8,128)}), f32[16,128,128]{2,1,0:T(8,128)S(1)}, u32[]{:S(2)}, u32[]{:S(2)}) async-start(f32[16,128,128]{2,1,0:T(8,128)} %copy-done.5), calls=%async_computation.2 | async-start | bytes 2097152 | tf_op jit(solution)/shard_map/all_to_all | solution.py:906
  81.5 18.9 %shard_map.119.carried = f32[4,64,256]{2,1,0:T(8,128)S(1)} custom-call(s32[1536]{0:T(1024)S(1)} %copy-done.7, f32[2,520,128]{2,1,0:T(8,128)S(1)} %copy-done, f32[2,520,128]{2,1,0:T(8,128)S(1)} %copy-done.1, f32[2,520,128]{2,1,0:T(8,128)S(1)} %copy-done.3, f32[64,256]{1,0:T(8,128)S(1)} %get-tuple-element.20.term), custom_call_target="tpu_custom_call" | custom-call | flops 335544320 | bytes 2097152 | tf_op jit(solution)/shard_map/pallas_call | solution.py:760
  100.4 19.4 %shard_map.120 = (f32[4,64,256]{2,1,0:T(8,128)S(1)}, f32[16,128,128]{2,1,0:T(8,128)S(1)}) custom-call(s32[1,16]{1,0:T(1,128)S(1)} %copy-done.11, s32[1536]{0:T(1024)S(1)} %copy-done.7, f32[2,520,128]{2,1,0:T(8,128)S(1)} %copy-done, f32[2,520,128]{2,1,0:T(8,128)S(1)} %copy-done.1, f32[64,256]{1,0:T(8,128)S(1)} %get-tuple-element.20.term, ...), custom_call_target="tpu_custom_call" | custom-call | flops 419430400 | bytes 2097152 | tf_op jit(solution)/shard_map/pallas_call | solution.py:837
  119.9 1.0 copy-done.4
  120.8 8.7 %all-to-all-start.3 = ((f32[16,128,128]{2,1,0:T(8,128)}), f32[16,128,128]{2,1,0:T(8,128)S(1)}, u32[]{:S(2)}, u32[]{:S(2)}) async-start(f32[16,128,128]{2,1,0:T(8,128)} %copy-done.4), calls=%async_computation.3 | async-start | bytes 2097152 | tf_op jit(solution)/shard_map/all_to_all | solution.py:906
  129.6 0.0 copy-start.10
  129.6 0.0 collective-permute-start.2
  129.6 2.9 %collective-permute-start.3 = (f32[4,256]{1,0:T(4,128)S(1)}, f32[4,256]{1,0:T(4,128)S(1)}, u32[]{:S(2)}, u32[]{:S(2)}) collective-permute-start(f32[4,256]{1,0:T(4,128)S(1)} %get-tuple-element.27), channel_id=1, source_target_pairs={{0,112},{16,0},{32,16},{48,32},{64,48},{80,64},{96,80},{112,96},{1... | collective-permute-start | bytes 12296 | tf_op jit(solution)/shard_map/ppermute | solution.py:916
  132.6 1.3 collective-permute-done.2
  133.8 0.0 collective-permute-done.3
  133.9 15.0 %shard_map.121.near = f32[4,64,256]{2,1,0:T(8,128)S(1)} custom-call(s32[1536]{0:T(1024)S(1)} %copy-done.7, f32[2,520,128]{2,1,0:T(8,128)S(1)} %copy-done, f32[2,520,128]{2,1,0:T(8,128)S(1)} %copy-done.1, f32[2,520,128]{2,1,0:T(8,128)S(1)} %copy-done.3, f32[64,256]{1,0:T(8,128)S(1)} %get-tuple-element.20.term, ...), custom_call_target="tpu_custom_call" | custom-call | flops 335544320 | bytes 2097152 | tf_op jit(solution)/shard_map/pallas_call | solution.py:760
  148.9 2.5 %shard_map.122 = f32[4,64,256]{2,1,0:T(8,128)} custom-call(s32[16,16]{1,0:T(8,128)S(1)} %bitcast.4, f32[4,64,256]{2,1,0:T(8,128)S(1)} %shard_map.121.near, f32[16,128,128]{2,1,0:T(8,128)S(1)} %all-to-all-done.3.returned, s32[64,256]{1,0:T(8,128)S(1)} %copy-done.10, f32[2,520,128]{2,1,0:T(8,128)S(1)} %copy-done), custom_call_target="tpu_custom_call" | custom-call | tf_op jit(solution)/shard_map/pallas_call | solution.py:890
  (31 shorter events, 0.1 us)
Async XLA Ops:
  4.9 15.5 %copy-start = (f32[2,520,128]{2,1,0:T(8,128)S(1)}, f32[2,520,128]{2,1,0:T(8,128)}, u32[]{:S(2)}) copy-start(f32[2,520,128]{2,1,0:T(8,128)} %get-tuple-element.13._.own) | copy-start | bytes 1597444
  4.9 15.5 %copy-start.1 = (f32[2,520,128]{2,1,0:T(8,128)S(1)}, f32[2,520,128]{2,1,0:T(8,128)}, u32[]{:S(2)}) copy-start(f32[2,520,128]{2,1,0:T(8,128)} %get-tuple-element.14.first) | copy-start | bytes 1597444
  4.9 15.5 %copy-start.3 = (f32[2,520,128]{2,1,0:T(8,128)S(1)}, f32[2,520,128]{2,1,0:T(8,128)}, u32[]{:S(2)}) copy-start(f32[2,520,128]{2,1,0:T(8,128)} %get-tuple-element.15.second) | copy-start | bytes 1597444
  4.9 31.2 %all-to-all-start = ((f32[16,160,128]{2,1,0:T(8,128)}), f32[16,160,128]{2,1,0:T(8,128)S(1)}, u32[]{:S(2)}, u32[]{:S(2)}) async-start(f32[16,160,128]{2,1,0:T(8,128)} %get-tuple-element.16), calls=%async_computation | async-start | bytes 2621440 | tf_op jit(solution)/shard_map/all_to_all | solution.py:906
  13.1 23.1 %copy-start.11 = (s32[1,16]{1,0:T(1,128)S(1)}, s32[1,16]{1,0:T(1,128)}, u32[]{:S(2)}) copy-start(s32[1,16]{1,0:T(1,128)} %fill.5) | copy-start | bytes 196
  13.8 44.5 %collective-permute-start = (f32[2,32,128]{2,1,0:T(8,128)S(1)}, f32[2,32,128]{2,1,0:T(8,128)S(1)}, u32[]{:S(2)}, u32[]{:S(2)}) collective-permute-start(f32[2,32,128]{2,1,0:T(8,128)S(1)} %get-tuple-element.25), channel_id=1, source_target_pairs={{0,16},{16,32},{32,48},{48,64},{64,80},{80,96},{96,112},{112,0},{1... | collective-permute-start | bytes 98312 | tf_op jit(solution)/shard_map/ppermute | solution.py:915
  13.9 44.5 %collective-permute-start.1 = (f32[2,32,128]{2,1,0:T(8,128)S(1)}, f32[2,32,128]{2,1,0:T(8,128)S(1)}, u32[]{:S(2)}, u32[]{:S(2)}) collective-permute-start(f32[2,32,128]{2,1,0:T(8,128)S(1)} %get-tuple-element.24), channel_id=1, source_target_pairs={{0,112},{16,0},{32,16},{48,32},{64,48},{80,64},{96,80},{112,96},{1... | collective-permute-start | bytes 98312 | tf_op jit(solution)/shard_map/ppermute | solution.py:916
  20.5 0.7 copy-start.6
  21.2 15.0 %copy-start.7 = (s32[1536]{0:T(1024)S(1)}, s32[1536]{0:T(1024)}, u32[]{:S(2)}) copy-start(s32[1536]{0:T(1024)} %shard_map.114.plan) | copy-start | bytes 18436
  36.1 13.6 %copy-start.2 = (f32[16,160,128]{2,1,0:T(8,128)}, f32[16,160,128]{2,1,0:T(8,128)S(1)}, u32[]{:S(2)}) copy-start(f32[16,160,128]{2,1,0:T(8,128)S(1)} %all-to-all-done.listed) | copy-start | bytes 3932164
  49.7 20.7 %copy-start.8 = (s32[1,16,16]{2,1,0:T(8,128)S(1)}, s32[1,16,16]{2,1,0:T(8,128)}, u32[]{:S(2)}) copy-start(s32[1,16,16]{2,1,0:T(8,128)} %param.19) | copy-start | bytes 3076
  49.7 20.7 %copy-start.9 = (f32[64,256]{1,0:T(8,128)S(1)}, f32[64,256]{1,0:T(8,128)}, u32[]{:S(2)}) copy-start(f32[64,256]{1,0:T(8,128)} %energy_in.1) | copy-start | bytes 196612
  49.7 20.7 %all-to-all-start.1 = ((f32[16,16,256]{2,1,0:T(8,128)}), f32[16,16,256]{2,1,0:T(8,128)S(1)}, u32[]{:S(2)}, u32[]{:S(2)}) async-start(f32[16,16,256]{2,1,0:T(8,128)} %get-tuple-element.18), calls=%async_computation.1 | async-start | bytes 524288 | tf_op jit(solution)/shard_map/all_to_all | solution.py:906
  73.4 1.0 copy-start.5
  74.4 26.1 %all-to-all-start.2 = ((f32[16,128,128]{2,1,0:T(8,128)}), f32[16,128,128]{2,1,0:T(8,128)S(1)}, u32[]{:S(2)}, u32[]{:S(2)}) async-start(f32[16,128,128]{2,1,0:T(8,128)} %copy-done.5), calls=%async_computation.2 | async-start | bytes 2097152 | tf_op jit(solution)/shard_map/all_to_all | solution.py:906
  119.8 1.0 copy-start.4
  120.8 28.1 %all-to-all-start.3 = ((f32[16,128,128]{2,1,0:T(8,128)}), f32[16,128,128]{2,1,0:T(8,128)S(1)}, u32[]{:S(2)}, u32[]{:S(2)}) async-start(f32[16,128,128]{2,1,0:T(8,128)} %copy-done.4), calls=%async_computation.3 | async-start | bytes 2097152 | tf_op jit(solution)/shard_map/all_to_all | solution.py:906
  129.6 19.4 %copy-start.10 = (s32[64,256]{1,0:T(8,128)S(1)}, s32[64,256]{1,0:T(8,128)}, u32[]{:S(2)}) copy-start(s32[64,256]{1,0:T(8,128)} %active_in.1) | copy-start | bytes 196612
  129.6 4.3 %collective-permute-start.2 = (f32[4,256]{1,0:T(4,128)S(1)}, f32[4,256]{1,0:T(4,128)S(1)}, u32[]{:S(2)}, u32[]{:S(2)}) collective-permute-start(f32[4,256]{1,0:T(4,128)S(1)} %get-tuple-element.26), channel_id=1, source_target_pairs={{0,16},{16,32},{32,48},{48,64},{64,80},{80,96},{96,112},{112,0},{1... | collective-permute-start | bytes 12296 | tf_op jit(solution)/shard_map/ppermute | solution.py:915
  129.6 4.3 %collective-permute-start.3 = (f32[4,256]{1,0:T(4,128)S(1)}, f32[4,256]{1,0:T(4,128)S(1)}, u32[]{:S(2)}, u32[]{:S(2)}) collective-permute-start(f32[4,256]{1,0:T(4,128)S(1)} %get-tuple-element.27), channel_id=1, source_target_pairs={{0,112},{16,0},{32,16},{48,32},{64,48},{80,64},{96,80},{112,96},{1... | collective-permute-start | bytes 12296 | tf_op jit(solution)/shard_map/ppermute | solution.py:916

commit v4 on v3

--- a/solution.py
+++ b/solution.py
@@ -31,15 +31,17 @@
 ROWS = 5
 MOVING = 4
 SPLIT = 40
-LOCAL_ROWS = (192, 224, 256)
-CROSS_ROWS = (192, 256)
+SIZES = (160, 192, 224, 256)
+KINDS = len(SIZES)
 UNIT = 4
 LOCAL_AT = 16
-LOCAL_LIST = 72
-LEAD = UNIT + 3
-CROSS_AT = LOCAL_AT + 2 * len(LOCAL_ROWS) * LOCAL_LIST
+LOCAL_LEAD = 2
+LOCAL_LIST = CELLS + 8
+CROSS_AT = LOCAL_AT + 2 * LOCAL_LIST
+CROSS_LEAD = 4
 CROSS_LIST = LISTED + 16
-PLAN = CROSS_AT + 2 * len(CROSS_ROWS) * CROSS_LIST
+PLAN = CROSS_AT + CROSS_LIST
+PACK = 128
 ANYWHERE = pl.BlockSpec(memory_space=pl.ANY)
 
 
@@ -109,10 +111,11 @@
     return both(lambda h: ref[h, pl.ds(index * size + k, 1), :])
 
 
-def listed_planes(listed, e, ids, size):
+def listed_planes(listed, e, part, ids, size):
     step = SLOTS * size
+    start = 8 * part * size
     return [
-        both(lambda h: listed[e, pl.ds(h * step + k, SLOTS, stride=size), :]) for k in ids
+        both(lambda h: listed[e, pl.ds(h * step + start + k, 8, stride=size), :]) for k in ids
     ]
 
 
@@ -140,10 +143,9 @@
     return jnp.broadcast_to(row, (128, WIDTH)).T
 
 
-def density_products(left, operands, count, s_ref, mix_ref):
-    part = left[:count]
-    s_ref[0:count] = jnp.dot(part, operands[0], preferred_element_type=F32)
-    mix_ref[0:count] = jnp.dot(part, operands[1], preferred_element_type=F32)
+def density_products(left, operands, s_ref, mix_ref):
+    s_ref[...] = jnp.dot(left, operands[0], preferred_element_type=F32)
+    mix_ref[...] = jnp.dot(left, operands[1], preferred_element_type=F32)
 
 
 def density_weights(count, s_ref, mix_ref, columns, row, one_sided):
@@ -178,63 +180,74 @@
     return jnp.where(m > 0.0, W_SCALE / jnp.where(m > 0.0, m, 1.0), 0.0)
 
 
-def plan_kernel(occ, fill, cells, _, plan):
-    classes = len(LOCAL_ROWS)
-    for kind in range(2 * classes):
-        plan[kind] = 0
-        for k in range(2):
-            plan[LOCAL_AT + kind * LOCAL_LIST + k] = CELLS
-
-    def local_step(c, _):
-        size = occ[c]
-        kind = sum((size > rows).astype(jnp.int32) for rows in LOCAL_ROWS[:-1])
-        kind = kind + jnp.where(c >= SPLIT, classes, 0)
-        count = plan[kind]
-        plan[LOCAL_AT + kind * LOCAL_LIST + 2 + count] = c
-        plan[kind] = count + 1
+def kind_of(size):
+    return sum((size > rows).astype(jnp.int32) for rows in SIZES[:-1])
+
+
+def plan_kernel(occ, fill, cells, _, plan, next_at):
+    for k in range(3 * KINDS):
+        next_at[k] = 0
+
+    def local_count(c, _):
+        kind = kind_of(occ[c]) + jnp.where(c >= SPLIT, KINDS, 0)
+        next_at[kind] = next_at[kind] + 1
         return 0
 
-    lax.fori_loop(0, CELLS, local_step, 0)
-    for kind in range(2 * classes):
-        count = plan[kind]
-        for k in range(2):
-            plan[LOCAL_AT + kind * LOCAL_LIST + 2 + count + k] = CELLS
-        plan[kind] = (count + 1) // 2
-
-    base = 2 * classes
+    lax.fori_loop(0, CELLS, local_count, 0)
+
+    def over_pairs(visit):
+        def peer_step(e, _):
+            def slot_step(s, _):
+                cell = cells[e, s]
+                visit(2 * KINDS + kind_of(occ[cell]), (e * SLOTS + s) * PACK + cell)
+                return 0
+
+            return lax.fori_loop(0, fill[0, e], slot_step, 0)
+
+        lax.fori_loop(0, PEERS, peer_step, 0)
+
+    def pair_count(kind, _):
+        next_at[kind] = next_at[kind] + 1
+
+    over_pairs(pair_count)
 
     unused = jnp.int32(0)
     for e in range(PEERS):
         unused = jnp.where(fill[0, e] == 0, e * SLOTS, unused)
 
-    def blank(at):
-        plan[at] = unused
-        plan[at + CROSS_LIST] = CELLS
-
-    for kind in range(len(CROSS_ROWS)):
-        for k in range(LEAD):
-            blank(CROSS_AT + 2 * kind * CROSS_LIST + k)
-
-    def peer_step(e, counts):
-        def slot_step(s, counts):
-            cell = cells[e, s]
-            wide = (occ[cell] > CROSS_ROWS[0]).astype(jnp.int32)
-            at = CROSS_AT + LEAD + jnp.where(
-                wide > 0, 2 * CROSS_LIST + counts[1], counts[0]
-            )
-            plan[at] = e * SLOTS + s
-            plan[at + CROSS_LIST] = cell
-            return (counts[0] + 1 - wide, counts[1] + wide)
-
-        return lax.fori_loop(0, fill[0, e], slot_step, counts)
-
-    counts = lax.fori_loop(0, PEERS, peer_step, (jnp.int32(0), jnp.int32(0)))
-    for kind in range(len(CROSS_ROWS)):
-        trips = (counts[kind] + UNIT - 1) // UNIT
-        plan[base + 2 * kind] = trips
-        plan[base + 2 * kind + 1] = LEAD + counts[kind] - UNIT * trips
-        for k in range(2):
-            blank(CROSS_AT + 2 * kind * CROSS_LIST + LEAD + counts[kind] + k)
+    for group, (start, lead, unit, blank) in enumerate(
+        [
+            (LOCAL_AT, LOCAL_LEAD, 2, CELLS),
+            (LOCAL_AT + LOCAL_LIST, LOCAL_LEAD, 2, CELLS),
+            (CROSS_AT, CROSS_LEAD, UNIT, unused * PACK + CELLS),
+        ]
+    ):
+        total = jnp.int32(0)
+        done = jnp.int32(0)
+        for k in range(KINDS):
+            at = group * KINDS + k
+            count = next_at[at]
+            next_at[at] = start + lead + total
+            total = total + count
+            upto = (total + (unit - 1 if k == KINDS - 1 else 0)) // unit
+            plan[at] = upto - done
+            done = upto
+        for k in range(lead):
+            plan[start + k] = blank
+        for k in range(unit + 1):
+            plan[start + lead + total + k] = blank
+
+    def place(kind, value):
+        at = next_at[kind]
+        plan[at] = value
+        next_at[kind] = at + 1
+
+    def local_place(c, _):
+        place(kind_of(occ[c]) + jnp.where(c >= SPLIT, KINDS, 0), c)
+        return 0
+
+    lax.fori_loop(0, CELLS, local_place, 0)
+    over_pairs(place)
 
 
 def make_plan(occ, fill, cells, own):
@@ -243,6 +256,7 @@
         in_specs=[SM] * 3 + [ANYWHERE],
         out_specs=SM,
         out_shape=jax.ShapeDtypeStruct((PLAN,), jnp.int32),
+        scratch_shapes=[pltpu.SMEM((3 * KINDS,), jnp.int32)],
     )(occ, fill, cells, own)
 
 
@@ -336,24 +350,56 @@
     return jnp.where(n < FACE, n, CELLS - 2 * FACE + n)
 
 
-def in_turns(trips, item, last, products, weights, slot_a, slot_b):
+def in_turns(trips, sizes, item, last, products, weights, slot_a, slot_b):
     products(item(0), slot_a)
-
-    def step(i, _):
-        products(item(2 * i + 1), slot_b)
-        weights(item(2 * i), slot_a)
-        after = 2 * i + 2
-        products(item(after if last is None else jnp.minimum(after, last - 1)), slot_a)
-        weights(item(2 * i + 1), slot_b)
+    base = 0
+    for count, size in zip(trips, sizes):
+
+        def step(i, _, size=size):
+            products(item(2 * i + 1), slot_b)
+            weights(size, item(2 * i), slot_a)
+            after = 2 * i + 2
+            products(item(after if last is None else jnp.minimum(after, last - 1)), slot_a)
+            weights(size, item(2 * i + 1), slot_b)
+            return 0
+
+        lax.fori_loop(base, base + count, step, 0)
+        base = base + count
+
+
+def cell_list(plan, part):
+    start = LOCAL_AT + part * LOCAL_LIST + LOCAL_LEAD
+    return [plan[part * KINDS + k] for k in range(KINDS)], lambda n: plan[start + n]
+
+
+def pair_list(plan):
+    start = CROSS_AT + CROSS_LEAD
+
+    def item(n):
+        entries = [plan[start + 2 * n + k] for k in range(2)]
+        return [(entry // PACK, entry % PACK) for entry in entries]
+
+    return [plan[2 * KINDS + k] for k in range(KINDS)], item
+
+
+def live_parts(fill, visit, other):
+    def step(n, _):
+        e, part = n // 2, n % 2
+        live = fill[0, e] > 8 * part
+
+        @pl.when(live)
+        def _():
+            visit(e, part)
+
+        if other is not None:
+
+            @pl.when(jnp.logical_not(live))
+            def _():
+                other(e, part)
+
         return 0
 
-    lax.fori_loop(0, trips, step, 0)
-
-
-def cell_list(plan, part, kind):
-    at = kind + part * len(LOCAL_ROWS)
-    start = LOCAL_AT + at * LOCAL_LIST + 2
-    return plan[at], lambda n: plan[start + n]
+    lax.fori_loop(0, 2 * PEERS, step, 0)
 
 
 def local_density_kernel(part, plan, own, first, second, *rest):
@@ -365,14 +411,12 @@
     slot_a, slot_b = slots[:6], slots[6:]
     total[...] = jnp.zeros_like(total)
 
-    def products(count, c, held):
+    def products(c, held):
         left = first_operand(block(first, c, CELL))
         after = jnp.minimum(c + 1, CELLS)
         held[4][...] = support_columns(line(own, c, CELL, 3))
-        density_products(left, second_operands(block(second, c, CELL), True), count, *held[0:2])
-        density_products(
-            left, second_operands(block(second, after, CELL), True), count, *held[2:4]
-        )
+        density_products(left, second_operands(block(second, c, CELL), True), *held[0:2])
+        density_products(left, second_operands(block(second, after, CELL), True), *held[2:4])
 
     def weights(count, c, held):
         after = jnp.minimum(c + 1, CELLS)
@@ -382,12 +426,8 @@
         add_block(total, c, CELL, own_sum + here)
         add_block(total, after, CELL, there)
 
-    for kind, count in enumerate(LOCAL_ROWS):
-        trips, item = cell_list(plan, part, kind)
-        in_turns(
-            trips, item, None, functools.partial(products, count),
-            functools.partial(weights, count), slot_a, slot_b,
-        )
+    trips, item = cell_list(plan, part)
+    in_turns(trips, SIZES, item, None, products, weights, slot_a, slot_b)
 
     if part:
         make_face_first(faces, face_first)
@@ -398,17 +438,19 @@
                 left = first_operand(block(face_first, n, CELL))
                 operands = second_operands(block(second, face_cell(n), CELL), True)
                 held[4 + k][...] = support_columns(line(faces, n, CELL, 3))
-                density_products(left, operands, WIDTH, *held[2 * k : 2 * k + 2])
-
-        def face_weights(i, held):
+                density_products(left, operands, *held[2 * k : 2 * k + 2])
+
+        def face_weights(size, i, held):
             for k in range(2):
                 c = face_cell(2 * i + k)
                 added = density_weights(
-                    WIDTH, *held[2 * k : 2 * k + 2], held[4 + k], line(own, c, CELL, 3), True
+                    size, *held[2 * k : 2 * k + 2], held[4 + k], line(own, c, CELL, 3), True
                 )
                 add_block(total, c, CELL, added)
 
-        in_turns(FACE // 2, lambda i: i, FACE, face_products, face_weights, slot_a, slot_b)
+        in_turns(
+            [FACE // 2], [WIDTH], lambda i: i, FACE, face_products, face_weights, slot_a, slot_b
+        )
 
     fold(total, own, rho, carried)
 
@@ -432,19 +474,9 @@
     )(plan, own, first, second, *rest)
 
 
-def pair_list(plan, kind):
-    base = 2 * len(LOCAL_ROWS) + 2 * kind
-    at = CROSS_AT + 2 * kind * CROSS_LIST + plan[base + 1]
-
-    def item(n):
-        return [(plan[at + 2 * n + k], plan[at + CROSS_LIST + 2 * n + k]) for k in range(2)]
-
-    return plan[base], item
-
-
-def live_rows(fill, e):
-    row = lax.broadcasted_iota(jnp.int32, (SLOTS, WIDTH), 0)
-    return row < fill[0, e]
+def live_rows(fill, e, part):
+    row = lax.broadcasted_iota(jnp.int32, (8, WIDTH), 0)
+    return row < fill[0, e] - 8 * part
 
 
 def cross_density_kernel(
@@ -453,19 +485,18 @@
     slot_a, slot_b = slots[:6], slots[6:]
     total[...] = jnp.zeros_like(total)
 
-    def peer_step(e, _):
-        after = pair_terms(*listed_planes(listed, e, range(ROWS), ROWS))[1]
-        put(theirs, after, e * SLOTS * CELL, SLOTS, CELL)
-        return 0
-
-    lax.fori_loop(0, PEERS, peer_step, 0, unroll=2)
-
-    def products(count, pairs, held):
+    def make(e, part):
+        after = pair_terms(*listed_planes(listed, e, part, range(ROWS), ROWS))[1]
+        put(theirs, after, (e * SLOTS + 8 * part) * CELL, 8, CELL)
+
+    live_parts(fill, make, None)
+
+    def products(pairs, held):
         for k, (slot, c) in enumerate(pairs):
             left = first_operand(block(first, c, CELL))
             held[4 + k][...] = support_columns(line(own, c, CELL, 3))
             operands = second_operands(block(theirs, slot, CELL), True)
-            density_products(left, operands, count, *held[2 * k : 2 * k + 2])
+            density_products(left, operands, *held[2 * k : 2 * k + 2])
 
     def weights(count, pairs, held):
         for k, (slot, c) in enumerate(pairs):
@@ -476,20 +507,20 @@
             add_block(total, c, CELL, here)
             set_block(there_of, slot, CELL, there)
 
-    for kind, count in enumerate(CROSS_ROWS):
-        trips, item = pair_list(plan, kind)
-        in_turns(
-            trips, item, None, functools.partial(products, count),
-            functools.partial(weights, count), slot_a, slot_b,
-        )
-
-    def back_step(e, _):
-        summed = sum(planes_of(there_of, range(CELL), e * SLOTS * CELL, SLOTS, CELL))
-        mass = listed_planes(listed, e, [4], ROWS)[0]
-        back[e] = jnp.where(live_rows(fill, e), summed * inverse_mass(mass), 0.0)
-        return 0
-
-    lax.fori_loop(0, PEERS, back_step, 0, unroll=2)
+    trips, item = pair_list(plan)
+    in_turns(trips, SIZES, item, None, products, weights, slot_a, slot_b)
+
+    def send(e, part):
+        start = (e * SLOTS + 8 * part) * CELL
+        summed = sum(planes_of(there_of, range(CELL), start, 8, CELL))
+        mass = listed_planes(listed, e, part, [4], ROWS)[0]
+        value = jnp.where(live_rows(fill, e, part), summed * inverse_mass(mass), 0.0)
+        back[e, rows_at(part, 8), :] = value
+
+    def send_none(e, part):
+        back[e, rows_at(part, 8), :] = jnp.zeros((8, WIDTH), F32)
+
+    live_parts(fill, send, send_none)
     fold(total, own, rho, carried)
 
 
@@ -617,10 +648,8 @@
         low[start : start + CHUNK] = (g - top.astype(F32)).astype(BF)
 
 
-def distances(left, rows, count, s_ref):
-    s_ref[0:count] = jnp.dot(
-        left[:count], second_operands(rows, False), preferred_element_type=F32
-    )
+def distances(left, rows, s_ref):
+    s_ref[...] = jnp.dot(left, second_operands(rows, False), preferred_element_type=F32)
 
 
 def to_seconds(rows, count, high, low):
@@ -636,22 +665,25 @@
     return both[:SUMS] + both[SUMS:]
 
 
-def in_three_turns(trips, item, last, products, tiles, sums, slot_a, slot_b):
+def in_three_turns(trips, sizes, item, last, products, tiles, sums, slot_a, slot_b):
     products(item(0), slot_a)
-
-    def step(i, _):
-        products(item(2 * i + 1), slot_b)
-        sums(item(2 * i - 2), slot_a)
-        tiles(item(2 * i), slot_a)
-        after = 2 * i + 2
-        products(item(after if last is None else jnp.minimum(after, last - 1)), slot_a)
-        sums(item(2 * i - 1), slot_b)
-        tiles(item(2 * i + 1), slot_b)
-        return 0
-
-    lax.fori_loop(0, trips, step, 0)
-    sums(item(2 * trips - 2), slot_a)
-    sums(item(2 * trips - 1), slot_b)
+    base = 0
+    for count, size in zip(trips, sizes):
+
+        def step(i, _, size=size):
+            products(item(2 * i + 1), slot_b)
+            sums(size, item(2 * i - 2), slot_a)
+            tiles(size, item(2 * i), slot_a)
+            after = 2 * i + 2
+            products(item(after if last is None else jnp.minimum(after, last - 1)), slot_a)
+            sums(size, item(2 * i - 1), slot_b)
+            tiles(size, item(2 * i + 1), slot_b)
+            return 0
+
+        lax.fori_loop(base, base + count, step, 0)
+        base = base + count
+    sums(sizes[-1], item(2 * base - 2), slot_a)
+    sums(sizes[-1], item(2 * base - 1), slot_b)
 
 
 def clear(slots):
@@ -677,11 +709,11 @@
     total[...] = jnp.zeros_like(total)
     clear([held[k] for held in (slot_a, slot_b) for k in (2, 3, 5, 6)])
 
-    def products(count, c, held):
+    def products(c, held):
         left = first_operand(block(first, c, CELL))
         held[0][...] = support_columns(line(own, c, CELL, 3))
-        distances(left, block(second, c, CELL), count, held[1])
-        distances(left, block(second, jnp.minimum(c + 1, CELLS), CELL), count, held[4])
+        distances(left, block(second, c, CELL), held[1])
+        distances(left, block(second, jnp.minimum(c + 1, CELLS), CELL), held[4])
 
     def tiles(count, c, held):
         other = line(own, jnp.minimum(c + 1, CELLS), CELL, 3)
@@ -697,12 +729,8 @@
         add_block(total, c, SUMS, to_seconds(mine, count, *held[2:4]) + added)
         add_block(total, after, SUMS, to_seconds(mine, count, *held[5:7]))
 
-    for kind, count in enumerate(LOCAL_ROWS):
-        trips, item = cell_list(plan, part, kind)
-        in_three_turns(
-            trips, item, None, functools.partial(products, count),
-            functools.partial(tiles, count), functools.partial(sums, count), slot_a, slot_b,
-        )
+    trips, item = cell_list(plan, part)
+    in_three_turns(trips, SIZES, item, None, products, tiles, sums, slot_a, slot_b)
 
     if part:
         make_face_first(faces, face_first)
@@ -715,27 +743,28 @@
             for k in range(2):
                 n = 2 * i + k
                 left = first_operand(block(face_first, n, CELL))
-                distances(left, block(second, face_cell(n), CELL), WIDTH, held[1 + 3 * k])
-
-        def face_tiles(i, held):
+                distances(left, block(second, face_cell(n), CELL), held[1 + 3 * k])
+
+        def face_tiles(size, i, held):
             for k in range(2):
                 n = 2 * i + k
                 columns = support_columns(line(faces, n, CELL, 3))
                 slopes(
-                    *held[1 + 3 * k : 4 + 3 * k], columns, line(own, face_cell(n), CELL, 3), WIDTH
+                    *held[1 + 3 * k : 4 + 3 * k], columns, line(own, face_cell(n), CELL, 3), size
                 )
 
-        def face_sums(i, held):
+        def face_sums(size, i, held):
             for k in range(2):
                 n = jnp.maximum(2 * i, 0) + k
                 c = jnp.where(i < 0, CELLS, face_cell(n))
                 theirs = force_operand(face_rows, n)
                 add_block(
-                    total, c, SUMS, to_seconds(theirs, WIDTH, *held[2 + 3 * k : 4 + 3 * k])
+                    total, c, SUMS, to_seconds(theirs, size, *held[2 + 3 * k : 4 + 3 * k])
                 )
 
         in_three_turns(
-            FACE // 2, lambda i: i, FACE, face_products, face_tiles, face_sums, slot_a, slot_b
+            [FACE // 2], [WIDTH], lambda i: i, FACE, face_products, face_tiles, face_sums,
+            slot_a, slot_b,
         )
 
     add_forces(total, own, term, out, carried)
@@ -779,22 +808,22 @@
     total[...] = jnp.zeros_like(total)
     clear([held[k] for held in (slot_a, slot_b) for k in (3, 4, 6, 7)])
 
-    def peer_step(e, _):
-        planes = listed_planes(listed, e, range(ROWS), ROWS)
-        put(theirs, pair_terms(*planes)[1], e * SLOTS * CELL, SLOTS, CELL)
-        *speed, pressed = listed_planes(arrived, e, range(MOVING), MOVING)
+    def make(e, part):
+        planes = listed_planes(listed, e, part, range(ROWS), ROWS)
+        at = e * SLOTS + 8 * part
+        put(theirs, pair_terms(*planes)[1], at * CELL, 8, CELL)
+        *speed, pressed = listed_planes(arrived, e, part, range(MOVING), MOVING)
         terms = force_terms(planes[0:3], planes[4], speed, pressed)
-        blank = jnp.zeros((SLOTS, WIDTH), F32)
-        put(their_rows, terms + [blank] * 4, e * SLOTS * SUMS, SLOTS, SUMS)
-        return 0
-
-    lax.fori_loop(0, PEERS, peer_step, 0)
-
-    def products(count, pairs, held):
+        blank = jnp.zeros((8, WIDTH), F32)
+        put(their_rows, terms + [blank] * 4, at * SUMS, 8, SUMS)
+
+    live_parts(fill, make, None)
+
+    def products(pairs, held):
         for k, (slot, c) in enumerate(pairs):
             held[k][...] = support_columns(line(own, c, CELL, 3))
             left = first_operand(block(first, c, CELL))
-            distances(left, block(theirs, slot, CELL), count, held[2 + 3 * k])
+            distances(left, block(theirs, slot, CELL), held[2 + 3 * k])
 
     def tiles(count, pairs, held):
         for k, (slot, c) in enumerate(pairs):
@@ -810,26 +839,26 @@
                 added = jnp.concatenate([added, jnp.zeros((SUMS, WIDTH - count), F32)], 1)
             add_block(total, c, SUMS, added)
 
-    for kind, count in enumerate(CROSS_ROWS):
-        trips, item = pair_list(plan, kind)
-        in_three_turns(
-            trips, item, None, functools.partial(products, count),
-            functools.partial(tiles, count), functools.partial(sums, count), slot_a, slot_b,
-        )
-
-    def back_step(e, _):
-        planes = listed_planes(listed, e, range(3), ROWS)
-        *speed, pressed = listed_planes(arrived, e, range(MOVING), MOVING)
-        summed = planes_of(sums_of, range(12), e * SLOTS * SUMS, SLOTS, SUMS)
-        live = live_rows(fill, e)
-        for k, force in enumerate(forces_of(summed, planes, speed, pressed)):
-            force = jnp.where(live, force, 0.0)
+    trips, item = pair_list(plan)
+    in_three_turns(trips, SIZES, item, None, products, tiles, sums, slot_a, slot_b)
+
+    def send(e, part):
+        planes = listed_planes(listed, e, part, range(3), ROWS)
+        *speed, pressed = listed_planes(arrived, e, part, range(MOVING), MOVING)
+        summed = planes_of(sums_of, range(12), (e * SLOTS + 8 * part) * SUMS, 8, SUMS)
+        live = live_rows(fill, e, part)
+        send_rows(e, part, [jnp.where(live, f, 0.0) for f in forces_of(summed, planes, speed, pressed)])
+
+    def send_none(e, part):
+        send_rows(e, part, [jnp.zeros((8, WIDTH), F32)] * MOVING)
+
+    def send_rows(e, part, forces):
+        for k, force in enumerate(forces):
             for h in range(2):
-                at = pl.ds(h * SLOTS * MOVING + k, SLOTS, stride=MOVING)
-                back[e, at, :] = half(force, h)
-        return 0
-
-    lax.fori_loop(0, PEERS, back_step, 0)
+                start = (h * SLOTS + 8 * part) * MOVING + k
+                back[e, pl.ds(start, 8, stride=MOVING), :] = half(force, h)
+
+    live_parts(fill, send, send_none)
     add_forces(total, own, term, out, carried)
 
 

time: 153 us -> 149 us (0.974)
  Pallas kernels: 107 us -> 96.3 us
  starting transfers between devices: 38.5 us -> 45.5 us
    all_to_all x4, starting transfers between devices: 32.6 us -> 39.5 us  [to_peers(): return lax.all_to_all(block, 'dev', split_axis=0, concat_axis=0, tiled=True)]
    pallas_call x2, Pallas kernels: 33.9 us -> 30 us  [local_force(): pl.pallas_call(functools.partial(local_force_kernel, part), in_specs=[SM]...]
    pallas_call x1, Pallas kernels: 19.4 us -> 15.5 us  [cross_force(): pl.pallas_call(cross_force_kernel, in_specs=[SM, SM] + [VM] * 6, out_spec...]
    pallas_call x2, Pallas kernels: 26.9 us -> 24.3 us  [local_density(): pl.pallas_call(functools.partial(local_density_kernel, part), in_specs=[S...]
    pallas_call x1, Pallas kernels: 13.6 us -> 11.5 us  [cross_density(): pl.pallas_call(cross_density_kernel, in_specs=[SM, SM] + [VM] * 4, out_sp...]
    pallas_call x1, Pallas kernels: 3.61 us -> 5.25 us  [make_plan(): pl.pallas_call(plan_kernel, in_specs=[SM] * 3 + [ANYWHERE], out_specs=SM,...]
  transfers between devices with their start and end apart: 8 -> 8, of which waited for: 1 -> 1; matrix products, arithmetic and copies ran while one was open for 1% -> 1% of each run, Pallas kernels for 51% -> 48%
where the time goes in v4:
time: 149 us; the launch traced here: 148 us
  Pallas kernels  96.3 us (65%)
  starting transfers between devices  45.5 us (31%)
  local copies, waits for them, and re-layouts  3.51 us (2%)
    all_to_all x4, starting transfers between devices, to_peers(): return lax.all_to_all(block, 'dev', split_axis=0, concat_axis=0, tiled=True)  39.5 us
    pallas_call x2, Pallas kernels, local_force(): pl.pallas_call(functools.partial(local_force_kernel, part), in_specs=[SM]...  30 us
    pallas_call x2, Pallas kernels, local_density(): pl.pallas_call(functools.partial(local_density_kernel, part), in_specs=[S...  24.3 us
    pallas_call x1, Pallas kernels, cross_force(): pl.pallas_call(cross_force_kernel, in_specs=[SM, SM] + [VM] * 6, out_spec...  15.5 us
    pallas_call x1, Pallas kernels, cross_density(): pl.pallas_call(cross_density_kernel, in_specs=[SM, SM] + [VM] * 4, out_sp...  11.5 us
    ppermute x2, starting transfers between devices, with_neighbours(): lax.ppermute(rows[..., :FACE * size, :], 'region', down)  5.89 us
    pallas_call x1, Pallas kernels, make_plan(): pl.pallas_call(plan_kernel, in_specs=[SM] * 3 + [ANYWHERE], out_specs=SM,...  5.25 us
    pallas_call x1, Pallas kernels, prepare(): pl.pallas_call(prepare_kernel, in_specs=[SM] * 2 + [ANYWHERE] * 4, out_sp...  4.27 us
  transfers between devices with their start and end apart: 8, of which 1 were waited for; matrix products, arithmetic and copies ran while one was open for 1% of the time, Pallas kernels for 48%

profile of v4, /device:TPU:0, one launch (start us, length us, event | category | flops | bytes accessed | tf_op | source)
XLA Modules:
  0.0 147.7 jit_solution(6325902337096446721)
XLA Ops:
  0.6 4.3 %shard_map.113 = (f32[2,520,128]{2,1,0:T(8,128)}, f32[2,520,128]{2,1,0:T(8,128)}, f32[2,520,128]{2,1,0:T(8,128)}, f32[16,160,128]{2,1,0:T(8,128)}) custom-call(s32[64]{0:T(128)} %occ.3, s32[16,16]{1,0:T(8,128)} %bitcast.2, f32[3,64,256]{2,1,0:T(8,128)} %pos_in.1, f32[3,64,256]{2,1,0:T(8,128)} %vel_in.1, f32[64,256]{1,0:T(8,128)} %smooth_in.1, f32[64,256]{1,0:T(8,128)} %mass_in.1), custom_call_target="tpu_custom_call" | custom-call | tf_op jit(solution)/shard_map/pallas_call | solution.py:319
  4.9 8.1 %all-to-all-start = ((f32[16,160,128]{2,1,0:T(8,128)}), f32[16,160,128]{2,1,0:T(8,128)S(1)}, u32[]{:S(2)}, u32[]{:S(2)}) async-start(f32[16,160,128]{2,1,0:T(8,128)} %get-tuple-element.16), calls=%async_computation | async-start | bytes 2621440 | tf_op jit(solution)/shard_map/all_to_all | solution.py:935
  13.1 0.0 copy-start.11
  13.1 0.8 fusion
  13.9 3.0 %collective-permute-start.1 = (f32[2,32,128]{2,1,0:T(8,128)S(1)}, f32[2,32,128]{2,1,0:T(8,128)S(1)}, u32[]{:S(2)}, u32[]{:S(2)}) collective-permute-start(f32[2,32,128]{2,1,0:T(8,128)S(1)} %get-tuple-element.24), channel_id=1, source_target_pairs={{0,112},{16,0},{32,16},{48,32},{64,48},{80,64},{96,80},{112,96},{1... | collective-permute-start | bytes 98312 | tf_op jit(solution)/shard_map/ppermute | solution.py:945
  16.8 5.2 %shard_map.114.plan = s32[432]{0:T(512)} custom-call(s32[64]{0:T(128)} %occ.3, s32[1,16]{1,0:T(1,128)} %fill.5, s32[16,16]{1,0:T(8,128)} %bitcast.5, f32[2,520,128]{2,1,0:T(8,128)} %get-tuple-element.13._.own), custom_call_target="tpu_custom_call" | custom-call | tf_op jit(solution)/shard_map/pallas_call | solution.py:254
  22.1 0.7 copy-done.6
  22.8 13.6 %shard_map.115.carried = f32[64,256]{1,0:T(8,128)S(1)} custom-call(s32[432]{0:T(512)S(1)} %copy-done.6, f32[2,520,128]{2,1,0:T(8,128)S(1)} %copy-done, f32[2,520,128]{2,1,0:T(8,128)S(1)} %copy-done.1, f32[2,520,128]{2,1,0:T(8,128)S(1)} %copy-done.3), custom_call_target="tpu_custom_call" | custom-call | flops 251658240 | bytes 2097152 | tf_op jit(solution)/shard_map/pallas_call | solution.py:462
  36.5 11.5 %shard_map.116 = (f32[64,256]{1,0:T(8,128)S(1)}, f32[16,16,256]{2,1,0:T(8,128)}) custom-call(s32[1,16]{1,0:T(1,128)S(1)} %copy-done.11, s32[432]{0:T(512)S(1)} %copy-done.7, f32[2,520,128]{2,1,0:T(8,128)S(1)} %copy-done, f32[2,520,128]{2,1,0:T(8,128)S(1)} %copy-done.1, f32[16,160,128]{2,1,0:T(8,128)S(1)} %all-to-all-done.listed, ...), custom_call_target="tpu_custom_call" | custom-call | flops 314572800 | bytes 2097152 | tf_op jit(solution)/shard_map/pallas_call | solution.py:528
  48.0 12.1 %all-to-all-start.1 = ((f32[16,16,256]{2,1,0:T(8,128)}), f32[16,16,256]{2,1,0:T(8,128)S(1)}, u32[]{:S(2)}, u32[]{:S(2)}) async-start(f32[16,16,256]{2,1,0:T(8,128)} %get-tuple-element.18), calls=%async_computation.1 | async-start | bytes 524288 | tf_op jit(solution)/shard_map/all_to_all | solution.py:935
  60.1 10.6 %shard_map.117.near = f32[64,256]{1,0:T(8,128)S(1)} custom-call(s32[432]{0:T(512)S(1)} %copy-done.7, f32[2,520,128]{2,1,0:T(8,128)S(1)} %copy-done, f32[2,520,128]{2,1,0:T(8,128)S(1)} %copy-done.1, f32[2,520,128]{2,1,0:T(8,128)S(1)} %copy-done.3, f32[2,64,128]{2,1,0:T(8,128)S(1)} %constant_dynamic-update-slice_fusion.rest_0_, ...), custom_call_target="tpu_custom_call" | custom-call | flops 251658240 | bytes 2097152 | tf_op jit(solution)/shard_map/pallas_call | solution.py:462
  70.8 3.0 %shard_map.118 = (f32[64,256]{1,0:T(8,128)}, f32[64,256]{1,0:T(8,128)S(1)}, f32[16,128,128]{2,1,0:T(8,128)S(1)}) custom-call(s32[16,16]{1,0:T(8,128)S(1)} %bitcast.3, f32[64,256]{1,0:T(8,128)S(1)} %shard_map.117.near, f32[16,16,256]{2,1,0:T(8,128)S(1)} %all-to-all-done.1.returned, f32[64,256]{1,0:T(8,128)S(1)} %copy-done.9, f32[2,520,128]{2,1,0:T(8,128)S(1)} %copy-done), custom_call_target="tpu_custom_call" | custom-call | tf_op jit(solution)/shard_map/pallas_call | solution.py:588
  73.8 1.0 copy-done.5
  74.7 7.3 %all-to-all-start.2 = ((f32[16,128,128]{2,1,0:T(8,128)}), f32[16,128,128]{2,1,0:T(8,128)S(1)}, u32[]{:S(2)}, u32[]{:S(2)}) async-start(f32[16,128,128]{2,1,0:T(8,128)} %copy-done.5), calls=%async_computation.2 | async-start | bytes 2097152 | tf_op jit(solution)/shard_map/all_to_all | solution.py:935
  82.0 16.9 %shard_map.119.carried = f32[4,64,256]{2,1,0:T(8,128)S(1)} custom-call(s32[432]{0:T(512)S(1)} %copy-done.7, f32[2,520,128]{2,1,0:T(8,128)S(1)} %copy-done, f32[2,520,128]{2,1,0:T(8,128)S(1)} %copy-done.1, f32[2,520,128]{2,1,0:T(8,128)S(1)} %copy-done.3, f32[64,256]{1,0:T(8,128)S(1)} %get-tuple-element.20.term), custom_call_target="tpu_custom_call" | custom-call | flops 335544320 | bytes 2097152 | tf_op jit(solution)/shard_map/pallas_call | solution.py:789
  99.0 15.5 %shard_map.120 = (f32[4,64,256]{2,1,0:T(8,128)S(1)}, f32[16,128,128]{2,1,0:T(8,128)S(1)}) custom-call(s32[1,16]{1,0:T(1,128)S(1)} %copy-done.11, s32[432]{0:T(512)S(1)} %copy-done.7, f32[2,520,128]{2,1,0:T(8,128)S(1)} %copy-done, f32[2,520,128]{2,1,0:T(8,128)S(1)} %copy-done.1, f32[64,256]{1,0:T(8,128)S(1)} %get-tuple-element.20.term, ...), custom_call_target="tpu_custom_call" | custom-call | flops 419430400 | bytes 2097152 | tf_op jit(solution)/shard_map/pallas_call | solution.py:866
  114.5 1.0 copy-done.4
  115.5 12.1 %all-to-all-start.3 = ((f32[16,128,128]{2,1,0:T(8,128)}), f32[16,128,128]{2,1,0:T(8,128)S(1)}, u32[]{:S(2)}, u32[]{:S(2)}) async-start(f32[16,128,128]{2,1,0:T(8,128)} %copy-done.4), calls=%async_computation.3 | async-start | bytes 2097152 | tf_op jit(solution)/shard_map/all_to_all | solution.py:935
  127.6 0.0 collective-permute-start.2
  127.6 2.9 %collective-permute-start.3 = (f32[4,256]{1,0:T(4,128)S(1)}, f32[4,256]{1,0:T(4,128)S(1)}, u32[]{:S(2)}, u32[]{:S(2)}) collective-permute-start(f32[4,256]{1,0:T(4,128)S(1)} %get-tuple-element.27), channel_id=1, source_target_pairs={{0,112},{16,0},{32,16},{48,32},{64,48},{80,64},{96,80},{112,96},{1... | collective-permute-start | bytes 12296 | tf_op jit(solution)/shard_map/ppermute | solution.py:945
  130.6 1.3 collective-permute-done.2
  131.9 0.0 collective-permute-done.3
  131.9 13.1 %shard_map.121.near = f32[4,64,256]{2,1,0:T(8,128)S(1)} custom-call(s32[432]{0:T(512)S(1)} %copy-done.7, f32[2,520,128]{2,1,0:T(8,128)S(1)} %copy-done, f32[2,520,128]{2,1,0:T(8,128)S(1)} %copy-done.1, f32[2,520,128]{2,1,0:T(8,128)S(1)} %copy-done.3, f32[64,256]{1,0:T(8,128)S(1)} %get-tuple-element.20.term, ...), custom_call_target="tpu_custom_call" | custom-call | flops 335544320 | bytes 2097152 | tf_op jit(solution)/shard_map/pallas_call | solution.py:789
  145.0 2.5 %shard_map.122 = f32[4,64,256]{2,1,0:T(8,128)} custom-call(s32[16,16]{1,0:T(8,128)S(1)} %bitcast.4, f32[4,64,256]{2,1,0:T(8,128)S(1)} %shard_map.121.near, f32[16,128,128]{2,1,0:T(8,128)S(1)} %all-to-all-done.3.returned, s32[64,256]{1,0:T(8,128)S(1)} %copy-done.10, f32[2,520,128]{2,1,0:T(8,128)S(1)} %copy-done), custom_call_target="tpu_custom_call" | custom-call | tf_op jit(solution)/shard_map/pallas_call | solution.py:919
  (31 shorter events, 0.1 us)
Async XLA Ops:
  4.9 17.2 %copy-start = (f32[2,520,128]{2,1,0:T(8,128)S(1)}, f32[2,520,128]{2,1,0:T(8,128)}, u32[]{:S(2)}) copy-start(f32[2,520,128]{2,1,0:T(8,128)} %get-tuple-element.13._.own) | copy-start | bytes 1597444
  4.9 17.2 %copy-start.1 = (f32[2,520,128]{2,1,0:T(8,128)S(1)}, f32[2,520,128]{2,1,0:T(8,128)}, u32[]{:S(2)}) copy-start(f32[2,520,128]{2,1,0:T(8,128)} %get-tuple-element.14.first) | copy-start | bytes 1597444
  4.9 17.2 %copy-start.3 = (f32[2,520,128]{2,1,0:T(8,128)S(1)}, f32[2,520,128]{2,1,0:T(8,128)}, u32[]{:S(2)}) copy-start(f32[2,520,128]{2,1,0:T(8,128)} %get-tuple-element.15.second) | copy-start | bytes 1597444
  4.9 31.5 %all-to-all-start = ((f32[16,160,128]{2,1,0:T(8,128)}), f32[16,160,128]{2,1,0:T(8,128)S(1)}, u32[]{:S(2)}, u32[]{:S(2)}) async-start(f32[16,160,128]{2,1,0:T(8,128)} %get-tuple-element.16), calls=%async_computation | async-start | bytes 2621440 | tf_op jit(solution)/shard_map/all_to_all | solution.py:935
  13.1 23.4 %copy-start.11 = (s32[1,16]{1,0:T(1,128)S(1)}, s32[1,16]{1,0:T(1,128)}, u32[]{:S(2)}) copy-start(s32[1,16]{1,0:T(1,128)} %fill.5) | copy-start | bytes 196
  13.8 46.2 %collective-permute-start = (f32[2,32,128]{2,1,0:T(8,128)S(1)}, f32[2,32,128]{2,1,0:T(8,128)S(1)}, u32[]{:S(2)}, u32[]{:S(2)}) collective-permute-start(f32[2,32,128]{2,1,0:T(8,128)S(1)} %get-tuple-element.25), channel_id=1, source_target_pairs={{0,16},{16,32},{32,48},{48,64},{64,80},{80,96},{96,112},{112,0},{1... | collective-permute-start | bytes 98312 | tf_op jit(solution)/shard_map/ppermute | solution.py:944
  13.9 46.2 %collective-permute-start.1 = (f32[2,32,128]{2,1,0:T(8,128)S(1)}, f32[2,32,128]{2,1,0:T(8,128)S(1)}, u32[]{:S(2)}, u32[]{:S(2)}) collective-permute-start(f32[2,32,128]{2,1,0:T(8,128)S(1)} %get-tuple-element.24), channel_id=1, source_target_pairs={{0,112},{16,0},{32,16},{48,32},{64,48},{80,64},{96,80},{112,96},{1... | collective-permute-start | bytes 98312 | tf_op jit(solution)/shard_map/ppermute | solution.py:945
  22.1 14.4 %copy-start.7 = (s32[432]{0:T(512)S(1)}, s32[432]{0:T(512)}, u32[]{:S(2)}) copy-start(s32[432]{0:T(512)} %shard_map.114.plan) | copy-start | bytes 5188
  22.1 0.7 copy-start.6
  36.5 11.5 %copy-start.2 = (f32[16,160,128]{2,1,0:T(8,128)}, f32[16,160,128]{2,1,0:T(8,128)S(1)}, u32[]{:S(2)}) copy-start(f32[16,160,128]{2,1,0:T(8,128)S(1)} %all-to-all-done.listed) | copy-start | bytes 3932164
  48.0 22.8 %copy-start.8 = (s32[1,16,16]{2,1,0:T(8,128)S(1)}, s32[1,16,16]{2,1,0:T(8,128)}, u32[]{:S(2)}) copy-start(s32[1,16,16]{2,1,0:T(8,128)} %param.19) | copy-start | bytes 3076
  48.0 22.8 %copy-start.9 = (f32[64,256]{1,0:T(8,128)S(1)}, f32[64,256]{1,0:T(8,128)}, u32[]{:S(2)}) copy-start(f32[64,256]{1,0:T(8,128)} %energy_in.1) | copy-start | bytes 196612
  48.0 22.8 %all-to-all-start.1 = ((f32[16,16,256]{2,1,0:T(8,128)}), f32[16,16,256]{2,1,0:T(8,128)S(1)}, u32[]{:S(2)}, u32[]{:S(2)}) async-start(f32[16,16,256]{2,1,0:T(8,128)} %get-tuple-element.18), calls=%async_computation.1 | async-start | bytes 524288 | tf_op jit(solution)/shard_map/all_to_all | solution.py:935
  73.8 1.0 copy-start.5
  74.7 24.2 %all-to-all-start.2 = ((f32[16,128,128]{2,1,0:T(8,128)}), f32[16,128,128]{2,1,0:T(8,128)S(1)}, u32[]{:S(2)}, u32[]{:S(2)}) async-start(f32[16,128,128]{2,1,0:T(8,128)} %copy-done.5), calls=%async_computation.2 | async-start | bytes 2097152 | tf_op jit(solution)/shard_map/all_to_all | solution.py:935
  114.5 1.0 copy-start.4
  115.5 29.5 %all-to-all-start.3 = ((f32[16,128,128]{2,1,0:T(8,128)}), f32[16,128,128]{2,1,0:T(8,128)S(1)}, u32[]{:S(2)}, u32[]{:S(2)}) async-start(f32[16,128,128]{2,1,0:T(8,128)} %copy-done.4), calls=%async_computation.3 | async-start | bytes 2097152 | tf_op jit(solution)/shard_map/all_to_all | solution.py:935
  127.6 17.5 %copy-start.10 = (s32[64,256]{1,0:T(8,128)S(1)}, s32[64,256]{1,0:T(8,128)}, u32[]{:S(2)}) copy-start(s32[64,256]{1,0:T(8,128)} %active_in.1) | copy-start | bytes 196612
  127.6 4.3 %collective-permute-start.2 = (f32[4,256]{1,0:T(4,128)S(1)}, f32[4,256]{1,0:T(4,128)S(1)}, u32[]{:S(2)}, u32[]{:S(2)}) collective-permute-start(f32[4,256]{1,0:T(4,128)S(1)} %get-tuple-element.26), channel_id=1, source_target_pairs={{0,16},{16,32},{32,48},{48,64},{64,80},{80,96},{96,112},{112,0},{1... | collective-permute-start | bytes 12296 | tf_op jit(solution)/shard_map/ppermute | solution.py:944
  127.6 4.3 %collective-permute-start.3 = (f32[4,256]{1,0:T(4,128)S(1)}, f32[4,256]{1,0:T(4,128)S(1)}, u32[]{:S(2)}, u32[]{:S(2)}) collective-permute-start(f32[4,256]{1,0:T(4,128)S(1)} %get-tuple-element.27), channel_id=1, source_target_pairs={{0,112},{16,0},{32,16},{48,32},{64,48},{80,64},{96,80},{112,96},{1... | collective-permute-start | bytes 12296 | tf_op jit(solution)/shard_map/ppermute | solution.py:945

commit v5 on v4

--- a/solution.py
+++ b/solution.py
@@ -43,10 +43,11 @@
 PLAN = CROSS_AT + CROSS_LIST
 PACK = 128
 ANYWHERE = pl.BlockSpec(memory_space=pl.ANY)
-
-
-def params():
-    return pltpu.CompilerParams(vmem_limit_bytes=50 * 2**20)
+OWN_ROWS = jax.ShapeDtypeStruct((2, (CELLS + 1) * CELL, 128), F32)
+
+
+def params(mib=50):
+    return pltpu.CompilerParams(vmem_limit_bytes=int(mib * 2**20))
 
 
 def split2(x):
@@ -148,19 +149,24 @@
     mix_ref[...] = jnp.dot(left, operands[1], preferred_element_type=F32)
 
 
+def weights_of(s, mix, columns, row):
+    s = jnp.maximum(s, TINY)
+    dist = s * lax.rsqrt(s)
+    support = columns + row
+    d = jnp.maximum(support - dist, 0.0)
+    x = pl.reciprocal(mix, approx=True) * d
+    x = x * x
+    x = x * x
+    return x * (support + 4.0 * dist)
+
+
 def density_weights(count, s_ref, mix_ref, columns, row, one_sided):
     second = jnp.zeros((8, WIDTH), F32)
     firsts = []
     for start in range(0, count, CHUNK):
-        s = jnp.maximum(s_ref[start : start + CHUNK], TINY)
-        dist = s * lax.rsqrt(s)
-        wide = columns[start : start + CHUNK]
-        support = jnp.concatenate([wide, wide], 1) + row
-        d = jnp.maximum(support - dist, 0.0)
-        x = pl.reciprocal(mix_ref[start : start + CHUNK], approx=True) * d
-        x = x * x
-        x = x * x
-        w = x * (support + 4.0 * dist)
+        part = slice(start, start + CHUNK)
+        wide = columns[part]
+        w = weights_of(s_ref[part], mix_ref[part], jnp.concatenate([wide, wide], 1), row)
         for k in range(CHUNK // 8):
             second = second + w[8 * k : 8 * k + 8]
         if not one_sided:
@@ -180,84 +186,22 @@
     return jnp.where(m > 0.0, W_SCALE / jnp.where(m > 0.0, m, 1.0), 0.0)
 
 
-def kind_of(size):
-    return sum((size > rows).astype(jnp.int32) for rows in SIZES[:-1])
-
-
-def plan_kernel(occ, fill, cells, _, plan, next_at):
-    for k in range(3 * KINDS):
-        next_at[k] = 0
-
-    def local_count(c, _):
-        kind = kind_of(occ[c]) + jnp.where(c >= SPLIT, KINDS, 0)
-        next_at[kind] = next_at[kind] + 1
-        return 0
-
-    lax.fori_loop(0, CELLS, local_count, 0)
-
-    def over_pairs(visit):
-        def peer_step(e, _):
-            def slot_step(s, _):
-                cell = cells[e, s]
-                visit(2 * KINDS + kind_of(occ[cell]), (e * SLOTS + s) * PACK + cell)
-                return 0
-
-            return lax.fori_loop(0, fill[0, e], slot_step, 0)
-
-        lax.fori_loop(0, PEERS, peer_step, 0)
-
-    def pair_count(kind, _):
-        next_at[kind] = next_at[kind] + 1
-
-    over_pairs(pair_count)
-
-    unused = jnp.int32(0)
-    for e in range(PEERS):
-        unused = jnp.where(fill[0, e] == 0, e * SLOTS, unused)
-
-    for group, (start, lead, unit, blank) in enumerate(
-        [
-            (LOCAL_AT, LOCAL_LEAD, 2, CELLS),
-            (LOCAL_AT + LOCAL_LIST, LOCAL_LEAD, 2, CELLS),
-            (CROSS_AT, CROSS_LEAD, UNIT, unused * PACK + CELLS),
-        ]
-    ):
-        total = jnp.int32(0)
-        done = jnp.int32(0)
-        for k in range(KINDS):
-            at = group * KINDS + k
-            count = next_at[at]
-            next_at[at] = start + lead + total
-            total = total + count
-            upto = (total + (unit - 1 if k == KINDS - 1 else 0)) // unit
-            plan[at] = upto - done
-            done = upto
-        for k in range(lead):
-            plan[start + k] = blank
-        for k in range(unit + 1):
-            plan[start + lead + total + k] = blank
-
-    def place(kind, value):
-        at = next_at[kind]
-        plan[at] = value
-        next_at[kind] = at + 1
-
-    def local_place(c, _):
-        place(kind_of(occ[c]) + jnp.where(c >= SPLIT, KINDS, 0), c)
-        return 0
-
-    lax.fori_loop(0, CELLS, local_place, 0)
-    over_pairs(place)
-
-
-def make_plan(occ, fill, cells, own):
-    return pl.pallas_call(
-        plan_kernel,
-        in_specs=[SM] * 3 + [ANYWHERE],
-        out_specs=SM,
-        out_shape=jax.ShapeDtypeStruct((PLAN,), jnp.int32),
-        scratch_shapes=[pltpu.SMEM((3 * KINDS,), jnp.int32)],
-    )(occ, fill, cells, own)
+def self_weights(count, s_ref, mix_ref, columns, row):
+    sums = [jnp.zeros((8, 128), F32)] * 2
+    crossing = []
+    for start in range(0, count, CHUNK):
+        part = slice(start, start + CHUNK)
+        for h in range(0 if start < 128 else 1, 2):
+            lanes = slice(128 * h, 128 * (h + 1))
+            w = weights_of(s_ref[part, lanes], mix_ref[part, lanes], columns[part], half(row, h))
+            for k in range(CHUNK // 8):
+                sums[h] = sums[h] + w[8 * k : 8 * k + 8]
+            if h and start < 128:
+                crossing.append(w)
+    turned = jnp.concatenate(crossing, 0).T
+    for k in range(16):
+        sums[0] = sums[0] + turned[8 * k : 8 * k + 8]
+    return jnp.concatenate(sums, 1)
 
 
 def fetch(pairs, sem):
@@ -271,8 +215,7 @@
 
 
 def prepare_kernel(
-    occ, pair, pos_in, vel_in, smooth_in, mass_in, own, first, second, out,
-    pos, vel, smooth, mass, full, cells, sem,
+    occ, pair, pos_in, vel_in, smooth_in, mass_in, own, out, pos, vel, smooth, mass, full, sem
 ):
     copies = fetch(
         [(pos_in, pos), (vel_in, vel), (smooth_in, smooth), (mass_in, mass)], sem
@@ -284,54 +227,98 @@
         copy.wait()
     place = [pos[k] - 0.5 for k in range(3)]
     m = jnp.where(full[...] > 0.0, mass[...], 0.0)
-    h = smooth[...]
-    put(own, place + [h, m] + [vel[k] for k in range(3)], 0, CELLS, CELL)
+    put(own, place + [smooth[...], m] + [vel[k] for k in range(3)], 0, CELLS, CELL)
     blank = jnp.zeros((CELL, WIDTH), F32)
     wide = jnp.full((1, WIDTH), 0.5, F32)
     set_block(own, CELLS, CELL, jnp.concatenate([blank[:3], wide, blank[:4]], 0))
-    before, after = pair_terms(*place, h, m)
-    put(first, before, 0, CELLS, CELL)
-    put(second, after, 0, CELLS, CELL)
-    before, after = pair_terms(*[blank[:1]] * 3, wide, blank[:1])
-    set_block(first, CELLS, CELL, jnp.concatenate(before, 0))
-    set_block(second, CELLS, CELL, jnp.concatenate(after, 0))
-
-    def cell_step(c, _):
-        cells[c] = block(own, c, CELL)
-        return 0
-
-    lax.fori_loop(0, CELLS, cell_step, 0, unroll=8)
 
     def peer_step(e, _):
         for s in range(SLOTS):
-            cell = cells[pair[e, s], 0:ROWS]
+            c = pair[e, s]
             for h in range(2):
                 at = (h * SLOTS + s) * ROWS
-                out[e, at : at + ROWS] = half(cell, h)
+                out[e, at : at + ROWS] = own[h, rows_at(c, CELL), :][:ROWS]
         return 0
 
     lax.fori_loop(0, PEERS, peer_step, 0)
 
 
 def prepare(occ, pair, pos, vel, smooth, mass):
-    rows = jax.ShapeDtypeStruct((2, (CELLS + 1) * CELL, 128), F32)
     plane = pltpu.VMEM((CELLS, WIDTH), F32)
     return pl.pallas_call(
         prepare_kernel,
         in_specs=[SM] * 2 + [ANYWHERE] * 4,
-        out_specs=[VM] * 4,
-        out_shape=[rows] * 3 + [jax.ShapeDtypeStruct((PEERS, 2 * SLOTS * ROWS, 128), F32)],
+        out_specs=[VM] * 2,
+        out_shape=[
+            OWN_ROWS,
+            jax.ShapeDtypeStruct((PEERS, 2 * SLOTS * ROWS, 128), F32),
+        ],
         scratch_shapes=[
             pltpu.VMEM((3, CELLS, WIDTH), F32),
             pltpu.VMEM((3, CELLS, WIDTH), F32),
             plane,
             plane,
             plane,
-            pltpu.VMEM((CELLS, CELL, WIDTH), F32),
             pltpu.SemaphoreType.DMA((4,)),
         ],
-        compiler_params=pltpu.CompilerParams(vmem_limit_bytes=60 * 2**20),
+        compiler_params=params(60),
     )(occ, pair, pos, vel, smooth, mass)
+
+
+def kind_of(size):
+    return jnp.maximum(size - SIZES[0] + 31, 0) >> 5
+
+
+def make_plan(occ, fill, cells, plan):
+    def over_local(visit, part, carry):
+        low, high = (SPLIT, CELLS) if part else (0, SPLIT)
+        step = lambda c, carry: visit(kind_of(occ[c]), c, carry)
+        return lax.fori_loop(low, high, step, carry, unroll=8)
+
+    def over_pairs(visit, carry):
+        def peer_step(e, carry):
+            def slot_step(s, carry):
+                cell = cells[e, s]
+                return visit(kind_of(occ[cell]), (e * SLOTS + s) * PACK + cell, carry)
+
+            return lax.fori_loop(0, fill[0, e], slot_step, carry)
+
+        return lax.fori_loop(0, PEERS, peer_step, carry)
+
+    unused = jnp.int32(0)
+    for e in range(PEERS):
+        unused = jnp.where(fill[0, e] == 0, e * SLOTS, unused)
+
+    def one_of(kind):
+        return jnp.left_shift(jnp.int32(1), 8 * kind)
+
+    for group, (walk, start, lead, unit, blank) in enumerate(
+        [
+            (lambda v, x: over_local(v, 0, x), LOCAL_AT, LOCAL_LEAD, 2, CELLS),
+            (lambda v, x: over_local(v, 1, x), LOCAL_AT + LOCAL_LIST, LOCAL_LEAD, 2, CELLS),
+            (over_pairs, CROSS_AT, CROSS_LEAD, UNIT, unused * PACK + CELLS),
+        ]
+    ):
+        counts = walk(lambda kind, value, packed: packed + one_of(kind), jnp.int32(0))
+        total = jnp.int32(0)
+        done = jnp.int32(0)
+        places = jnp.int32(0)
+        for k in range(KINDS):
+            places = places + jnp.left_shift(total, 8 * k)
+            total = total + ((counts >> (8 * k)) & 255)
+            upto = (total + (unit - 1 if k == KINDS - 1 else 0)) // unit
+            plan[group * KINDS + k] = upto - done
+            done = upto
+        for k in range(lead):
+            plan[start + k] = blank
+        for k in range(unit + 1):
+            plan[start + lead + total + k] = blank
+
+        def place(kind, value, packed, start=start + lead):
+            plan[start + ((packed >> (8 * kind)) & 255)] = value
+            return packed + one_of(kind)
+
+        walk(place, places)
 
 
 def fold(total, own, out, carried):
@@ -402,12 +389,20 @@
     lax.fori_loop(0, 2 * PEERS, step, 0)
 
 
-def local_density_kernel(part, plan, own, first, second, *rest):
+def local_density_kernel(part, *refs):
     if part:
-        faces, carried, rho, total, face_first, *slots = rest
+        plan, own, first, second, faces, carried, rho, total, face_first, *slots = refs
     else:
         carried = None
-        rho, total, *slots = rest
+        occ, fill, cells, own, rho, first, second, plan, total, *slots = refs
+        make_plan(occ, fill, cells, plan)
+        planes = planes_of(own, range(ROWS), 0, CELLS, CELL)
+        blank = [jnp.zeros((1, WIDTH), F32)] * 3 + [jnp.full((1, WIDTH), 0.5, F32)]
+        for ref, some, none in zip(
+            (first, second), pair_terms(*planes), pair_terms(*blank, blank[0])
+        ):
+            put(ref, some, 0, CELLS, CELL)
+            set_block(ref, CELLS, CELL, jnp.concatenate(none, 0))
     slot_a, slot_b = slots[:6], slots[6:]
     total[...] = jnp.zeros_like(total)
 
@@ -421,7 +416,7 @@
     def weights(count, c, held):
         after = jnp.minimum(c + 1, CELLS)
         row, other = line(own, c, CELL, 3), line(own, after, CELL, 3)
-        own_sum = density_weights(count, *held[0:2], held[4], row, True)
+        own_sum = self_weights(count, *held[0:2], held[4], row)
         there, here = density_weights(count, *held[2:4], held[4], other, False)
         add_block(total, c, CELL, own_sum + here)
         add_block(total, after, CELL, there)
@@ -458,12 +453,18 @@
 DENSITY_SLOT = [pltpu.VMEM((WIDTH, WIDTH), F32)] * 4 + [pltpu.VMEM((WIDTH, 128), F32)] * 2
 
 
-def local_density(part, plan, own, first, second, *rest):
+def local_density(part, *operands):
+    plane = jax.ShapeDtypeStruct((CELLS, WIDTH), F32)
+    if part:
+        in_specs, out_specs, out_shape = [SM] + [VM] * 5, VM, plane
+    else:
+        in_specs, out_specs = [SM] * 3 + [VM], [VM] * 3 + [SM]
+        out_shape = [plane, OWN_ROWS, OWN_ROWS, jax.ShapeDtypeStruct((PLAN,), jnp.int32)]
     return pl.pallas_call(
         functools.partial(local_density_kernel, part),
-        in_specs=[SM] + [VM] * (3 + len(rest)),
-        out_specs=VM,
-        out_shape=jax.ShapeDtypeStruct((CELLS, WIDTH), F32),
+        in_specs=in_specs,
+        out_specs=out_specs,
+        out_shape=out_shape,
         scratch_shapes=[pltpu.VMEM((2, (CELLS + 1) * CELL, 128), F32)]
         + [pltpu.VMEM((2, 2 * FACE * CELL, 128), F32)] * part
         + DENSITY_SLOT * 2,
@@ -471,7 +472,7 @@
             flops=64 * 65536 * 60, bytes_accessed=2 * 2**20, transcendentals=0
         ),
         compiler_params=params(),
-    )(plan, own, first, second, *rest)
+    )(*operands)
 
 
 def live_rows(fill, e, part):
@@ -800,7 +801,7 @@
 
 
 def cross_force_kernel(
-    fill, plan, own, first, term, listed, arrived, carried, out, back,
+    fill, plan, own, first, term, listed, arrived, carried, _, out, back,
     rows, total, theirs, their_rows, sums_of, *slots
 ):
     slot_a, slot_b = slots[:8], slots[8:]
@@ -862,10 +863,10 @@
     add_forces(total, own, term, out, carried)
 
 
-def cross_force(fill, plan, own, first, term, listed, arrived, carried):
+def cross_force(fill, plan, own, first, term, listed, arrived, carried, after):
     return pl.pallas_call(
         cross_force_kernel,
-        in_specs=[SM, SM] + [VM] * 6,
+        in_specs=[SM, SM] + [VM] * 6 + [ANYWHERE],
         out_specs=[VM, VM],
         out_shape=[
             jax.ShapeDtypeStruct((4, CELLS, WIDTH), F32),
@@ -883,7 +884,7 @@
             flops=80 * 65536 * 80, bytes_accessed=2 * 2**20, transcendentals=0
         ),
         compiler_params=params(),
-    )(fill, plan, own, first, term, listed, arrived, carried)
+    )(fill, plan, own, first, term, listed, arrived, carried, after)
 
 
 def finish_kernel(pair, near, returned, active_in, own, out, total, active, gate, sem):
@@ -953,13 +954,10 @@
     pair_cell,
 ):
     pair = pair_cell[0]
-    own, first, second, listed = prepare(
-        occupancy, pair, positions, velocity, smoothing, masses
-    )
+    own, listed = prepare(occupancy, pair, positions, velocity, smoothing, masses)
     arrived = to_peers(listed)
-    plan = make_plan(occupancy, send_fill, send_cells[0], own)
     faces = with_neighbours(own, CELL)
-    rho = local_density(0, plan, own, first, second)
+    rho, first, second, plan = local_density(0, occupancy, send_fill, send_cells[0], own)
     rho, back = cross_density(send_fill, plan, own, first, arrived, rho)
     returned = to_peers(back)
     rho = local_density(1, plan, own, first, second, faces, rho)
@@ -968,7 +966,7 @@
     face_terms = with_neighbours(term, 1)
     sums = local_force(0, plan, own, first, second, term)
     sums, force_back = cross_force(
-        send_fill, plan, own, first, term, arrived, arrived_moving, sums
+        send_fill, plan, own, first, term, arrived, arrived_moving, sums, face_terms
     )
     returned_force = to_peers(force_back)
     sums = local_force(1, plan, own, first, second, term, faces, face_terms, sums)

time: 149 us -> 141 us (0.946)
  starting transfers between devices: 45.5 us -> 37.7 us
  waiting for transfers between devices: 1.34 us -> 5.7 us
  Pallas kernels: 96.3 us -> 93.2 us
    all_to_all x4, starting transfers between devices: 39.5 us -> 32.5 us  [to_peers(): return lax.all_to_all(block, 'dev', split_axis=0, concat_axis=0, tiled=True)]
    all_to_all x4, waiting for transfers between devices: 0.01 us -> 5.69 us  [to_peers(): return lax.all_to_all(block, 'dev', split_axis=0, concat_axis=0, tiled=True)]
    pallas_call x4 -> x3, Pallas kernels: 45 us -> 41.5 us  [the longest x2 25.1 us: local_density(): pl.pallas_call(functools.partial(local_density_kernel, part), in_specs=in...]
  transfers between devices with their start and end apart: 8 -> 8, of which waited for: 1 -> 2; matrix products, arithmetic and copies ran while one was open for 1% -> 0% of each run, Pallas kernels for 48% -> 48%
where the time goes in v5:
time: 141 us; the launch traced here: 140 us
  Pallas kernels  93.2 us (66%)
  starting transfers between devices  37.7 us (27%)
  waiting for transfers between devices  5.7 us (4%)
  local copies, waits for them, and re-layouts  2.04 us (1%)
    all_to_all x4, starting transfers between devices, to_peers(): return lax.all_to_all(block, 'dev', split_axis=0, concat_axis=0, tiled=True)  32.5 us
    pallas_call x2, Pallas kernels, local_force(): pl.pallas_call(functools.partial(local_force_kernel, part), in_specs=[SM]...  30.3 us
    pallas_call x2, Pallas kernels, local_density(): pl.pallas_call(functools.partial(local_density_kernel, part), in_specs=in...  25.1 us
    pallas_call x1, Pallas kernels, cross_force(): pl.pallas_call(cross_force_kernel, in_specs=[SM, SM] + [VM] * 6 + [ANYWHE...  16.4 us
    pallas_call x1, Pallas kernels, cross_density(): pl.pallas_call(cross_density_kernel, in_specs=[SM, SM] + [VM] * 4, out_sp...  12.3 us
    all_to_all x4, waiting for transfers between devices, to_peers(): return lax.all_to_all(block, 'dev', split_axis=0, concat_axis=0, tiled=True)  5.69 us
    ppermute x2, starting transfers between devices, with_neighbours(): lax.ppermute(rows[..., :FACE * size, :], 'region', down)  5.13 us
    pallas_call x1, Pallas kernels, prepare(): pl.pallas_call(prepare_kernel, in_specs=[SM] * 2 + [ANYWHERE] * 4, out_sp...  3.66 us
  transfers between devices with their start and end apart: 8, of which 2 were waited for; matrix products, arithmetic and copies ran while one was open for 0% of the time, Pallas kernels for 48%

profile of v5, /device:TPU:0, one launch (start us, length us, event | category | flops | bytes accessed | tf_op | source)
XLA Modules:
  0.0 139.7 jit_solution(9116874047116894470)
XLA Ops:
  0.6 3.7 %shard_map.113 = (f32[2,520,128]{2,1,0:T(8,128)}, f32[16,160,128]{2,1,0:T(8,128)}) custom-call(s32[64]{0:T(128)} %refs_0_.1, s32[16,16]{1,0:T(8,128)} %bitcast.2, f32[3,64,256]{2,1,0:T(8,128)} %pos_in.1, f32[3,64,256]{2,1,0:T(8,128)} %vel_in.1, f32[64,256]{1,0:T(8,128)} %smooth_in.1, f32[64,256]{1,0:T(8,128)} %mass_in.1), custom_call_target="tpu_custom_call" | custom-call | tf_op jit(solution)/shard_map/pallas_call | solution.py:248
  4.3 0.0 copy-start.7
  4.3 0.0 copy-start.8
  4.3 0.0 copy-start.9
  4.3 8.1 %all-to-all-start = ((f32[16,160,128]{2,1,0:T(8,128)}), f32[16,160,128]{2,1,0:T(8,128)S(1)}, u32[]{:S(2)}, u32[]{:S(2)}) async-start(f32[16,160,128]{2,1,0:T(8,128)} %get-tuple-element.19), calls=%async_computation | async-start | bytes 2621440 | tf_op jit(solution)/shard_map/all_to_all | solution.py:936
  12.5 2.2 %collective-permute-start.1 = (f32[2,32,128]{2,1,0:T(8,128)S(1)}, f32[2,32,128]{2,1,0:T(8,128)S(1)}, u32[]{:S(2)}, u32[]{:S(2)}) collective-permute-start(f32[2,32,128]{2,1,0:T(8,128)S(1)} %get-tuple-element.28), channel_id=1, source_target_pairs={{0,112},{16,0},{32,16},{48,32},{64,48},{80,64},{96,80},{112,96},{1... | collective-permute-start | bytes 98312 | tf_op jit(solution)/shard_map/ppermute | solution.py:946
  14.7 15.3 %shard_map.114 = (f32[64,256]{1,0:T(8,128)S(1)}, f32[2,520,128]{2,1,0:T(8,128)S(1)}, f32[2,520,128]{2,1,0:T(8,128)S(1)}, s32[432]{0:T(512)S(1)}) custom-call(s32[64]{0:T(128)S(1)} %copy-done.8, s32[1,16]{1,0:T(1,128)S(1)} %copy-done.7, s32[16,16]{1,0:T(8,128)S(1)} %bitcast.5, f32[2,520,128]{2,1,0:T(8,128)S(1)} %copy-done), custom_call_target="tpu_custom_call" | custom-call | flops 251658240 | bytes 2097152 | tf_op jit(solution)/shard_map/pallas_call | solution.py:463
  30.0 3.3 %all-to-all-done.listed = f32[16,160,128]{2,1,0:T(8,128)S(1)} async-done(((f32[16,160,128]{2,1,0:T(8,128)}), f32[16,160,128]{2,1,0:T(8,128)S(1)}, u32[]{:S(2)}, u32[]{:S(2)}) %all-to-all-start) | async-done | bytes 1310752 | tf_op jit(solution)/shard_map/all_to_all | solution.py:936
  33.3 12.3 %shard_map.115 = (f32[64,256]{1,0:T(8,128)S(1)}, f32[16,16,256]{2,1,0:T(8,128)}) custom-call(s32[1,16]{1,0:T(1,128)S(1)} %copy-done.7, s32[432]{0:T(512)S(1)} %get-tuple-element.16.plan.refs_0_, f32[2,520,128]{2,1,0:T(8,128)S(1)} %copy-done, f32[2,520,128]{2,1,0:T(8,128)S(1)} %get-tuple-element.17.first.refs_2_, f32[16,160,128]{2,1,0:T(8,128)S(1)} %all-to-all-done.listed, ...), custom_call_target="tpu_custom_call" | custom-call | flops 314572800 | bytes 2097152 | tf_op jit(solution)/shard_map/pallas_call | solution.py:529
  45.6 6.9 %all-to-all-start.1 = ((f32[16,16,256]{2,1,0:T(8,128)}), f32[16,16,256]{2,1,0:T(8,128)S(1)}, u32[]{:S(2)}, u32[]{:S(2)}) async-start(f32[16,16,256]{2,1,0:T(8,128)} %get-tuple-element.22), calls=%async_computation.1 | async-start | bytes 524288 | tf_op jit(solution)/shard_map/all_to_all | solution.py:936
  52.5 9.8 %shard_map.116.near = f32[64,256]{1,0:T(8,128)S(1)} custom-call(s32[432]{0:T(512)S(1)} %get-tuple-element.16.plan.refs_0_, f32[2,520,128]{2,1,0:T(8,128)S(1)} %copy-done, f32[2,520,128]{2,1,0:T(8,128)S(1)} %get-tuple-element.17.first.refs_2_, f32[2,520,128]{2,1,0:T(8,128)S(1)} %get-tuple-element.18.refs_3_.second, ...), custom_call_target="tpu_custom_call" | custom-call | flops 251658240 | bytes 2097152 | tf_op jit(solution)/shard_map/pallas_call | solution.py:463
  62.3 3.0 %shard_map.117 = (f32[64,256]{1,0:T(8,128)}, f32[64,256]{1,0:T(8,128)S(1)}, f32[16,128,128]{2,1,0:T(8,128)S(1)}) custom-call(s32[16,16]{1,0:T(8,128)S(1)} %bitcast.3, f32[64,256]{1,0:T(8,128)S(1)} %shard_map.116.near, f32[16,16,256]{2,1,0:T(8,128)S(1)} %all-to-all-done.1.returned, f32[64,256]{1,0:T(8,128)S(1)} %copy-done.5, f32[2,520,128]{2,1,0:T(8,128)S(1)} %copy-done), custom_call_target="tpu_custom_call" | custom-call | tf_op jit(solution)/shard_map/pallas_call | solution.py:589
  65.3 1.0 copy-done.2
  66.3 7.0 %all-to-all-start.2 = ((f32[16,128,128]{2,1,0:T(8,128)}), f32[16,128,128]{2,1,0:T(8,128)S(1)}, u32[]{:S(2)}, u32[]{:S(2)}) async-start(f32[16,128,128]{2,1,0:T(8,128)} %copy-done.2), calls=%async_computation.2 | async-start | bytes 2097152 | tf_op jit(solution)/shard_map/all_to_all | solution.py:936
  73.3 0.0 collective-permute-start.2
  73.4 2.9 %collective-permute-start.3 = (f32[4,256]{1,0:T(4,128)S(1)}, f32[4,256]{1,0:T(4,128)S(1)}, u32[]{:S(2)}, u32[]{:S(2)}) collective-permute-start(f32[4,256]{1,0:T(4,128)S(1)} %get-tuple-element.31), channel_id=1, source_target_pairs={{0,112},{16,0},{32,16},{48,32},{64,48},{80,64},{96,80},{112,96},{1... | collective-permute-start | bytes 12296 | tf_op jit(solution)/shard_map/ppermute | solution.py:946
  76.3 17.1 %shard_map.118.carried = f32[4,64,256]{2,1,0:T(8,128)S(1)} custom-call(s32[432]{0:T(512)S(1)} %get-tuple-element.16.plan.refs_0_, f32[2,520,128]{2,1,0:T(8,128)S(1)} %copy-done, f32[2,520,128]{2,1,0:T(8,128)S(1)} %get-tuple-element.17.first.refs_2_, f32[2,520,128]{2,1,0:T(8,128)S(1)} %get-tuple-element.18.refs_3_.second, f32[64,256]{1,0:T(8,128)S(1)} %get-tuple-element.24.term), custom_call_target="tpu_custom_call" | custom-call | flops 335544320 | bytes 2097152 | tf_op jit(solution)/shard_map/pallas_call | solution.py:790
  93.4 16.4 %shard_map.119 = (f32[4,64,256]{2,1,0:T(8,128)S(1)}, f32[16,128,128]{2,1,0:T(8,128)S(1)}) custom-call(s32[1,16]{1,0:T(1,128)S(1)} %copy-done.7, s32[432]{0:T(512)S(1)} %get-tuple-element.16.plan.refs_0_, f32[2,520,128]{2,1,0:T(8,128)S(1)} %copy-done, f32[2,520,128]{2,1,0:T(8,128)S(1)} %get-tuple-element.17.first.refs_2_, ...), custom_call_target="tpu_custom_call" | custom-call | flops 419430400 | bytes 2097152 | tf_op jit(solution)/shard_map/pallas_call | solution.py:867
  109.9 1.0 copy-done.3
  110.9 10.5 %all-to-all-start.3 = ((f32[16,128,128]{2,1,0:T(8,128)}), f32[16,128,128]{2,1,0:T(8,128)S(1)}, u32[]{:S(2)}, u32[]{:S(2)}) async-start(f32[16,128,128]{2,1,0:T(8,128)} %copy-done.3), calls=%async_computation.3 | async-start | bytes 2097152 | tf_op jit(solution)/shard_map/all_to_all | solution.py:936
  121.4 0.0 copy-start.6
  121.4 13.2 %shard_map.120.near = f32[4,64,256]{2,1,0:T(8,128)S(1)} custom-call(s32[432]{0:T(512)S(1)} %get-tuple-element.16.plan.refs_0_, f32[2,520,128]{2,1,0:T(8,128)S(1)} %copy-done, f32[2,520,128]{2,1,0:T(8,128)S(1)} %get-tuple-element.17.first.refs_2_, f32[2,520,128]{2,1,0:T(8,128)S(1)} %get-tuple-element.18.refs_3_.second, f32[64,256]{1,0:T(8,128)S(1)} %get-tuple-element.24.term, ...), custom_call_target="tpu_custom_call" | custom-call | flops 335544320 | bytes 2097152 | tf_op jit(solution)/shard_map/pallas_call | solution.py:790
  134.6 2.4 %all-to-all-done.3.returned = f32[16,128,128]{2,1,0:T(8,128)S(1)} async-done(((f32[16,128,128]{2,1,0:T(8,128)}), f32[16,128,128]{2,1,0:T(8,128)S(1)}, u32[]{:S(2)}, u32[]{:S(2)}) %all-to-all-start.3) | async-done | bytes 1048608 | tf_op jit(solution)/shard_map/all_to_all | solution.py:936
  137.0 2.5 %shard_map.121 = f32[4,64,256]{2,1,0:T(8,128)} custom-call(s32[16,16]{1,0:T(8,128)S(1)} %bitcast.4, f32[4,64,256]{2,1,0:T(8,128)S(1)} %shard_map.120.near, f32[16,128,128]{2,1,0:T(8,128)S(1)} %all-to-all-done.3.returned, s32[64,256]{1,0:T(8,128)S(1)} %copy-done.6, f32[2,520,128]{2,1,0:T(8,128)S(1)} %copy-done), custom_call_target="tpu_custom_call" | custom-call | tf_op jit(solution)/shard_map/pallas_call | solution.py:920
  (26 shorter events, 0.1 us)
Async XLA Ops:
  4.3 8.2 %copy-start = (f32[2,520,128]{2,1,0:T(8,128)S(1)}, f32[2,520,128]{2,1,0:T(8,128)}, u32[]{:S(2)}) copy-start(f32[2,520,128]{2,1,0:T(8,128)} %get-tuple-element.15.refs_3_.own.refs_1_) | copy-start | bytes 1597444
  4.3 10.4 %copy-start.7 = (s32[1,16]{1,0:T(1,128)S(1)}, s32[1,16]{1,0:T(1,128)}, u32[]{:S(2)}) copy-start(s32[1,16]{1,0:T(1,128)} %fill.3) | copy-start | bytes 196
  4.3 10.4 %copy-start.8 = (s32[64]{0:T(128)S(1)}, s32[64]{0:T(128)}, u32[]{:S(2)}) copy-start(s32[64]{0:T(128)} %refs_0_.1) | copy-start | bytes 772
  4.3 10.3 %copy-start.9 = (s32[1,16,16]{2,1,0:T(8,128)S(1)}, s32[1,16,16]{2,1,0:T(8,128)}, u32[]{:S(2)}) copy-start(s32[1,16,16]{2,1,0:T(8,128)} %param.17) | copy-start | bytes 3076
  4.3 28.9 %all-to-all-start = ((f32[16,160,128]{2,1,0:T(8,128)}), f32[16,160,128]{2,1,0:T(8,128)S(1)}, u32[]{:S(2)}, u32[]{:S(2)}) async-start(f32[16,160,128]{2,1,0:T(8,128)} %get-tuple-element.19), calls=%async_computation | async-start | bytes 2621440 | tf_op jit(solution)/shard_map/all_to_all | solution.py:936
  12.5 40.0 %collective-permute-start.1 = (f32[2,32,128]{2,1,0:T(8,128)S(1)}, f32[2,32,128]{2,1,0:T(8,128)S(1)}, u32[]{:S(2)}, u32[]{:S(2)}) collective-permute-start(f32[2,32,128]{2,1,0:T(8,128)S(1)} %get-tuple-element.28), channel_id=1, source_target_pairs={{0,112},{16,0},{32,16},{48,32},{64,48},{80,64},{96,80},{112,96},{1... | collective-permute-start | bytes 98312 | tf_op jit(solution)/shard_map/ppermute | solution.py:946
  14.7 37.8 %collective-permute-start = (f32[2,32,128]{2,1,0:T(8,128)S(1)}, f32[2,32,128]{2,1,0:T(8,128)S(1)}, u32[]{:S(2)}, u32[]{:S(2)}) collective-permute-start(f32[2,32,128]{2,1,0:T(8,128)S(1)} %get-tuple-element.29), channel_id=1, source_target_pairs={{0,16},{16,32},{32,48},{48,64},{64,80},{80,96},{96,112},{112,0},{1... | collective-permute-start | bytes 98312 | tf_op jit(solution)/shard_map/ppermute | solution.py:945
  33.3 12.3 %copy-start.1 = (f32[16,160,128]{2,1,0:T(8,128)}, f32[16,160,128]{2,1,0:T(8,128)S(1)}, u32[]{:S(2)}) copy-start(f32[16,160,128]{2,1,0:T(8,128)S(1)} %all-to-all-done.listed) | copy-start | bytes 3932164
  45.6 16.8 %copy-start.4 = (s32[1,16,16]{2,1,0:T(8,128)S(1)}, s32[1,16,16]{2,1,0:T(8,128)}, u32[]{:S(2)}) copy-start(s32[1,16,16]{2,1,0:T(8,128)} %param.19) | copy-start | bytes 3076
  45.6 16.8 %copy-start.5 = (f32[64,256]{1,0:T(8,128)S(1)}, f32[64,256]{1,0:T(8,128)}, u32[]{:S(2)}) copy-start(f32[64,256]{1,0:T(8,128)} %energy_in.1) | copy-start | bytes 196612
  45.6 16.7 %all-to-all-start.1 = ((f32[16,16,256]{2,1,0:T(8,128)}), f32[16,16,256]{2,1,0:T(8,128)S(1)}, u32[]{:S(2)}, u32[]{:S(2)}) async-start(f32[16,16,256]{2,1,0:T(8,128)} %get-tuple-element.22), calls=%async_computation.1 | async-start | bytes 524288 | tf_op jit(solution)/shard_map/all_to_all | solution.py:936
  65.3 1.0 copy-start.2
  66.3 27.1 %all-to-all-start.2 = ((f32[16,128,128]{2,1,0:T(8,128)}), f32[16,128,128]{2,1,0:T(8,128)S(1)}, u32[]{:S(2)}, u32[]{:S(2)}) async-start(f32[16,128,128]{2,1,0:T(8,128)} %copy-done.2), calls=%async_computation.2 | async-start | bytes 2097152 | tf_op jit(solution)/shard_map/all_to_all | solution.py:936
  73.3 20.0 %collective-permute-start.2 = (f32[4,256]{1,0:T(4,128)S(1)}, f32[4,256]{1,0:T(4,128)S(1)}, u32[]{:S(2)}, u32[]{:S(2)}) collective-permute-start(f32[4,256]{1,0:T(4,128)S(1)} %get-tuple-element.30), channel_id=1, source_target_pairs={{0,16},{16,32},{32,48},{48,64},{64,80},{80,96},{96,112},{112,0},{1... | collective-permute-start | bytes 12296 | tf_op jit(solution)/shard_map/ppermute | solution.py:945
  73.4 20.0 %collective-permute-start.3 = (f32[4,256]{1,0:T(4,128)S(1)}, f32[4,256]{1,0:T(4,128)S(1)}, u32[]{:S(2)}, u32[]{:S(2)}) collective-permute-start(f32[4,256]{1,0:T(4,128)S(1)} %get-tuple-element.31), channel_id=1, source_target_pairs={{0,112},{16,0},{32,16},{48,32},{64,48},{80,64},{96,80},{112,96},{1... | collective-permute-start | bytes 12296 | tf_op jit(solution)/shard_map/ppermute | solution.py:946
  109.9 1.0 copy-start.3
  110.9 26.2 %all-to-all-start.3 = ((f32[16,128,128]{2,1,0:T(8,128)}), f32[16,128,128]{2,1,0:T(8,128)S(1)}, u32[]{:S(2)}, u32[]{:S(2)}) async-start(f32[16,128,128]{2,1,0:T(8,128)} %copy-done.3), calls=%async_computation.3 | async-start | bytes 2097152 | tf_op jit(solution)/shard_map/all_to_all | solution.py:936
  121.4 15.7 %copy-start.6 = (s32[64,256]{1,0:T(8,128)S(1)}, s32[64,256]{1,0:T(8,128)}, u32[]{:S(2)}) copy-start(s32[64,256]{1,0:T(8,128)} %active_in.1) | copy-start | bytes 196612

commit v6 on v5

--- a/solution.py
+++ b/solution.py
@@ -121,8 +121,8 @@
 
 
 def listed_support(listed, slot):
-    at = (slot % SLOTS) * ROWS + 3
-    return both(lambda h: listed[slot // SLOTS, pl.ds(h * SLOTS * ROWS + at, 1), :])
+    at = (slot & (SLOTS - 1)) * ROWS + 3
+    return both(lambda h: listed[slot >> 4, pl.ds(h * SLOTS * ROWS + at, 1), :])
 
 
 def first_operand(rows):
@@ -306,7 +306,7 @@
         for k in range(KINDS):
             places = places + jnp.left_shift(total, 8 * k)
             total = total + ((counts >> (8 * k)) & 255)
-            upto = (total + (unit - 1 if k == KINDS - 1 else 0)) // unit
+            upto = (total + (unit - 1 if k == KINDS - 1 else 0)) >> (unit.bit_length() - 1)
             plan[group * KINDS + k] = upto - done
             done = upto
         for k in range(lead):
@@ -364,14 +364,14 @@
 
     def item(n):
         entries = [plan[start + 2 * n + k] for k in range(2)]
-        return [(entry // PACK, entry % PACK) for entry in entries]
+        return [(entry >> 7, entry & (PACK - 1)) for entry in entries]
 
     return [plan[2 * KINDS + k] for k in range(KINDS)], item
 
 
 def live_parts(fill, visit, other):
     def step(n, _):
-        e, part = n // 2, n % 2
+        e, part = n >> 1, n & 1
         live = fill[0, e] > 8 * part
 
         @pl.when(live)
@@ -653,43 +653,55 @@
     s_ref[...] = jnp.dot(left, second_operands(rows, False), preferred_element_type=F32)
 
 
+def slope_sums(rows, high, low, dims):
+    top = lax.dot_general(rows, high, dims, preferred_element_type=F32)
+    rest = lax.dot_general(rows[:SUMS], low, dims, preferred_element_type=F32)
+    return top[:SUMS] + top[SUMS:] + rest
+
+
 def to_seconds(rows, count, high, low):
-    part = rows[:, :count]
-    top = lax.dot_general(part, high[0:count], NN, preferred_element_type=F32)
-    both = top + lax.dot_general(part, low[0:count], NN, preferred_element_type=F32)
-    return both[:SUMS] + both[SUMS:]
+    return slope_sums(rows[:, :count], high[0:count], low[0:count], NN)
 
 
 def to_firsts(rows, count, high, low):
-    top = lax.dot_general(rows, high[0:count], NT, preferred_element_type=F32)
-    both = top + lax.dot_general(rows, low[0:count], NT, preferred_element_type=F32)
-    return both[:SUMS] + both[SUMS:]
-
-
-def in_three_turns(trips, sizes, item, last, products, tiles, sums, slot_a, slot_b):
+    return slope_sums(rows, high[0:count], low[0:count], NT)
+
+
+def in_three_turns(trips, sizes, item, last, products, tiles, sums, slot_a, slot_b, lag):
     products(item(0), slot_a)
     base = 0
     for count, size in zip(trips, sizes):
 
         def step(i, _, size=size):
-            products(item(2 * i + 1), slot_b)
-            sums(size, item(2 * i - 2), slot_a)
-            tiles(size, item(2 * i), slot_a)
             after = 2 * i + 2
-            products(item(after if last is None else jnp.minimum(after, last - 1)), slot_a)
-            sums(size, item(2 * i - 1), slot_b)
-            tiles(size, item(2 * i + 1), slot_b)
+            if last is not None:
+                after = jnp.minimum(after, last - 1)
+            if lag == 1:
+                sums(size, item(2 * i - 1), slot_b)
+                tiles(size, item(2 * i), slot_a)
+                products(item(2 * i + 1), slot_b)
+                sums(size, item(2 * i), slot_a)
+                tiles(size, item(2 * i + 1), slot_b)
+                products(item(after), slot_a)
+            else:
+                products(item(2 * i + 1), slot_b)
+                sums(size, item(2 * i - 2), slot_a)
+                tiles(size, item(2 * i), slot_a)
+                products(item(after), slot_a)
+                sums(size, item(2 * i - 1), slot_b)
+                tiles(size, item(2 * i + 1), slot_b)
             return 0
 
         lax.fori_loop(base, base + count, step, 0)
         base = base + count
-    sums(sizes[-1], item(2 * base - 2), slot_a)
+    if lag == 2:
+        sums(sizes[-1], item(2 * base - 2), slot_a)
     sums(sizes[-1], item(2 * base - 1), slot_b)
 
 
 def clear(slots):
     for held in slots:
-        held[...] = jnp.zeros_like(held)
+        held[SIZES[0] :, :] = jnp.zeros((WIDTH - SIZES[0], WIDTH), BF)
 
 
 def add_forces(total, own, term, out, carried):
@@ -731,7 +743,7 @@
         add_block(total, after, SUMS, to_seconds(mine, count, *held[5:7]))
 
     trips, item = cell_list(plan, part)
-    in_three_turns(trips, SIZES, item, None, products, tiles, sums, slot_a, slot_b)
+    in_three_turns(trips, SIZES, item, None, products, tiles, sums, slot_a, slot_b, 1)
 
     if part:
         make_face_first(faces, face_first)
@@ -765,7 +777,7 @@
 
         in_three_turns(
             [FACE // 2], [WIDTH], lambda i: i, FACE, face_products, face_tiles, face_sums,
-            slot_a, slot_b,
+            slot_a, slot_b, 1,
         )
 
     add_forces(total, own, term, out, carried)
@@ -841,7 +853,7 @@
             add_block(total, c, SUMS, added)
 
     trips, item = pair_list(plan)
-    in_three_turns(trips, SIZES, item, None, products, tiles, sums, slot_a, slot_b)
+    in_three_turns(trips, SIZES, item, None, products, tiles, sums, slot_a, slot_b, 2)
 
     def send(e, part):
         planes = listed_planes(listed, e, part, range(3), ROWS)

time: 141 us -> 138 us (0.979); the launches traced: 140 us -> 135 us
  starting transfers between devices: 37.7 us -> 32.8 us
  waiting for transfers between devices: 5.7 us -> 7.15 us
    all_to_all x4, starting transfers between devices: 32.5 us -> 26.5 us  [to_peers(): return lax.all_to_all(block, 'dev', split_axis=0, concat_axis=0, tiled=True)]
    pallas_call x2, Pallas kernels: 30.3 us -> 27 us  [local_force(): pl.pallas_call(functools.partial(local_force_kernel, part), in_specs=[SM]...]
    all_to_all x4, waiting for transfers between devices: 5.69 us -> 7.14 us  [to_peers(): return lax.all_to_all(block, 'dev', split_axis=0, concat_axis=0, tiled=True)]
where the time goes in v6:
time: 138 us; the launch traced here: 135 us
  Pallas kernels  92.1 us (67%)
  starting transfers between devices  32.8 us (24%)
  waiting for transfers between devices  7.15 us (5%)
  local copies, waits for them, and re-layouts  2.04 us (1%)
    pallas_call x2, Pallas kernels, local_force(): pl.pallas_call(functools.partial(local_force_kernel, part), in_specs=[SM]...  27 us
    all_to_all x4, starting transfers between devices, to_peers(): return lax.all_to_all(block, 'dev', split_axis=0, concat_axis=0, tiled=True)  26.5 us
    pallas_call x2, Pallas kernels, local_density(): pl.pallas_call(functools.partial(local_density_kernel, part), in_specs=in...  25.2 us
    pallas_call x1, Pallas kernels, cross_force(): pl.pallas_call(cross_force_kernel, in_specs=[SM, SM] + [VM] * 6 + [ANYWHE...  17.5 us
    pallas_call x1, Pallas kernels, cross_density(): pl.pallas_call(cross_density_kernel, in_specs=[SM, SM] + [VM] * 4, out_sp...  13.3 us
    all_to_all x4, waiting for transfers between devices, to_peers(): return lax.all_to_all(block, 'dev', split_axis=0, concat_axis=0, tiled=True)  7.14 us
    ppermute x2, starting transfers between devices, with_neighbours(): lax.ppermute(rows[..., :FACE * size, :], 'region', down)  6.28 us
    pallas_call x1, Pallas kernels, prepare(): pl.pallas_call(prepare_kernel, in_specs=[SM] * 2 + [ANYWHERE] * 4, out_sp...  3.67 us
  transfers between devices with their start and end apart: 8, of which 2 were waited for; matrix products, arithmetic and copies ran while one was open for 0% of the time, Pallas kernels for 48%

profile of v6, /device:TPU:0, one launch (start us, length us, event | category | flops | bytes accessed | tf_op | source)
XLA Modules:
  0.0 135.2 jit_solution(11828636378486957880)
XLA Ops:
  0.6 3.7 %shard_map.113 = (f32[2,520,128]{2,1,0:T(8,128)}, f32[16,160,128]{2,1,0:T(8,128)}) custom-call(s32[64]{0:T(128)} %refs_0_.1, s32[16,16]{1,0:T(8,128)} %bitcast.2, f32[3,64,256]{2,1,0:T(8,128)} %pos_in.1, f32[3,64,256]{2,1,0:T(8,128)} %vel_in.1, f32[64,256]{1,0:T(8,128)} %smooth_in.1, f32[64,256]{1,0:T(8,128)} %mass_in.1), custom_call_target="tpu_custom_call" | custom-call | tf_op jit(solution)/shard_map/pallas_call | solution.py:248
  4.3 0.0 copy-start.7
  4.3 0.0 copy-start.8
  4.3 0.0 copy-start.9
  4.3 8.1 %all-to-all-start = ((f32[16,160,128]{2,1,0:T(8,128)}), f32[16,160,128]{2,1,0:T(8,128)S(1)}, u32[]{:S(2)}, u32[]{:S(2)}) async-start(f32[16,160,128]{2,1,0:T(8,128)} %get-tuple-element.19), calls=%async_computation | async-start | bytes 2621440 | tf_op jit(solution)/shard_map/all_to_all | solution.py:948
  12.5 2.2 %collective-permute-start.1 = (f32[2,32,128]{2,1,0:T(8,128)S(1)}, f32[2,32,128]{2,1,0:T(8,128)S(1)}, u32[]{:S(2)}, u32[]{:S(2)}) collective-permute-start(f32[2,32,128]{2,1,0:T(8,128)S(1)} %get-tuple-element.28), channel_id=1, source_target_pairs={{0,112},{16,0},{32,16},{48,32},{64,48},{80,64},{96,80},{112,96},{1... | collective-permute-start | bytes 98312 | tf_op jit(solution)/shard_map/ppermute | solution.py:958
  14.7 15.6 %shard_map.114 = (f32[64,256]{1,0:T(8,128)S(1)}, f32[2,520,128]{2,1,0:T(8,128)S(1)}, f32[2,520,128]{2,1,0:T(8,128)S(1)}, s32[432]{0:T(512)S(1)}) custom-call(s32[64]{0:T(128)S(1)} %copy-done.8, s32[1,16]{1,0:T(1,128)S(1)} %copy-done.7, s32[16,16]{1,0:T(8,128)S(1)} %bitcast.5, f32[2,520,128]{2,1,0:T(8,128)S(1)} %copy-done), custom_call_target="tpu_custom_call" | custom-call | flops 251658240 | bytes 2097152 | tf_op jit(solution)/shard_map/pallas_call | solution.py:463
  30.3 3.0 %all-to-all-done.listed = f32[16,160,128]{2,1,0:T(8,128)S(1)} async-done(((f32[16,160,128]{2,1,0:T(8,128)}), f32[16,160,128]{2,1,0:T(8,128)S(1)}, u32[]{:S(2)}, u32[]{:S(2)}) %all-to-all-start) | async-done | bytes 1310752 | tf_op jit(solution)/shard_map/all_to_all | solution.py:948
  33.3 13.3 %shard_map.115 = (f32[64,256]{1,0:T(8,128)S(1)}, f32[16,16,256]{2,1,0:T(8,128)}) custom-call(s32[1,16]{1,0:T(1,128)S(1)} %copy-done.7, s32[432]{0:T(512)S(1)} %get-tuple-element.16.plan.refs_0_, f32[2,520,128]{2,1,0:T(8,128)S(1)} %copy-done, f32[2,520,128]{2,1,0:T(8,128)S(1)} %get-tuple-element.17.first.refs_2_, f32[16,160,128]{2,1,0:T(8,128)S(1)} %all-to-all-done.listed, ...), custom_call_target="tpu_custom_call" | custom-call | flops 314572800 | bytes 2097152 | tf_op jit(solution)/shard_map/pallas_call | solution.py:529
  46.6 4.1 %all-to-all-start.1 = ((f32[16,16,256]{2,1,0:T(8,128)}), f32[16,16,256]{2,1,0:T(8,128)S(1)}, u32[]{:S(2)}, u32[]{:S(2)}) async-start(f32[16,16,256]{2,1,0:T(8,128)} %get-tuple-element.22), calls=%async_computation.1 | async-start | bytes 524288 | tf_op jit(solution)/shard_map/all_to_all | solution.py:948
  50.7 9.6 %shard_map.116.near = f32[64,256]{1,0:T(8,128)S(1)} custom-call(s32[432]{0:T(512)S(1)} %get-tuple-element.16.plan.refs_0_, f32[2,520,128]{2,1,0:T(8,128)S(1)} %copy-done, f32[2,520,128]{2,1,0:T(8,128)S(1)} %get-tuple-element.17.first.refs_2_, f32[2,520,128]{2,1,0:T(8,128)S(1)} %get-tuple-element.18.refs_3_.second, ...), custom_call_target="tpu_custom_call" | custom-call | flops 251658240 | bytes 2097152 | tf_op jit(solution)/shard_map/pallas_call | solution.py:463
  60.3 3.0 %shard_map.117 = (f32[64,256]{1,0:T(8,128)}, f32[64,256]{1,0:T(8,128)S(1)}, f32[16,128,128]{2,1,0:T(8,128)S(1)}) custom-call(s32[16,16]{1,0:T(8,128)S(1)} %bitcast.3, f32[64,256]{1,0:T(8,128)S(1)} %shard_map.116.near, f32[16,16,256]{2,1,0:T(8,128)S(1)} %all-to-all-done.1.returned, f32[64,256]{1,0:T(8,128)S(1)} %copy-done.5, f32[2,520,128]{2,1,0:T(8,128)S(1)} %copy-done), custom_call_target="tpu_custom_call" | custom-call | tf_op jit(solution)/shard_map/pallas_call | solution.py:589
  63.3 1.0 copy-done.2
  64.3 7.3 %all-to-all-start.2 = ((f32[16,128,128]{2,1,0:T(8,128)}), f32[16,128,128]{2,1,0:T(8,128)S(1)}, u32[]{:S(2)}, u32[]{:S(2)}) async-start(f32[16,128,128]{2,1,0:T(8,128)} %copy-done.2), calls=%async_computation.2 | async-start | bytes 2097152 | tf_op jit(solution)/shard_map/all_to_all | solution.py:948
  71.6 0.0 collective-permute-start.2
  71.6 4.1 %collective-permute-start.3 = (f32[4,256]{1,0:T(4,128)S(1)}, f32[4,256]{1,0:T(4,128)S(1)}, u32[]{:S(2)}, u32[]{:S(2)}) collective-permute-start(f32[4,256]{1,0:T(4,128)S(1)} %get-tuple-element.31), channel_id=1, source_target_pairs={{0,112},{16,0},{32,16},{48,32},{64,48},{80,64},{96,80},{112,96},{1... | collective-permute-start | bytes 12296 | tf_op jit(solution)/shard_map/ppermute | solution.py:958
  75.7 15.2 %shard_map.118.carried = f32[4,64,256]{2,1,0:T(8,128)S(1)} custom-call(s32[432]{0:T(512)S(1)} %get-tuple-element.16.plan.refs_0_, f32[2,520,128]{2,1,0:T(8,128)S(1)} %copy-done, f32[2,520,128]{2,1,0:T(8,128)S(1)} %get-tuple-element.17.first.refs_2_, f32[2,520,128]{2,1,0:T(8,128)S(1)} %get-tuple-element.18.refs_3_.second, f32[64,256]{1,0:T(8,128)S(1)} %get-tuple-element.24.term), custom_call_target="tpu_custom_call" | custom-call | flops 335544320 | bytes 2097152 | tf_op jit(solution)/shard_map/pallas_call | solution.py:802
  91.0 17.5 %shard_map.119 = (f32[4,64,256]{2,1,0:T(8,128)S(1)}, f32[16,128,128]{2,1,0:T(8,128)S(1)}) custom-call(s32[1,16]{1,0:T(1,128)S(1)} %copy-done.7, s32[432]{0:T(512)S(1)} %get-tuple-element.16.plan.refs_0_, f32[2,520,128]{2,1,0:T(8,128)S(1)} %copy-done, f32[2,520,128]{2,1,0:T(8,128)S(1)} %get-tuple-element.17.first.refs_2_, ...), custom_call_target="tpu_custom_call" | custom-call | flops 419430400 | bytes 2097152 | tf_op jit(solution)/shard_map/pallas_call | solution.py:879
  108.5 1.0 copy-done.3
  109.5 7.1 %all-to-all-start.3 = ((f32[16,128,128]{2,1,0:T(8,128)}), f32[16,128,128]{2,1,0:T(8,128)S(1)}, u32[]{:S(2)}, u32[]{:S(2)}) async-start(f32[16,128,128]{2,1,0:T(8,128)} %copy-done.3), calls=%async_computation.3 | async-start | bytes 2097152 | tf_op jit(solution)/shard_map/all_to_all | solution.py:948
  116.6 0.0 copy-start.6
  116.6 11.8 %shard_map.120.near = f32[4,64,256]{2,1,0:T(8,128)S(1)} custom-call(s32[432]{0:T(512)S(1)} %get-tuple-element.16.plan.refs_0_, f32[2,520,128]{2,1,0:T(8,128)S(1)} %copy-done, f32[2,520,128]{2,1,0:T(8,128)S(1)} %get-tuple-element.17.first.refs_2_, f32[2,520,128]{2,1,0:T(8,128)S(1)} %get-tuple-element.18.refs_3_.second, f32[64,256]{1,0:T(8,128)S(1)} %get-tuple-element.24.term, ...), custom_call_target="tpu_custom_call" | custom-call | flops 335544320 | bytes 2097152 | tf_op jit(solution)/shard_map/pallas_call | solution.py:802
  128.4 4.1 %all-to-all-done.3.returned = f32[16,128,128]{2,1,0:T(8,128)S(1)} async-done(((f32[16,128,128]{2,1,0:T(8,128)}), f32[16,128,128]{2,1,0:T(8,128)S(1)}, u32[]{:S(2)}, u32[]{:S(2)}) %all-to-all-start.3) | async-done | bytes 1048608 | tf_op jit(solution)/shard_map/all_to_all | solution.py:948
  132.6 2.5 %shard_map.121 = f32[4,64,256]{2,1,0:T(8,128)} custom-call(s32[16,16]{1,0:T(8,128)S(1)} %bitcast.4, f32[4,64,256]{2,1,0:T(8,128)S(1)} %shard_map.120.near, f32[16,128,128]{2,1,0:T(8,128)S(1)} %all-to-all-done.3.returned, s32[64,256]{1,0:T(8,128)S(1)} %copy-done.6, f32[2,520,128]{2,1,0:T(8,128)S(1)} %copy-done), custom_call_target="tpu_custom_call" | custom-call | tf_op jit(solution)/shard_map/pallas_call | solution.py:932
  (26 shorter events, 0.1 us)
Async XLA Ops:
  4.3 8.2 %copy-start = (f32[2,520,128]{2,1,0:T(8,128)S(1)}, f32[2,520,128]{2,1,0:T(8,128)}, u32[]{:S(2)}) copy-start(f32[2,520,128]{2,1,0:T(8,128)} %get-tuple-element.15.refs_3_.own.refs_1_) | copy-start | bytes 1597444
  4.3 10.4 %copy-start.7 = (s32[1,16]{1,0:T(1,128)S(1)}, s32[1,16]{1,0:T(1,128)}, u32[]{:S(2)}) copy-start(s32[1,16]{1,0:T(1,128)} %fill.3) | copy-start | bytes 196
  4.3 10.4 %copy-start.8 = (s32[64]{0:T(128)S(1)}, s32[64]{0:T(128)}, u32[]{:S(2)}) copy-start(s32[64]{0:T(128)} %refs_0_.1) | copy-start | bytes 772
  4.3 10.3 %copy-start.9 = (s32[1,16,16]{2,1,0:T(8,128)S(1)}, s32[1,16,16]{2,1,0:T(8,128)}, u32[]{:S(2)}) copy-start(s32[1,16,16]{2,1,0:T(8,128)} %param.17) | copy-start | bytes 3076
  4.3 28.9 %all-to-all-start = ((f32[16,160,128]{2,1,0:T(8,128)}), f32[16,160,128]{2,1,0:T(8,128)S(1)}, u32[]{:S(2)}, u32[]{:S(2)}) async-start(f32[16,160,128]{2,1,0:T(8,128)} %get-tuple-element.19), calls=%async_computation | async-start | bytes 2621440 | tf_op jit(solution)/shard_map/all_to_all | solution.py:948
  12.5 38.2 %collective-permute-start.1 = (f32[2,32,128]{2,1,0:T(8,128)S(1)}, f32[2,32,128]{2,1,0:T(8,128)S(1)}, u32[]{:S(2)}, u32[]{:S(2)}) collective-permute-start(f32[2,32,128]{2,1,0:T(8,128)S(1)} %get-tuple-element.28), channel_id=1, source_target_pairs={{0,112},{16,0},{32,16},{48,32},{64,48},{80,64},{96,80},{112,96},{1... | collective-permute-start | bytes 98312 | tf_op jit(solution)/shard_map/ppermute | solution.py:958
  14.7 36.0 %collective-permute-start = (f32[2,32,128]{2,1,0:T(8,128)S(1)}, f32[2,32,128]{2,1,0:T(8,128)S(1)}, u32[]{:S(2)}, u32[]{:S(2)}) collective-permute-start(f32[2,32,128]{2,1,0:T(8,128)S(1)} %get-tuple-element.29), channel_id=1, source_target_pairs={{0,16},{16,32},{32,48},{48,64},{64,80},{80,96},{96,112},{112,0},{1... | collective-permute-start | bytes 98312 | tf_op jit(solution)/shard_map/ppermute | solution.py:957
  33.3 13.3 %copy-start.1 = (f32[16,160,128]{2,1,0:T(8,128)}, f32[16,160,128]{2,1,0:T(8,128)S(1)}, u32[]{:S(2)}) copy-start(f32[16,160,128]{2,1,0:T(8,128)S(1)} %all-to-all-done.listed) | copy-start | bytes 3932164
  46.6 13.8 %copy-start.4 = (s32[1,16,16]{2,1,0:T(8,128)S(1)}, s32[1,16,16]{2,1,0:T(8,128)}, u32[]{:S(2)}) copy-start(s32[1,16,16]{2,1,0:T(8,128)} %param.19) | copy-start | bytes 3076
  46.6 13.8 %copy-start.5 = (f32[64,256]{1,0:T(8,128)S(1)}, f32[64,256]{1,0:T(8,128)}, u32[]{:S(2)}) copy-start(f32[64,256]{1,0:T(8,128)} %energy_in.1) | copy-start | bytes 196612
  46.6 13.7 %all-to-all-start.1 = ((f32[16,16,256]{2,1,0:T(8,128)}), f32[16,16,256]{2,1,0:T(8,128)S(1)}, u32[]{:S(2)}, u32[]{:S(2)}) async-start(f32[16,16,256]{2,1,0:T(8,128)} %get-tuple-element.22), calls=%async_computation.1 | async-start | bytes 524288 | tf_op jit(solution)/shard_map/all_to_all | solution.py:948
  63.3 1.0 copy-start.2
  64.3 26.7 %all-to-all-start.2 = ((f32[16,128,128]{2,1,0:T(8,128)}), f32[16,128,128]{2,1,0:T(8,128)S(1)}, u32[]{:S(2)}, u32[]{:S(2)}) async-start(f32[16,128,128]{2,1,0:T(8,128)} %copy-done.2), calls=%async_computation.2 | async-start | bytes 2097152 | tf_op jit(solution)/shard_map/all_to_all | solution.py:948
  71.6 19.3 %collective-permute-start.2 = (f32[4,256]{1,0:T(4,128)S(1)}, f32[4,256]{1,0:T(4,128)S(1)}, u32[]{:S(2)}, u32[]{:S(2)}) collective-permute-start(f32[4,256]{1,0:T(4,128)S(1)} %get-tuple-element.30), channel_id=1, source_target_pairs={{0,16},{16,32},{32,48},{48,64},{64,80},{80,96},{96,112},{112,0},{1... | collective-permute-start | bytes 12296 | tf_op jit(solution)/shard_map/ppermute | solution.py:957
  71.6 19.3 %collective-permute-start.3 = (f32[4,256]{1,0:T(4,128)S(1)}, f32[4,256]{1,0:T(4,128)S(1)}, u32[]{:S(2)}, u32[]{:S(2)}) collective-permute-start(f32[4,256]{1,0:T(4,128)S(1)} %get-tuple-element.31), channel_id=1, source_target_pairs={{0,112},{16,0},{32,16},{48,32},{64,48},{80,64},{96,80},{112,96},{1... | collective-permute-start | bytes 12296 | tf_op jit(solution)/shard_map/ppermute | solution.py:958
  108.5 1.0 copy-start.3
  109.5 23.0 %all-to-all-start.3 = ((f32[16,128,128]{2,1,0:T(8,128)}), f32[16,128,128]{2,1,0:T(8,128)S(1)}, u32[]{:S(2)}, u32[]{:S(2)}) async-start(f32[16,128,128]{2,1,0:T(8,128)} %copy-done.3), calls=%async_computation.3 | async-start | bytes 2097152 | tf_op jit(solution)/shard_map/all_to_all | solution.py:948
  116.6 15.9 %copy-start.6 = (s32[64,256]{1,0:T(8,128)S(1)}, s32[64,256]{1,0:T(8,128)}, u32[]{:S(2)}) copy-start(s32[64,256]{1,0:T(8,128)} %active_in.1) | copy-start | bytes 196612

commit v7 on v6

--- a/solution.py
+++ b/solution.py
@@ -30,14 +30,15 @@
 SM = pl.BlockSpec(memory_space=pltpu.SMEM)
 ROWS = 5
 MOVING = 4
-SPLIT = 40
+SPEEDS = 3
+SPLITS = (40, 24)
 SIZES = (160, 192, 224, 256)
 KINDS = len(SIZES)
 UNIT = 4
-LOCAL_AT = 16
+LOCAL_AT = 5 * KINDS
 LOCAL_LEAD = 2
 LOCAL_LIST = CELLS + 8
-CROSS_AT = LOCAL_AT + 2 * LOCAL_LIST
+CROSS_AT = LOCAL_AT + 4 * LOCAL_LIST
 CROSS_LEAD = 4
 CROSS_LIST = LISTED + 16
 PLAN = CROSS_AT + CROSS_LIST
@@ -270,8 +271,9 @@
 
 
 def make_plan(occ, fill, cells, plan):
-    def over_local(visit, part, carry):
-        low, high = (SPLIT, CELLS) if part else (0, SPLIT)
+    def over_local(visit, group, carry):
+        split = SPLITS[group // 2]
+        low, high = (split, CELLS) if group % 2 else (0, split)
         step = lambda c, carry: visit(kind_of(occ[c]), c, carry)
         return lax.fori_loop(low, high, step, carry, unroll=8)
 
@@ -292,13 +294,15 @@
     def one_of(kind):
         return jnp.left_shift(jnp.int32(1), 8 * kind)
 
-    for group, (walk, start, lead, unit, blank) in enumerate(
-        [
-            (lambda v, x: over_local(v, 0, x), LOCAL_AT, LOCAL_LEAD, 2, CELLS),
-            (lambda v, x: over_local(v, 1, x), LOCAL_AT + LOCAL_LIST, LOCAL_LEAD, 2, CELLS),
-            (over_pairs, CROSS_AT, CROSS_LEAD, UNIT, unused * PACK + CELLS),
-        ]
-    ):
+    groups = [
+        (
+            functools.partial(lambda g, v, x: over_local(v, g, x), g),
+            LOCAL_AT + g * LOCAL_LIST, LOCAL_LEAD, 2, CELLS,
+        )
+        for g in range(4)
+    ]
+    groups.append((over_pairs, CROSS_AT, CROSS_LEAD, UNIT, unused * PACK + CELLS))
+    for group, (walk, start, lead, unit, blank) in enumerate(groups):
         counts = walk(lambda kind, value, packed: packed + one_of(kind), jnp.int32(0))
         total = jnp.int32(0)
         done = jnp.int32(0)
@@ -354,9 +358,9 @@
         base = base + count
 
 
-def cell_list(plan, part):
-    start = LOCAL_AT + part * LOCAL_LIST + LOCAL_LEAD
-    return [plan[part * KINDS + k] for k in range(KINDS)], lambda n: plan[start + n]
+def cell_list(plan, group):
+    start = LOCAL_AT + group * LOCAL_LIST + LOCAL_LEAD
+    return [plan[group * KINDS + k] for k in range(KINDS)], lambda n: plan[start + n]
 
 
 def pair_list(plan):
@@ -366,7 +370,7 @@
         entries = [plan[start + 2 * n + k] for k in range(2)]
         return [(entry >> 7, entry & (PACK - 1)) for entry in entries]
 
-    return [plan[2 * KINDS + k] for k in range(KINDS)], item
+    return [plan[4 * KINDS + k] for k in range(KINDS)], item
 
 
 def live_parts(fill, visit, other):
@@ -394,8 +398,18 @@
         plan, own, first, second, faces, carried, rho, total, face_first, *slots = refs
     else:
         carried = None
-        occ, fill, cells, own, rho, first, second, plan, total, *slots = refs
+        occ, fill, cells, pair, own, rho, first, second, speeds, plan, total, *slots = refs
         make_plan(occ, fill, cells, plan)
+
+        def peer_step(e, _):
+            for s in range(SLOTS):
+                c = pair[e, s]
+                for h in range(2):
+                    at = (h * SLOTS + s) * SPEEDS
+                    speeds[e, at : at + SPEEDS] = own[h, rows_at(c, CELL), :][5:8]
+            return 0
+
+        lax.fori_loop(0, PEERS, peer_step, 0)
         planes = planes_of(own, range(ROWS), 0, CELLS, CELL)
         blank = [jnp.zeros((1, WIDTH), F32)] * 3 + [jnp.full((1, WIDTH), 0.5, F32)]
         for ref, some, none in zip(
@@ -458,8 +472,14 @@
     if part:
         in_specs, out_specs, out_shape = [SM] + [VM] * 5, VM, plane
     else:
-        in_specs, out_specs = [SM] * 3 + [VM], [VM] * 3 + [SM]
-        out_shape = [plane, OWN_ROWS, OWN_ROWS, jax.ShapeDtypeStruct((PLAN,), jnp.int32)]
+        in_specs, out_specs = [SM] * 4 + [VM], [VM] * 4 + [SM]
+        out_shape = [
+            plane,
+            OWN_ROWS,
+            OWN_ROWS,
+            jax.ShapeDtypeStruct((PEERS, 2 * SLOTS * SPEEDS, 128), F32),
+            jax.ShapeDtypeStruct((PLAN,), jnp.int32),
+        ]
     return pl.pallas_call(
         functools.partial(local_density_kernel, part),
         in_specs=in_specs,
@@ -548,7 +568,7 @@
 
 
 def pressure_kernel(
-    pair, near, returned, energy_in, own, density, term, out, energy, sum_of, moving, sem
+    pair, near, returned, energy_in, own, density, term, out, energy, sum_of, sem
 ):
     copies = fetch([(energy_in, energy)], sem)
     sum_of[...] = near[...]
@@ -565,20 +585,9 @@
     density[...] = rho
     term[...] = jnp.where(full, GAMMA_LESS * energy[...] / jnp.where(full, rho, 1.0), 0.0)
 
-    def cell_step(c, _):
-        moving[c] = jnp.concatenate(
-            [line(own, c, CELL, k) for k in (5, 6, 7)] + [term[pl.ds(c, 1), :]], 0
-        )
-        return 0
-
-    lax.fori_loop(0, CELLS, cell_step, 0, unroll=8)
-
     def send_step(e, _):
         for s in range(SLOTS):
-            cell = moving[pair[e, s]]
-            for h in range(2):
-                at = (h * SLOTS + s) * MOVING
-                out[e, at : at + MOVING] = half(cell, h)
+            out[e, s : s + 1] = term[pl.ds(pair[e, s], 1), :]
         return 0
 
     lax.fori_loop(0, PEERS, send_step, 0)
@@ -593,12 +602,11 @@
         out_shape=[
             plane,
             plane,
-            jax.ShapeDtypeStruct((PEERS, 2 * SLOTS * MOVING, 128), F32),
+            jax.ShapeDtypeStruct((PEERS, SLOTS, WIDTH), F32),
         ],
         scratch_shapes=[
             pltpu.VMEM((CELLS, WIDTH), F32),
             pltpu.VMEM((CELLS, WIDTH), F32),
-            pltpu.VMEM((CELLS, MOVING, WIDTH), F32),
             pltpu.SemaphoreType.DMA((1,)),
         ],
         compiler_params=params(),
@@ -742,7 +750,7 @@
         add_block(total, c, SUMS, to_seconds(mine, count, *held[2:4]) + added)
         add_block(total, after, SUMS, to_seconds(mine, count, *held[5:7]))
 
-    trips, item = cell_list(plan, part)
+    trips, item = cell_list(plan, 2 + part)
     in_three_turns(trips, SIZES, item, None, products, tiles, sums, slot_a, slot_b, 1)
 
     if part:
@@ -813,7 +821,7 @@
 
 
 def cross_force_kernel(
-    fill, plan, own, first, term, listed, arrived, carried, _, out, back,
+    fill, plan, own, first, term, listed, speeds, terms_of, carried, _, out, back,
     rows, total, theirs, their_rows, sums_of, *slots
 ):
     slot_a, slot_b = slots[:8], slots[8:]
@@ -825,7 +833,8 @@
         planes = listed_planes(listed, e, part, range(ROWS), ROWS)
         at = e * SLOTS + 8 * part
         put(theirs, pair_terms(*planes)[1], at * CELL, 8, CELL)
-        *speed, pressed = listed_planes(arrived, e, part, range(MOVING), MOVING)
+        speed = listed_planes(speeds, e, part, range(SPEEDS), SPEEDS)
+        pressed = terms_of[e, rows_at(part, 8), :]
         terms = force_terms(planes[0:3], planes[4], speed, pressed)
         blank = jnp.zeros((8, WIDTH), F32)
         put(their_rows, terms + [blank] * 4, at * SUMS, 8, SUMS)
@@ -857,7 +866,8 @@
 
     def send(e, part):
         planes = listed_planes(listed, e, part, range(3), ROWS)
-        *speed, pressed = listed_planes(arrived, e, part, range(MOVING), MOVING)
+        speed = listed_planes(speeds, e, part, range(SPEEDS), SPEEDS)
+        pressed = terms_of[e, rows_at(part, 8), :]
         summed = planes_of(sums_of, range(12), (e * SLOTS + 8 * part) * SUMS, 8, SUMS)
         live = live_rows(fill, e, part)
         send_rows(e, part, [jnp.where(live, f, 0.0) for f in forces_of(summed, planes, speed, pressed)])
@@ -875,10 +885,10 @@
     add_forces(total, own, term, out, carried)
 
 
-def cross_force(fill, plan, own, first, term, listed, arrived, carried, after):
+def cross_force(fill, plan, own, first, term, listed, speeds, terms, carried, after):
     return pl.pallas_call(
         cross_force_kernel,
-        in_specs=[SM, SM] + [VM] * 6 + [ANYWHERE],
+        in_specs=[SM, SM] + [VM] * 7 + [ANYWHERE],
         out_specs=[VM, VM],
         out_shape=[
             jax.ShapeDtypeStruct((4, CELLS, WIDTH), F32),
@@ -896,7 +906,7 @@
             flops=80 * 65536 * 80, bytes_accessed=2 * 2**20, transcendentals=0
         ),
         compiler_params=params(),
-    )(fill, plan, own, first, term, listed, arrived, carried, after)
+    )(fill, plan, own, first, term, listed, speeds, terms, carried, after)
 
 
 def finish_kernel(pair, near, returned, active_in, own, out, total, active, gate, sem):
@@ -969,16 +979,20 @@
     own, listed = prepare(occupancy, pair, positions, velocity, smoothing, masses)
     arrived = to_peers(listed)
     faces = with_neighbours(own, CELL)
-    rho, first, second, plan = local_density(0, occupancy, send_fill, send_cells[0], own)
+    rho, first, second, speeds, plan = local_density(
+        0, occupancy, send_fill, send_cells[0], pair, own
+    )
+    arrived_speeds = to_peers(speeds)
     rho, back = cross_density(send_fill, plan, own, first, arrived, rho)
     returned = to_peers(back)
     rho = local_density(1, plan, own, first, second, faces, rho)
     density, term, leaving = pressure(pair, rho, returned, energy, own)
-    arrived_moving = to_peers(leaving)
+    arrived_terms = to_peers(leaving)
     face_terms = with_neighbours(term, 1)
     sums = local_force(0, plan, own, first, second, term)
     sums, force_back = cross_force(
-        send_fill, plan, own, first, term, arrived, arrived_moving, sums, face_terms
+        send_fill, plan, own, first, term, arrived, arrived_speeds, arrived_terms, sums,
+        face_terms,
     )
     returned_force = to_peers(force_back)
     sums = local_force(1, plan, own, first, second, term, faces, face_terms, sums)

time: 138 us -> 150 us (1.087); the launches traced: 135 us -> 149 us
  blocking collectives: 0 us -> 16.6 us
  Pallas kernels: 92.1 us -> 87.7 us
  starting transfers between devices: 32.8 us -> 36.4 us
  waiting for transfers between devices: 7.15 us -> 5.18 us
    all_to_all x0 -> x1, blocking collectives: none -> 16.6 us  [to_peers(): return lax.all_to_all(block, 'dev', split_axis=0, concat_axis=0, tiled=True)]
    all_to_all x4, starting transfers between devices: 26.5 us -> 30.1 us  [to_peers(): return lax.all_to_all(block, 'dev', split_axis=0, concat_axis=0, tiled=True)]
    all_to_all x4, waiting for transfers between devices: 7.14 us -> 3.58 us  [to_peers(): return lax.all_to_all(block, 'dev', split_axis=0, concat_axis=0, tiled=True)]
    pallas_call x1, Pallas kernels: 13.3 us -> 10.6 us  [cross_density(): pl.pallas_call(cross_density_kernel, in_specs=[SM, SM] + [VM] * 4, out_sp...]
    pallas_call x1, Pallas kernels: 17.5 us -> 15 us  [cross_force(): pl.pallas_call(cross_force_kernel, in_specs=[SM, SM] + [VM] * 7 + [ANYWHE...]
    ppermute x2, waiting for transfers between devices: 0.01 us -> 1.6 us  [with_neighbours(): lax.ppermute(rows[..., (CELLS - FACE) * size:CELLS * size, :], 'region', up)]
  transfers between devices with their start and end apart: 8 -> 8, of which waited for: 2 -> 2; matrix products, arithmetic and copies ran while one was open for 0% -> 0% of each run, Pallas kernels for 48% -> 38%
where the time goes in v7:
time: 150 us; the launch traced here: 149 us
  Pallas kernels  87.7 us (58%)
  starting transfers between devices  36.4 us (24%)
  blocking collectives  16.6 us (11%)
  waiting for transfers between devices  5.18 us (3%)
  local copies, waits for them, and re-layouts  1.94 us (1%)
    all_to_all x4, starting transfers between devices, to_peers(): return lax.all_to_all(block, 'dev', split_axis=0, concat_axis=0, tiled=True)  30.1 us
    pallas_call x2, Pallas kernels, local_force(): pl.pallas_call(functools.partial(local_force_kernel, part), in_specs=[SM]...  26.9 us
    pallas_call x2, Pallas kernels, local_density(): pl.pallas_call(functools.partial(local_density_kernel, part), in_specs=in...  26 us
    all_to_all x1, blocking collectives, to_peers(): return lax.all_to_all(block, 'dev', split_axis=0, concat_axis=0, tiled=True)  16.6 us
    pallas_call x1, Pallas kernels, cross_force(): pl.pallas_call(cross_force_kernel, in_specs=[SM, SM] + [VM] * 7 + [ANYWHE...  15 us
    pallas_call x1, Pallas kernels, cross_density(): pl.pallas_call(cross_density_kernel, in_specs=[SM, SM] + [VM] * 4, out_sp...  10.6 us
    ppermute x2, starting transfers between devices, with_neighbours(): lax.ppermute(rows[..., :FACE * size, :], 'region', down)  5.23 us
    pallas_call x1, Pallas kernels, prepare(): pl.pallas_call(prepare_kernel, in_specs=[SM] * 2 + [ANYWHERE] * 4, out_sp...  3.66 us
  transfers between devices with their start and end apart: 8, of which 2 were waited for; matrix products, arithmetic and copies ran while one was open for 0% of the time, Pallas kernels for 38%

profile of v7, /device:TPU:0, one launch (start us, length us, event | category | flops | bytes accessed | tf_op | source)
XLA Modules:
  0.0 148.9 jit_solution(16713854278123599714)
XLA Ops:
  0.6 3.7 %shard_map.113 = (f32[2,520,128]{2,1,0:T(8,128)}, f32[16,160,128]{2,1,0:T(8,128)}) custom-call(s32[64]{0:T(128)} %refs_0_.1, s32[16,16]{1,0:T(8,128)} %bitcast.2, f32[3,64,256]{2,1,0:T(8,128)} %pos_in.1, f32[3,64,256]{2,1,0:T(8,128)} %vel_in.1, f32[64,256]{1,0:T(8,128)} %smooth_in.1, f32[64,256]{1,0:T(8,128)} %mass_in.1), custom_call_target="tpu_custom_call" | custom-call | tf_op jit(solution)/shard_map/pallas_call | solution.py:249
  4.3 0.0 copy-start.7
  4.3 0.0 copy-start.8
  4.4 8.1 %all-to-all-start = ((f32[16,160,128]{2,1,0:T(8,128)}), f32[16,160,128]{2,1,0:T(8,128)S(1)}, u32[]{:S(2)}, u32[]{:S(2)}) async-start(f32[16,160,128]{2,1,0:T(8,128)} %get-tuple-element.20), calls=%async_computation | async-start | bytes 2621440 | tf_op jit(solution)/shard_map/all_to_all | solution.py:958
  12.5 16.3 %shard_map.114 = (f32[64,256]{1,0:T(8,128)S(1)}, f32[2,520,128]{2,1,0:T(8,128)S(1)}, f32[2,520,128]{2,1,0:T(8,128)S(1)}, f32[16,96,128]{2,1,0:T(8,128)S(1)}, s32[580]{0:T(1024)S(1)}) custom-call(s32[64]{0:T(128)S(1)} %copy-done.8, s32[1,16]{1,0:T(1,128)S(1)} %copy-done.7, s32[16,16]{1,0:T(8,128)S(1)} %bitcast.6, s32[16,16]{1,0:T(8,128)S(1)} %bitcast.3, ...), custom_call_target="tpu_custom_call" | custom-call | flops 251658240 | bytes 2097152 | tf_op jit(solution)/shard_map/pallas_call | solution.py:483
  28.9 0.9 copy-done.3
  29.7 3.6 %all-to-all-done.listed = f32[16,160,128]{2,1,0:T(8,128)S(1)} async-done(((f32[16,160,128]{2,1,0:T(8,128)}), f32[16,160,128]{2,1,0:T(8,128)S(1)}, u32[]{:S(2)}, u32[]{:S(2)}) %all-to-all-start) | async-done | bytes 1310752 | tf_op jit(solution)/shard_map/all_to_all | solution.py:958
  33.3 10.6 %shard_map.115 = (f32[64,256]{1,0:T(8,128)S(1)}, f32[16,16,256]{2,1,0:T(8,128)S(1)}) custom-call(s32[1,16]{1,0:T(1,128)S(1)} %copy-done.7, s32[580]{0:T(1024)S(1)} %get-tuple-element.17.plan.refs_0_, f32[2,520,128]{2,1,0:T(8,128)S(1)} %copy-done, f32[2,520,128]{2,1,0:T(8,128)S(1)} %get-tuple-element.18.first.refs_2_, ...), custom_call_target="tpu_custom_call" | custom-call | flops 314572800 | bytes 2097152 | tf_op jit(solution)/shard_map/pallas_call | solution.py:549
  43.9 16.6 %all_to_all.25.returned = f32[16,16,256]{2,1,0:T(8,128)S(1)} all-to-all(f32[16,16,256]{2,1,0:T(8,128)S(1)} %get-tuple-element.23), channel_id=1, replica_groups=mesh['region'=8,'dev'=16] {'dev'}, dimensions={0} | all-to-all | bytes 524288 | tf_op jit(solution)/shard_map/all_to_all | solution.py:958
  60.5 3.6 %all-to-all-start.2 = ((f32[16,96,128]{2,1,0:T(8,128)}), f32[16,96,128]{2,1,0:T(8,128)S(1)}, u32[]{:S(2)}, u32[]{:S(2)}) async-start(f32[16,96,128]{2,1,0:T(8,128)} %copy-done.3), calls=%async_computation.2 | async-start | bytes 1572864 | tf_op jit(solution)/shard_map/all_to_all | solution.py:958
  64.2 0.0 collective-permute-start
  64.2 2.9 %collective-permute-start.1 = (f32[2,32,128]{2,1,0:T(8,128)S(1)}, f32[2,32,128]{2,1,0:T(8,128)S(1)}, u32[]{:S(2)}, u32[]{:S(2)}) collective-permute-start(f32[2,32,128]{2,1,0:T(8,128)S(1)} %get-tuple-element.30), channel_id=1, source_target_pairs={{0,112},{16,0},{32,16},{48,32},{64,48},{80,64},{96,80},{112,96},{1... | collective-permute-start | bytes 98312 | tf_op jit(solution)/shard_map/ppermute | solution.py:968
  67.2 1.6 %collective-permute-done = f32[2,32,128]{2,1,0:T(8,128)S(1)} collective-permute-done((f32[2,32,128]{2,1,0:T(8,128)S(1)}, f32[2,32,128]{2,1,0:T(8,128)S(1)}, u32[]{:S(2)}, u32[]{:S(2)}) %collective-permute-start) | collective-permute-done | bytes 32800 | tf_op jit(solution)/shard_map/ppermute | solution.py:967
  68.8 9.6 %shard_map.116.near = f32[64,256]{1,0:T(8,128)S(1)} custom-call(s32[580]{0:T(1024)S(1)} %get-tuple-element.17.plan.refs_0_, f32[2,520,128]{2,1,0:T(8,128)S(1)} %copy-done, f32[2,520,128]{2,1,0:T(8,128)S(1)} %get-tuple-element.18.first.refs_2_, f32[2,520,128]{2,1,0:T(8,128)S(1)} %get-tuple-element.19.refs_3_.second, ...), custom_call_target="tpu_custom_call" | custom-call | flops 251658240 | bytes 2097152 | tf_op jit(solution)/shard_map/pallas_call | solution.py:483
  78.4 3.0 %shard_map.117 = (f32[64,256]{1,0:T(8,128)}, f32[64,256]{1,0:T(8,128)S(1)}, f32[16,16,256]{2,1,0:T(8,128)}) custom-call(s32[16,16]{1,0:T(8,128)S(1)} %bitcast.4, f32[64,256]{1,0:T(8,128)S(1)} %shard_map.116.near, f32[16,16,256]{2,1,0:T(8,128)S(1)} %all_to_all.25.returned, f32[64,256]{1,0:T(8,128)S(1)} %copy-done.5, f32[2,520,128]{2,1,0:T(8,128)S(1)} %copy-done), custom_call_target="tpu_custom_call" | custom-call | tf_op jit(solution)/shard_map/pallas_call | solution.py:598
  81.4 7.0 %all-to-all-start.3 = ((f32[16,16,256]{2,1,0:T(8,128)}), f32[16,16,256]{2,1,0:T(8,128)S(1)}, u32[]{:S(2)}, u32[]{:S(2)}) async-start(f32[16,16,256]{2,1,0:T(8,128)} %get-tuple-element.27), calls=%async_computation.3 | async-start | bytes 524288 | tf_op jit(solution)/shard_map/all_to_all | solution.py:958
  88.4 1.0 collective-permute-start.2
  89.4 2.3 %collective-permute-start.3 = (f32[4,256]{1,0:T(4,128)S(1)}, f32[4,256]{1,0:T(4,128)S(1)}, u32[]{:S(2)}, u32[]{:S(2)}) collective-permute-start(f32[4,256]{1,0:T(4,128)S(1)} %get-tuple-element.33), channel_id=1, source_target_pairs={{0,112},{16,0},{32,16},{48,32},{64,48},{80,64},{96,80},{112,96},{1... | collective-permute-start | bytes 12296 | tf_op jit(solution)/shard_map/ppermute | solution.py:968
  91.7 10.1 %shard_map.118.carried = f32[4,64,256]{2,1,0:T(8,128)S(1)} custom-call(s32[580]{0:T(1024)S(1)} %get-tuple-element.17.plan.refs_0_, f32[2,520,128]{2,1,0:T(8,128)S(1)} %copy-done, f32[2,520,128]{2,1,0:T(8,128)S(1)} %get-tuple-element.18.first.refs_2_, f32[2,520,128]{2,1,0:T(8,128)S(1)} %get-tuple-element.19.refs_3_.second, f32[64,256]{1,0:T(8,128)S(1)} %get-tuple-element.25.term), custom_call_target="tpu_custom_call" | custom-call | flops 335544320 | bytes 2097152 | tf_op jit(solution)/shard_map/pallas_call | solution.py:810
  101.9 15.0 %shard_map.119 = (f32[4,64,256]{2,1,0:T(8,128)S(1)}, f32[16,128,128]{2,1,0:T(8,128)S(1)}) custom-call(s32[1,16]{1,0:T(1,128)S(1)} %copy-done.7, s32[580]{0:T(1024)S(1)} %get-tuple-element.17.plan.refs_0_, f32[2,520,128]{2,1,0:T(8,128)S(1)} %copy-done, f32[2,520,128]{2,1,0:T(8,128)S(1)} %get-tuple-element.18.first.refs_2_, ...), custom_call_target="tpu_custom_call" | custom-call | flops 419430400 | bytes 2097152 | tf_op jit(solution)/shard_map/pallas_call | solution.py:889
  116.9 1.0 copy-done.2
  118.0 11.4 %all-to-all-start.4 = ((f32[16,128,128]{2,1,0:T(8,128)}), f32[16,128,128]{2,1,0:T(8,128)S(1)}, u32[]{:S(2)}, u32[]{:S(2)}) async-start(f32[16,128,128]{2,1,0:T(8,128)} %copy-done.2), calls=%async_computation.4 | async-start | bytes 2097152 | tf_op jit(solution)/shard_map/all_to_all | solution.py:958
  129.4 16.8 %shard_map.120.near = f32[4,64,256]{2,1,0:T(8,128)S(1)} custom-call(s32[580]{0:T(1024)S(1)} %get-tuple-element.17.plan.refs_0_, f32[2,520,128]{2,1,0:T(8,128)S(1)} %copy-done, f32[2,520,128]{2,1,0:T(8,128)S(1)} %get-tuple-element.18.first.refs_2_, f32[2,520,128]{2,1,0:T(8,128)S(1)} %get-tuple-element.19.refs_3_.second, ...), custom_call_target="tpu_custom_call" | custom-call | flops 335544320 | bytes 2097152 | tf_op jit(solution)/shard_map/pallas_call | solution.py:810
  146.2 2.5 %shard_map.121 = f32[4,64,256]{2,1,0:T(8,128)} custom-call(s32[16,16]{1,0:T(8,128)S(1)} %bitcast.5, f32[4,64,256]{2,1,0:T(8,128)S(1)} %shard_map.120.near, f32[16,128,128]{2,1,0:T(8,128)S(1)} %all-to-all-done.4.returned, s32[64,256]{1,0:T(8,128)S(1)} %copy-done.6, f32[2,520,128]{2,1,0:T(8,128)S(1)} %copy-done), custom_call_target="tpu_custom_call" | custom-call | tf_op jit(solution)/shard_map/pallas_call | solution.py:942
  (27 shorter events, 0.1 us)
Async XLA Ops:
  4.3 8.2 %copy-start = (f32[2,520,128]{2,1,0:T(8,128)S(1)}, f32[2,520,128]{2,1,0:T(8,128)}, u32[]{:S(2)}) copy-start(f32[2,520,128]{2,1,0:T(8,128)} %get-tuple-element.16.refs_4_.own.refs_1_) | copy-start | bytes 1597444
  4.3 8.2 %copy-start.4 = (s32[1,16,16]{2,1,0:T(8,128)S(1)}, s32[1,16,16]{2,1,0:T(8,128)}, u32[]{:S(2)}) copy-start(s32[1,16,16]{2,1,0:T(8,128)} %param.19) | copy-start | bytes 3076
  4.3 8.2 %copy-start.7 = (s32[1,16]{1,0:T(1,128)S(1)}, s32[1,16]{1,0:T(1,128)}, u32[]{:S(2)}) copy-start(s32[1,16]{1,0:T(1,128)} %fill.3) | copy-start | bytes 196
  4.3 8.2 %copy-start.8 = (s32[64]{0:T(128)S(1)}, s32[64]{0:T(128)}, u32[]{:S(2)}) copy-start(s32[64]{0:T(128)} %refs_0_.1) | copy-start | bytes 772
  4.3 8.2 %copy-start.9 = (s32[1,16,16]{2,1,0:T(8,128)S(1)}, s32[1,16,16]{2,1,0:T(8,128)}, u32[]{:S(2)}) copy-start(s32[1,16,16]{2,1,0:T(8,128)} %param.17) | copy-start | bytes 3076
  4.4 28.9 %all-to-all-start = ((f32[16,160,128]{2,1,0:T(8,128)}), f32[16,160,128]{2,1,0:T(8,128)S(1)}, u32[]{:S(2)}, u32[]{:S(2)}) async-start(f32[16,160,128]{2,1,0:T(8,128)} %get-tuple-element.20), calls=%async_computation | async-start | bytes 2621440 | tf_op jit(solution)/shard_map/all_to_all | solution.py:958
  28.8 0.9 copy-start.3
  33.3 27.3 %copy-start.1 = (f32[16,160,128]{2,1,0:T(8,128)}, f32[16,160,128]{2,1,0:T(8,128)S(1)}, u32[]{:S(2)}) copy-start(f32[16,160,128]{2,1,0:T(8,128)S(1)} %all-to-all-done.listed) | copy-start | bytes 3932164
  60.5 20.9 %all-to-all-start.2 = ((f32[16,96,128]{2,1,0:T(8,128)}), f32[16,96,128]{2,1,0:T(8,128)S(1)}, u32[]{:S(2)}, u32[]{:S(2)}) async-start(f32[16,96,128]{2,1,0:T(8,128)} %copy-done.3), calls=%async_computation.2 | async-start | bytes 1572864 | tf_op jit(solution)/shard_map/all_to_all | solution.py:958
  64.2 14.2 %copy-start.5 = (f32[64,256]{1,0:T(8,128)S(1)}, f32[64,256]{1,0:T(8,128)}, u32[]{:S(2)}) copy-start(f32[64,256]{1,0:T(8,128)} %energy_in.1) | copy-start | bytes 196612
  64.2 4.6 %collective-permute-start = (f32[2,32,128]{2,1,0:T(8,128)S(1)}, f32[2,32,128]{2,1,0:T(8,128)S(1)}, u32[]{:S(2)}, u32[]{:S(2)}) collective-permute-start(f32[2,32,128]{2,1,0:T(8,128)S(1)} %get-tuple-element.31), channel_id=1, source_target_pairs={{0,16},{16,32},{32,48},{48,64},{64,80},{80,96},{96,112},{112,0},{1... | collective-permute-start | bytes 98312 | tf_op jit(solution)/shard_map/ppermute | solution.py:967
  64.2 4.5 %collective-permute-start.1 = (f32[2,32,128]{2,1,0:T(8,128)S(1)}, f32[2,32,128]{2,1,0:T(8,128)S(1)}, u32[]{:S(2)}, u32[]{:S(2)}) collective-permute-start(f32[2,32,128]{2,1,0:T(8,128)S(1)} %get-tuple-element.30), channel_id=1, source_target_pairs={{0,112},{16,0},{32,16},{48,32},{64,48},{80,64},{96,80},{112,96},{1... | collective-permute-start | bytes 98312 | tf_op jit(solution)/shard_map/ppermute | solution.py:968
  81.4 20.5 %all-to-all-start.3 = ((f32[16,16,256]{2,1,0:T(8,128)}), f32[16,16,256]{2,1,0:T(8,128)S(1)}, u32[]{:S(2)}, u32[]{:S(2)}) async-start(f32[16,16,256]{2,1,0:T(8,128)} %get-tuple-element.27), calls=%async_computation.3 | async-start | bytes 524288 | tf_op jit(solution)/shard_map/all_to_all | solution.py:958
  88.4 13.4 %collective-permute-start.2 = (f32[4,256]{1,0:T(4,128)S(1)}, f32[4,256]{1,0:T(4,128)S(1)}, u32[]{:S(2)}, u32[]{:S(2)}) collective-permute-start(f32[4,256]{1,0:T(4,128)S(1)} %get-tuple-element.32), channel_id=1, source_target_pairs={{0,16},{16,32},{32,48},{48,64},{64,80},{80,96},{96,112},{112,0},{1... | collective-permute-start | bytes 12296 | tf_op jit(solution)/shard_map/ppermute | solution.py:967
  89.4 12.5 %collective-permute-start.3 = (f32[4,256]{1,0:T(4,128)S(1)}, f32[4,256]{1,0:T(4,128)S(1)}, u32[]{:S(2)}, u32[]{:S(2)}) collective-permute-start(f32[4,256]{1,0:T(4,128)S(1)} %get-tuple-element.33), channel_id=1, source_target_pairs={{0,112},{16,0},{32,16},{48,32},{64,48},{80,64},{96,80},{112,96},{1... | collective-permute-start | bytes 12296 | tf_op jit(solution)/shard_map/ppermute | solution.py:968
  116.9 1.0 copy-start.2
  118.0 28.2 %all-to-all-start.4 = ((f32[16,128,128]{2,1,0:T(8,128)}), f32[16,128,128]{2,1,0:T(8,128)S(1)}, u32[]{:S(2)}, u32[]{:S(2)}) async-start(f32[16,128,128]{2,1,0:T(8,128)} %copy-done.2), calls=%async_computation.4 | async-start | bytes 2097152 | tf_op jit(solution)/shard_map/all_to_all | solution.py:958
  129.4 16.8 %copy-start.6 = (s32[64,256]{1,0:T(8,128)S(1)}, s32[64,256]{1,0:T(8,128)}, u32[]{:S(2)}) copy-start(s32[64,256]{1,0:T(8,128)} %active_in.1) | copy-start | bytes 196612

commit v8 on v6

--- a/solution.py
+++ b/solution.py
@@ -30,14 +30,14 @@
 SM = pl.BlockSpec(memory_space=pltpu.SMEM)
 ROWS = 5
 MOVING = 4
-SPLIT = 40
+SPLITS = (44, 40)
 SIZES = (160, 192, 224, 256)
 KINDS = len(SIZES)
 UNIT = 4
-LOCAL_AT = 16
+LOCAL_AT = 5 * KINDS
 LOCAL_LEAD = 2
 LOCAL_LIST = CELLS + 8
-CROSS_AT = LOCAL_AT + 2 * LOCAL_LIST
+CROSS_AT = LOCAL_AT + 4 * LOCAL_LIST
 CROSS_LEAD = 4
 CROSS_LIST = LISTED + 16
 PLAN = CROSS_AT + CROSS_LIST
@@ -270,10 +270,11 @@
 
 
 def make_plan(occ, fill, cells, plan):
-    def over_local(visit, part, carry):
-        low, high = (SPLIT, CELLS) if part else (0, SPLIT)
+    def over_local(visit, group, carry):
+        split = SPLITS[group // 2]
+        low, high = (split, CELLS) if group % 2 else (0, split)
         step = lambda c, carry: visit(kind_of(occ[c]), c, carry)
-        return lax.fori_loop(low, high, step, carry, unroll=8)
+        return lax.fori_loop(low, high, step, carry, unroll=4)
 
     def over_pairs(visit, carry):
         def peer_step(e, carry):
@@ -292,13 +293,15 @@
     def one_of(kind):
         return jnp.left_shift(jnp.int32(1), 8 * kind)
 
-    for group, (walk, start, lead, unit, blank) in enumerate(
-        [
-            (lambda v, x: over_local(v, 0, x), LOCAL_AT, LOCAL_LEAD, 2, CELLS),
-            (lambda v, x: over_local(v, 1, x), LOCAL_AT + LOCAL_LIST, LOCAL_LEAD, 2, CELLS),
-            (over_pairs, CROSS_AT, CROSS_LEAD, UNIT, unused * PACK + CELLS),
-        ]
-    ):
+    groups = [
+        (
+            functools.partial(lambda g, v, x: over_local(v, g, x), g),
+            LOCAL_AT + g * LOCAL_LIST, LOCAL_LEAD, 2, CELLS,
+        )
+        for g in range(4)
+    ]
+    groups.append((over_pairs, CROSS_AT, CROSS_LEAD, UNIT, unused * PACK + CELLS))
+    for group, (walk, start, lead, unit, blank) in enumerate(groups):
         counts = walk(lambda kind, value, packed: packed + one_of(kind), jnp.int32(0))
         total = jnp.int32(0)
         done = jnp.int32(0)
@@ -354,9 +357,9 @@
         base = base + count
 
 
-def cell_list(plan, part):
-    start = LOCAL_AT + part * LOCAL_LIST + LOCAL_LEAD
-    return [plan[part * KINDS + k] for k in range(KINDS)], lambda n: plan[start + n]
+def cell_list(plan, group):
+    start = LOCAL_AT + group * LOCAL_LIST + LOCAL_LEAD
+    return [plan[group * KINDS + k] for k in range(KINDS)], lambda n: plan[start + n]
 
 
 def pair_list(plan):
@@ -366,7 +369,7 @@
         entries = [plan[start + 2 * n + k] for k in range(2)]
         return [(entry >> 7, entry & (PACK - 1)) for entry in entries]
 
-    return [plan[2 * KINDS + k] for k in range(KINDS)], item
+    return [plan[4 * KINDS + k] for k in range(KINDS)], item
 
 
 def live_parts(fill, visit, other):
@@ -548,20 +551,26 @@
 
 
 def pressure_kernel(
-    pair, near, returned, energy_in, own, density, term, out, energy, sum_of, moving, sem
+    pair, near, returned, energy_in, own, density, term, out, energy, moving, sem, *sums
 ):
     copies = fetch([(energy_in, energy)], sem)
-    sum_of[...] = near[...]
-
-    def peer_step(e, _):
+    for ref in sums:
+        ref[...] = jnp.zeros_like(ref)
+
+    def peer_step(i, _):
         for s in range(SLOTS):
-            sum_of[pl.ds(pair[e, s], 1), :] += returned[e, s : s + 1]
+            for j in range(2):
+                at = pl.ds(pair[2 * i + j, s], 1)
+                row = returned[2 * i + j, s : s + 1]
+                for h in range(2):
+                    sums[2 * j + h][at, :] += half(row, h)
         return 0
 
-    lax.fori_loop(0, PEERS, peer_step, 0)
+    lax.fori_loop(0, PEERS // 2, peer_step, 0)
     copies[0].wait()
+    sum_of = near[...] + both(lambda h: sums[h][...] + sums[2 + h][...])
     full = planes_of(own, [4], 0, CELLS, CELL)[0] > 0.0
-    rho = jnp.where(full, sum_of[...], 0.0)
+    rho = jnp.where(full, sum_of, 0.0)
     density[...] = rho
     term[...] = jnp.where(full, GAMMA_LESS * energy[...] / jnp.where(full, rho, 1.0), 0.0)
 
@@ -597,10 +606,10 @@
         ],
         scratch_shapes=[
             pltpu.VMEM((CELLS, WIDTH), F32),
-            pltpu.VMEM((CELLS, WIDTH), F32),
             pltpu.VMEM((CELLS, MOVING, WIDTH), F32),
             pltpu.SemaphoreType.DMA((1,)),
-        ],
+        ]
+        + [pltpu.VMEM((CELLS, 128), F32)] * 4,
         compiler_params=params(),
     )(pair, near, returned, energy, own)
 
@@ -742,7 +751,7 @@
         add_block(total, c, SUMS, to_seconds(mine, count, *held[2:4]) + added)
         add_block(total, after, SUMS, to_seconds(mine, count, *held[5:7]))
 
-    trips, item = cell_list(plan, part)
+    trips, item = cell_list(plan, 2 + part)
     in_three_turns(trips, SIZES, item, None, products, tiles, sums, slot_a, slot_b, 1)
 
     if part:
@@ -899,21 +908,21 @@
     )(fill, plan, own, first, term, listed, arrived, carried, after)
 
 
-def finish_kernel(pair, near, returned, active_in, own, out, total, active, gate, sem):
+def finish_kernel(pair, near, returned, active_in, own, out, active, gate, sem, *sums):
     copies = fetch([(active_in, active)], sem)
-    total[...] = jnp.zeros_like(total)
-
-    def peer_step(e, _):
+    for ref in sums:
+        ref[...] = jnp.zeros_like(ref)
+
+    def peer_step(i, _):
         for s in range(SLOTS):
-            at = s * MOVING
-            total[pair[e, s]] += both(
-                lambda h: returned[
-                    e, h * SLOTS * MOVING + at : h * SLOTS * MOVING + at + MOVING
-                ]
-            )
+            for j in range(2):
+                c = pair[2 * i + j, s]
+                for h in range(2):
+                    at = (h * SLOTS + s) * MOVING
+                    sums[2 * j + h][c] += returned[2 * i + j, at : at + MOVING]
         return 0
 
-    lax.fori_loop(0, PEERS, peer_step, 0)
+    lax.fori_loop(0, PEERS // 2, peer_step, 0)
     copies[0].wait()
     full = planes_of(own, [4], 0, CELLS, CELL)[0] > 0.0
     gate[...] = jnp.where(full, active[...].astype(F32), 0.0)
@@ -921,8 +930,9 @@
     def cell_step(c, _):
         one = pl.ds(c, 1)
         open_to = gate[one, :]
+        total = both(lambda h: sums[h][c] + sums[2 + h][c])
         for k in range(4):
-            out[k, one, :] = (near[k, one, :] + total[c, k : k + 1]) * open_to
+            out[k, one, :] = (near[k, one, :] + total[k : k + 1]) * open_to
         return 0
 
     lax.fori_loop(0, CELLS, cell_step, 0, unroll=8)
@@ -935,11 +945,11 @@
         out_specs=VM,
         out_shape=jax.ShapeDtypeStruct((4, CELLS, WIDTH), F32),
         scratch_shapes=[
-            pltpu.VMEM((CELLS, 4, WIDTH), F32),
             pltpu.VMEM((CELLS, WIDTH), jnp.int32),
             pltpu.VMEM((CELLS, WIDTH), F32),
             pltpu.SemaphoreType.DMA((1,)),
-        ],
+        ]
+        + [pltpu.VMEM((CELLS, MOVING, 128), F32)] * 4,
         compiler_params=params(),
     )(pair, near, returned, active, own)
 

time: 138 us -> 139 us (level); the launches traced: 135 us -> 138 us
  starting transfers between devices: 32.8 us -> 36.3 us
  waiting for transfers between devices: 7.15 us -> 5.3 us
  Pallas kernels: 92.1 us -> 93.6 us
    all_to_all x4, starting transfers between devices: 26.5 us -> 31.1 us  [to_peers(): return lax.all_to_all(block, 'dev', split_axis=0, concat_axis=0, tiled=True)]
    all_to_all x4, waiting for transfers between devices: 7.14 us -> 5.29 us  [to_peers(): return lax.all_to_all(block, 'dev', split_axis=0, concat_axis=0, tiled=True)]
  transfers between devices with their start and end apart: 8 -> 8, of which waited for: 2 -> 3; matrix products, arithmetic and copies ran while one was open for 0% -> 0% of each run, Pallas kernels for 48% -> 49%
where the time goes in v8:
time: 139 us; the launch traced here: 138 us
  Pallas kernels  93.6 us (67%)
  starting transfers between devices  36.3 us (26%)
  waiting for transfers between devices  5.3 us (4%)
  local copies, waits for them, and re-layouts  2.04 us (1%)
    all_to_all x4, starting transfers between devices, to_peers(): return lax.all_to_all(block, 'dev', split_axis=0, concat_axis=0, tiled=True)  31.1 us
    pallas_call x2, Pallas kernels, local_force(): pl.pallas_call(functools.partial(local_force_kernel, part), in_specs=[SM]...  27.5 us
    pallas_call x2, Pallas kernels, local_density(): pl.pallas_call(functools.partial(local_density_kernel, part), in_specs=in...  26.1 us
    pallas_call x1, Pallas kernels, cross_force(): pl.pallas_call(cross_force_kernel, in_specs=[SM, SM] + [VM] * 6 + [ANYWHE...  17.7 us
    pallas_call x1, Pallas kernels, cross_density(): pl.pallas_call(cross_density_kernel, in_specs=[SM, SM] + [VM] * 4, out_sp...  13.6 us
    all_to_all x4, waiting for transfers between devices, to_peers(): return lax.all_to_all(block, 'dev', split_axis=0, concat_axis=0, tiled=True)  5.29 us
    ppermute x2, starting transfers between devices, with_neighbours(): lax.ppermute(rows[..., :FACE * size, :], 'region', down)  5.13 us
    pallas_call x1, Pallas kernels, prepare(): pl.pallas_call(prepare_kernel, in_specs=[SM] * 2 + [ANYWHERE] * 4, out_sp...  3.66 us
  transfers between devices with their start and end apart: 8, of which 3 were waited for; matrix products, arithmetic and copies ran while one was open for 0% of the time, Pallas kernels for 49%

profile of v8, /device:TPU:0, one launch (start us, length us, event | category | flops | bytes accessed | tf_op | source)
XLA Modules:
  0.0 138.3 jit_solution(1119150970917615996)
XLA Ops:
  0.6 3.7 %shard_map.113 = (f32[2,520,128]{2,1,0:T(8,128)}, f32[16,160,128]{2,1,0:T(8,128)}) custom-call(s32[64]{0:T(128)} %refs_0_.1, s32[16,16]{1,0:T(8,128)} %bitcast.2, f32[3,64,256]{2,1,0:T(8,128)} %pos_in.1, f32[3,64,256]{2,1,0:T(8,128)} %vel_in.1, f32[64,256]{1,0:T(8,128)} %smooth_in.1, f32[64,256]{1,0:T(8,128)} %mass_in.1), custom_call_target="tpu_custom_call" | custom-call | tf_op jit(solution)/shard_map/pallas_call | solution.py:248
  4.3 0.0 copy-start.7
  4.3 0.0 copy-start.8
  4.3 0.0 copy-start.9
  4.3 8.1 %all-to-all-start = ((f32[16,160,128]{2,1,0:T(8,128)}), f32[16,160,128]{2,1,0:T(8,128)S(1)}, u32[]{:S(2)}, u32[]{:S(2)}) async-start(f32[16,160,128]{2,1,0:T(8,128)} %get-tuple-element.19), calls=%async_computation | async-start | bytes 2621440 | tf_op jit(solution)/shard_map/all_to_all | solution.py:958
  12.5 2.2 %collective-permute-start.1 = (f32[2,32,128]{2,1,0:T(8,128)S(1)}, f32[2,32,128]{2,1,0:T(8,128)S(1)}, u32[]{:S(2)}, u32[]{:S(2)}) collective-permute-start(f32[2,32,128]{2,1,0:T(8,128)S(1)} %get-tuple-element.28), channel_id=1, source_target_pairs={{0,112},{16,0},{32,16},{48,32},{64,48},{80,64},{96,80},{112,96},{1... | collective-permute-start | bytes 98312 | tf_op jit(solution)/shard_map/ppermute | solution.py:968
  14.7 17.5 %shard_map.114 = (f32[64,256]{1,0:T(8,128)S(1)}, f32[2,520,128]{2,1,0:T(8,128)S(1)}, f32[2,520,128]{2,1,0:T(8,128)S(1)}, s32[580]{0:T(1024)S(1)}) custom-call(s32[64]{0:T(128)S(1)} %copy-done.8, s32[1,16]{1,0:T(1,128)S(1)} %copy-done.7, s32[16,16]{1,0:T(8,128)S(1)} %bitcast.5, f32[2,520,128]{2,1,0:T(8,128)S(1)} %copy-done), custom_call_target="tpu_custom_call" | custom-call | flops 251658240 | bytes 2097152 | tf_op jit(solution)/shard_map/pallas_call | solution.py:466
  32.1 1.1 all-to-all-done.listed
  33.3 13.6 %shard_map.115 = (f32[64,256]{1,0:T(8,128)S(1)}, f32[16,16,256]{2,1,0:T(8,128)}) custom-call(s32[1,16]{1,0:T(1,128)S(1)} %copy-done.7, s32[580]{0:T(1024)S(1)} %get-tuple-element.16.plan.refs_0_, f32[2,520,128]{2,1,0:T(8,128)S(1)} %copy-done, f32[2,520,128]{2,1,0:T(8,128)S(1)} %get-tuple-element.17.first.refs_2_, f32[16,160,128]{2,1,0:T(8,128)S(1)} %all-to-all-done.listed, ...), custom_call_target="tpu_custom_call" | custom-call | flops 314572800 | bytes 2097152 | tf_op jit(solution)/shard_map/pallas_call | solution.py:532
  46.8 7.5 %all-to-all-start.1 = ((f32[16,16,256]{2,1,0:T(8,128)}), f32[16,16,256]{2,1,0:T(8,128)S(1)}, u32[]{:S(2)}, u32[]{:S(2)}) async-start(f32[16,16,256]{2,1,0:T(8,128)} %get-tuple-element.22), calls=%async_computation.1 | async-start | bytes 524288 | tf_op jit(solution)/shard_map/all_to_all | solution.py:958
  54.4 8.6 %shard_map.116.near = f32[64,256]{1,0:T(8,128)S(1)} custom-call(s32[580]{0:T(1024)S(1)} %get-tuple-element.16.plan.refs_0_, f32[2,520,128]{2,1,0:T(8,128)S(1)} %copy-done, f32[2,520,128]{2,1,0:T(8,128)S(1)} %get-tuple-element.17.first.refs_2_, f32[2,520,128]{2,1,0:T(8,128)S(1)} %get-tuple-element.18.refs_3_.second, ...), custom_call_target="tpu_custom_call" | custom-call | flops 251658240 | bytes 2097152 | tf_op jit(solution)/shard_map/pallas_call | solution.py:466
  63.0 0.3 all-to-all-done.1.returned
  63.3 2.7 %shard_map.117 = (f32[64,256]{1,0:T(8,128)}, f32[64,256]{1,0:T(8,128)S(1)}, f32[16,128,128]{2,1,0:T(8,128)S(1)}) custom-call(s32[16,16]{1,0:T(8,128)S(1)} %bitcast.3, f32[64,256]{1,0:T(8,128)S(1)} %shard_map.116.near, f32[16,16,256]{2,1,0:T(8,128)S(1)} %all-to-all-done.1.returned, f32[64,256]{1,0:T(8,128)S(1)} %copy-done.5, f32[2,520,128]{2,1,0:T(8,128)S(1)} %copy-done), custom_call_target="tpu_custom_call" | custom-call | tf_op jit(solution)/shard_map/pallas_call | solution.py:598
  66.0 1.0 copy-done.2
  66.9 6.9 %all-to-all-start.2 = ((f32[16,128,128]{2,1,0:T(8,128)}), f32[16,128,128]{2,1,0:T(8,128)S(1)}, u32[]{:S(2)}, u32[]{:S(2)}) async-start(f32[16,128,128]{2,1,0:T(8,128)} %copy-done.2), calls=%async_computation.2 | async-start | bytes 2097152 | tf_op jit(solution)/shard_map/all_to_all | solution.py:958
  73.8 0.0 collective-permute-start.2
  73.9 2.9 %collective-permute-start.3 = (f32[4,256]{1,0:T(4,128)S(1)}, f32[4,256]{1,0:T(4,128)S(1)}, u32[]{:S(2)}, u32[]{:S(2)}) collective-permute-start(f32[4,256]{1,0:T(4,128)S(1)} %get-tuple-element.31), channel_id=1, source_target_pairs={{0,112},{16,0},{32,16},{48,32},{64,48},{80,64},{96,80},{112,96},{1... | collective-permute-start | bytes 12296 | tf_op jit(solution)/shard_map/ppermute | solution.py:968
  76.8 15.5 %shard_map.118.carried = f32[4,64,256]{2,1,0:T(8,128)S(1)} custom-call(s32[580]{0:T(1024)S(1)} %get-tuple-element.16.plan.refs_0_, f32[2,520,128]{2,1,0:T(8,128)S(1)} %copy-done, f32[2,520,128]{2,1,0:T(8,128)S(1)} %get-tuple-element.17.first.refs_2_, f32[2,520,128]{2,1,0:T(8,128)S(1)} %get-tuple-element.18.refs_3_.second, f32[64,256]{1,0:T(8,128)S(1)} %get-tuple-element.24.term), custom_call_target="tpu_custom_call" | custom-call | flops 335544320 | bytes 2097152 | tf_op jit(solution)/shard_map/pallas_call | solution.py:811
  92.4 17.7 %shard_map.119 = (f32[4,64,256]{2,1,0:T(8,128)S(1)}, f32[16,128,128]{2,1,0:T(8,128)S(1)}) custom-call(s32[1,16]{1,0:T(1,128)S(1)} %copy-done.7, s32[580]{0:T(1024)S(1)} %get-tuple-element.16.plan.refs_0_, f32[2,520,128]{2,1,0:T(8,128)S(1)} %copy-done, f32[2,520,128]{2,1,0:T(8,128)S(1)} %get-tuple-element.17.first.refs_2_, ...), custom_call_target="tpu_custom_call" | custom-call | flops 419430400 | bytes 2097152 | tf_op jit(solution)/shard_map/pallas_call | solution.py:888
  110.0 1.0 copy-done.3
  111.0 8.7 %all-to-all-start.3 = ((f32[16,128,128]{2,1,0:T(8,128)}), f32[16,128,128]{2,1,0:T(8,128)S(1)}, u32[]{:S(2)}, u32[]{:S(2)}) async-start(f32[16,128,128]{2,1,0:T(8,128)} %copy-done.3), calls=%async_computation.3 | async-start | bytes 2097152 | tf_op jit(solution)/shard_map/all_to_all | solution.py:958
  119.7 12.0 %shard_map.120.near = f32[4,64,256]{2,1,0:T(8,128)S(1)} custom-call(s32[580]{0:T(1024)S(1)} %get-tuple-element.16.plan.refs_0_, f32[2,520,128]{2,1,0:T(8,128)S(1)} %copy-done, f32[2,520,128]{2,1,0:T(8,128)S(1)} %get-tuple-element.17.first.refs_2_, f32[2,520,128]{2,1,0:T(8,128)S(1)} %get-tuple-element.18.refs_3_.second, ...), custom_call_target="tpu_custom_call" | custom-call | flops 335544320 | bytes 2097152 | tf_op jit(solution)/shard_map/pallas_call | solution.py:811
  131.7 3.9 %all-to-all-done.3.returned = f32[16,128,128]{2,1,0:T(8,128)S(1)} async-done(((f32[16,128,128]{2,1,0:T(8,128)}), f32[16,128,128]{2,1,0:T(8,128)S(1)}, u32[]{:S(2)}, u32[]{:S(2)}) %all-to-all-start.3) | async-done | bytes 1048608 | tf_op jit(solution)/shard_map/all_to_all | solution.py:958
  135.6 2.5 %shard_map.121 = f32[4,64,256]{2,1,0:T(8,128)} custom-call(s32[16,16]{1,0:T(8,128)S(1)} %bitcast.4, f32[4,64,256]{2,1,0:T(8,128)S(1)} %shard_map.120.near, f32[16,128,128]{2,1,0:T(8,128)S(1)} %all-to-all-done.3.returned, s32[64,256]{1,0:T(8,128)S(1)} %copy-done.6, f32[2,520,128]{2,1,0:T(8,128)S(1)} %copy-done), custom_call_target="tpu_custom_call" | custom-call | tf_op jit(solution)/shard_map/pallas_call | solution.py:942
  (26 shorter events, 0.1 us)
Async XLA Ops:
  4.3 8.2 %copy-start = (f32[2,520,128]{2,1,0:T(8,128)S(1)}, f32[2,520,128]{2,1,0:T(8,128)}, u32[]{:S(2)}) copy-start(f32[2,520,128]{2,1,0:T(8,128)} %get-tuple-element.15.refs_3_.own.refs_1_) | copy-start | bytes 1597444
  4.3 10.4 %copy-start.7 = (s32[1,16]{1,0:T(1,128)S(1)}, s32[1,16]{1,0:T(1,128)}, u32[]{:S(2)}) copy-start(s32[1,16]{1,0:T(1,128)} %fill.3) | copy-start | bytes 196
  4.3 10.4 %copy-start.8 = (s32[64]{0:T(128)S(1)}, s32[64]{0:T(128)}, u32[]{:S(2)}) copy-start(s32[64]{0:T(128)} %refs_0_.1) | copy-start | bytes 772
  4.3 10.3 %copy-start.9 = (s32[1,16,16]{2,1,0:T(8,128)S(1)}, s32[1,16,16]{2,1,0:T(8,128)}, u32[]{:S(2)}) copy-start(s32[1,16,16]{2,1,0:T(8,128)} %param.17) | copy-start | bytes 3076
  4.3 28.9 %all-to-all-start = ((f32[16,160,128]{2,1,0:T(8,128)}), f32[16,160,128]{2,1,0:T(8,128)S(1)}, u32[]{:S(2)}, u32[]{:S(2)}) async-start(f32[16,160,128]{2,1,0:T(8,128)} %get-tuple-element.19), calls=%async_computation | async-start | bytes 2621440 | tf_op jit(solution)/shard_map/all_to_all | solution.py:958
  12.5 41.9 %collective-permute-start.1 = (f32[2,32,128]{2,1,0:T(8,128)S(1)}, f32[2,32,128]{2,1,0:T(8,128)S(1)}, u32[]{:S(2)}, u32[]{:S(2)}) collective-permute-start(f32[2,32,128]{2,1,0:T(8,128)S(1)} %get-tuple-element.28), channel_id=1, source_target_pairs={{0,112},{16,0},{32,16},{48,32},{64,48},{80,64},{96,80},{112,96},{1... | collective-permute-start | bytes 98312 | tf_op jit(solution)/shard_map/ppermute | solution.py:968
  14.7 39.7 %collective-permute-start = (f32[2,32,128]{2,1,0:T(8,128)S(1)}, f32[2,32,128]{2,1,0:T(8,128)S(1)}, u32[]{:S(2)}, u32[]{:S(2)}) collective-permute-start(f32[2,32,128]{2,1,0:T(8,128)S(1)} %get-tuple-element.29), channel_id=1, source_target_pairs={{0,16},{16,32},{32,48},{48,64},{64,80},{80,96},{96,112},{112,0},{1... | collective-permute-start | bytes 98312 | tf_op jit(solution)/shard_map/ppermute | solution.py:967
  33.3 13.6 %copy-start.1 = (f32[16,160,128]{2,1,0:T(8,128)}, f32[16,160,128]{2,1,0:T(8,128)S(1)}, u32[]{:S(2)}) copy-start(f32[16,160,128]{2,1,0:T(8,128)S(1)} %all-to-all-done.listed) | copy-start | bytes 3932164
  46.8 16.4 %copy-start.4 = (s32[1,16,16]{2,1,0:T(8,128)S(1)}, s32[1,16,16]{2,1,0:T(8,128)}, u32[]{:S(2)}) copy-start(s32[1,16,16]{2,1,0:T(8,128)} %param.19) | copy-start | bytes 3076
  46.8 16.4 %copy-start.5 = (f32[64,256]{1,0:T(8,128)S(1)}, f32[64,256]{1,0:T(8,128)}, u32[]{:S(2)}) copy-start(f32[64,256]{1,0:T(8,128)} %energy_in.1) | copy-start | bytes 196612
  46.8 16.4 %all-to-all-start.1 = ((f32[16,16,256]{2,1,0:T(8,128)}), f32[16,16,256]{2,1,0:T(8,128)S(1)}, u32[]{:S(2)}, u32[]{:S(2)}) async-start(f32[16,16,256]{2,1,0:T(8,128)} %get-tuple-element.22), calls=%async_computation.1 | async-start | bytes 524288 | tf_op jit(solution)/shard_map/all_to_all | solution.py:958
  66.0 1.0 copy-start.2
  66.9 25.4 %all-to-all-start.2 = ((f32[16,128,128]{2,1,0:T(8,128)}), f32[16,128,128]{2,1,0:T(8,128)S(1)}, u32[]{:S(2)}, u32[]{:S(2)}) async-start(f32[16,128,128]{2,1,0:T(8,128)} %copy-done.2), calls=%async_computation.2 | async-start | bytes 2097152 | tf_op jit(solution)/shard_map/all_to_all | solution.py:958
  73.8 18.5 %collective-permute-start.2 = (f32[4,256]{1,0:T(4,128)S(1)}, f32[4,256]{1,0:T(4,128)S(1)}, u32[]{:S(2)}, u32[]{:S(2)}) collective-permute-start(f32[4,256]{1,0:T(4,128)S(1)} %get-tuple-element.30), channel_id=1, source_target_pairs={{0,16},{16,32},{32,48},{48,64},{64,80},{80,96},{96,112},{112,0},{1... | collective-permute-start | bytes 12296 | tf_op jit(solution)/shard_map/ppermute | solution.py:967
  73.9 18.5 %collective-permute-start.3 = (f32[4,256]{1,0:T(4,128)S(1)}, f32[4,256]{1,0:T(4,128)S(1)}, u32[]{:S(2)}, u32[]{:S(2)}) collective-permute-start(f32[4,256]{1,0:T(4,128)S(1)} %get-tuple-element.31), channel_id=1, source_target_pairs={{0,112},{16,0},{32,16},{48,32},{64,48},{80,64},{96,80},{112,96},{1... | collective-permute-start | bytes 12296 | tf_op jit(solution)/shard_map/ppermute | solution.py:968
  110.0 1.0 copy-start.3
  111.0 24.5 %all-to-all-start.3 = ((f32[16,128,128]{2,1,0:T(8,128)}), f32[16,128,128]{2,1,0:T(8,128)S(1)}, u32[]{:S(2)}, u32[]{:S(2)}) async-start(f32[16,128,128]{2,1,0:T(8,128)} %copy-done.3), calls=%async_computation.3 | async-start | bytes 2097152 | tf_op jit(solution)/shard_map/all_to_all | solution.py:958
  119.7 15.8 %copy-start.6 = (s32[64,256]{1,0:T(8,128)S(1)}, s32[64,256]{1,0:T(8,128)}, u32[]{:S(2)}) copy-start(s32[64,256]{1,0:T(8,128)} %active_in.1) | copy-start | bytes 196612

commit v9 on v8

--- a/solution.py
+++ b/solution.py
@@ -36,7 +36,7 @@
 UNIT = 4
 LOCAL_AT = 5 * KINDS
 LOCAL_LEAD = 2
-LOCAL_LIST = CELLS + 8
+LOCAL_LIST = CELLS + 16
 CROSS_AT = LOCAL_AT + 4 * LOCAL_LIST
 CROSS_LEAD = 4
 CROSS_LIST = LISTED + 16
@@ -314,7 +314,7 @@
             done = upto
         for k in range(lead):
             plan[start + k] = blank
-        for k in range(unit + 1):
+        for k in range(unit + 5):
             plan[start + lead + total + k] = blank
 
         def place(kind, value, packed, start=start + lead):
@@ -340,36 +340,49 @@
     return jnp.where(n < FACE, n, CELLS - 2 * FACE + n)
 
 
-def in_turns(trips, sizes, item, last, products, weights, slot_a, slot_b):
-    products(item(0), slot_a)
+def in_turns(trips, sizes, item, products, weights, slot_a, slot_b):
+    read, decode = item
+    products(decode(read(0)), slot_a)
     base = 0
+    held = tuple(read(n) for n in range(3))
     for count, size in zip(trips, sizes):
 
-        def step(i, _, size=size):
-            products(item(2 * i + 1), slot_b)
-            weights(size, item(2 * i), slot_a)
-            after = 2 * i + 2
-            products(item(after if last is None else jnp.minimum(after, last - 1)), slot_a)
-            weights(size, item(2 * i + 1), slot_b)
-            return 0
-
-        lax.fori_loop(base, base + count, step, 0)
+        def step(i, held, size=size):
+            ahead = (read(2 * i + 3), read(2 * i + 4))
+            now, then, after = [decode(entry) for entry in held]
+            products(then, slot_b)
+            weights(size, now, slot_a)
+            products(after, slot_a)
+            weights(size, then, slot_b)
+            return held[2:] + ahead
+
+        held = lax.fori_loop(base, base + count, step, held)
         base = base + count
 
 
 def cell_list(plan, group):
     start = LOCAL_AT + group * LOCAL_LIST + LOCAL_LEAD
-    return [plan[group * KINDS + k] for k in range(KINDS)], lambda n: plan[start + n]
+    trips = [plan[group * KINDS + k] for k in range(KINDS)]
+    return trips, (lambda n: plan[start + n], lambda entry: entry)
 
 
 def pair_list(plan):
     start = CROSS_AT + CROSS_LEAD
 
-    def item(n):
-        entries = [plan[start + 2 * n + k] for k in range(2)]
+    def read(n):
+        return tuple(plan[start + 2 * n + k] for k in range(2))
+
+    def decode(entries):
         return [(entry >> 7, entry & (PACK - 1)) for entry in entries]
 
-    return [plan[4 * KINDS + k] for k in range(KINDS)], item
+    return [plan[4 * KINDS + k] for k in range(KINDS)], (read, decode)
+
+
+def face_list(n):
+    return jnp.minimum(n, FACE - 1)
+
+
+FACES = (face_list, lambda n: n)
 
 
 def live_parts(fill, visit, other):
@@ -425,7 +438,7 @@
         add_block(total, after, CELL, there)
 
     trips, item = cell_list(plan, part)
-    in_turns(trips, SIZES, item, None, products, weights, slot_a, slot_b)
+    in_turns(trips, SIZES, item, products, weights, slot_a, slot_b)
 
     if part:
         make_face_first(faces, face_first)
@@ -447,7 +460,7 @@
                 add_block(total, c, CELL, added)
 
         in_turns(
-            [FACE // 2], [WIDTH], lambda i: i, FACE, face_products, face_weights, slot_a, slot_b
+            [FACE // 2], [WIDTH], FACES, face_products, face_weights, slot_a, slot_b
         )
 
     fold(total, own, rho, carried)
@@ -512,7 +525,7 @@
             set_block(there_of, slot, CELL, there)
 
     trips, item = pair_list(plan)
-    in_turns(trips, SIZES, item, None, products, weights, slot_a, slot_b)
+    in_turns(trips, SIZES, item, products, weights, slot_a, slot_b)
 
     def send(e, part):
         start = (e * SLOTS + 8 * part) * CELL
@@ -574,20 +587,14 @@
     density[...] = rho
     term[...] = jnp.where(full, GAMMA_LESS * energy[...] / jnp.where(full, rho, 1.0), 0.0)
 
-    def cell_step(c, _):
-        moving[c] = jnp.concatenate(
-            [line(own, c, CELL, k) for k in (5, 6, 7)] + [term[pl.ds(c, 1), :]], 0
-        )
-        return 0
-
-    lax.fori_loop(0, CELLS, cell_step, 0, unroll=8)
+    put(moving, planes_of(own, (5, 6, 7), 0, CELLS, CELL) + [term[...]], 0, CELLS, CELL)
 
     def send_step(e, _):
         for s in range(SLOTS):
-            cell = moving[pair[e, s]]
+            cell = pl.ds(pl.multiple_of(pair[e, s] * CELL, CELL), MOVING)
             for h in range(2):
                 at = (h * SLOTS + s) * MOVING
-                out[e, at : at + MOVING] = half(cell, h)
+                out[e, at : at + MOVING] = moving[h, cell, :]
         return 0
 
     lax.fori_loop(0, PEERS, send_step, 0)
@@ -606,7 +613,7 @@
         ],
         scratch_shapes=[
             pltpu.VMEM((CELLS, WIDTH), F32),
-            pltpu.VMEM((CELLS, MOVING, WIDTH), F32),
+            pltpu.VMEM((2, CELLS * CELL, 128), F32),
             pltpu.SemaphoreType.DMA((1,)),
         ]
         + [pltpu.VMEM((CELLS, 128), F32)] * 4,
@@ -676,36 +683,37 @@
     return slope_sums(rows, high[0:count], low[0:count], NT)
 
 
-def in_three_turns(trips, sizes, item, last, products, tiles, sums, slot_a, slot_b, lag):
-    products(item(0), slot_a)
+def in_three_turns(trips, sizes, item, products, tiles, sums, slot_a, slot_b, lag):
+    read, decode = item
+    products(decode(read(0)), slot_a)
     base = 0
+    held = tuple(read(n) for n in range(-2, 3))
     for count, size in zip(trips, sizes):
 
-        def step(i, _, size=size):
-            after = 2 * i + 2
-            if last is not None:
-                after = jnp.minimum(after, last - 1)
+        def step(i, held, size=size):
+            ahead = (read(2 * i + 3), read(2 * i + 4))
+            before, last, now, then, after = [decode(entry) for entry in held]
             if lag == 1:
-                sums(size, item(2 * i - 1), slot_b)
-                tiles(size, item(2 * i), slot_a)
-                products(item(2 * i + 1), slot_b)
-                sums(size, item(2 * i), slot_a)
-                tiles(size, item(2 * i + 1), slot_b)
-                products(item(after), slot_a)
+                sums(size, last, slot_b)
+                tiles(size, now, slot_a)
+                products(then, slot_b)
+                sums(size, now, slot_a)
+                tiles(size, then, slot_b)
+                products(after, slot_a)
             else:
-                products(item(2 * i + 1), slot_b)
-                sums(size, item(2 * i - 2), slot_a)
-                tiles(size, item(2 * i), slot_a)
-                products(item(after), slot_a)
-                sums(size, item(2 * i - 1), slot_b)
-                tiles(size, item(2 * i + 1), slot_b)
-            return 0
-
-        lax.fori_loop(base, base + count, step, 0)
+                products(then, slot_b)
+                sums(size, before, slot_a)
+                tiles(size, now, slot_a)
+                products(after, slot_a)
+                sums(size, last, slot_b)
+                tiles(size, then, slot_b)
+            return held[2:] + ahead
+
+        held = lax.fori_loop(base, base + count, step, held)
         base = base + count
     if lag == 2:
-        sums(sizes[-1], item(2 * base - 2), slot_a)
-    sums(sizes[-1], item(2 * base - 1), slot_b)
+        sums(sizes[-1], decode(held[0]), slot_a)
+    sums(sizes[-1], decode(held[1]), slot_b)
 
 
 def clear(slots):
@@ -752,7 +760,7 @@
         add_block(total, after, SUMS, to_seconds(mine, count, *held[5:7]))
 
     trips, item = cell_list(plan, 2 + part)
-    in_three_turns(trips, SIZES, item, None, products, tiles, sums, slot_a, slot_b, 1)
+    in_three_turns(trips, SIZES, item, products, tiles, sums, slot_a, slot_b, 1)
 
     if part:
         make_face_first(faces, face_first)
@@ -785,7 +793,7 @@
                 )
 
         in_three_turns(
-            [FACE // 2], [WIDTH], lambda i: i, FACE, face_products, face_tiles, face_sums,
+            [FACE // 2], [WIDTH], FACES, face_products, face_tiles, face_sums,
             slot_a, slot_b, 1,
         )
 
@@ -862,7 +870,7 @@
             add_block(total, c, SUMS, added)
 
     trips, item = pair_list(plan)
-    in_three_turns(trips, SIZES, item, None, products, tiles, sums, slot_a, slot_b, 2)
+    in_three_turns(trips, SIZES, item, products, tiles, sums, slot_a, slot_b, 2)
 
     def send(e, part):
         planes = listed_planes(listed, e, part, range(3), ROWS)
@@ -908,7 +916,7 @@
     )(fill, plan, own, first, term, listed, arrived, carried, after)
 
 
-def finish_kernel(pair, near, returned, active_in, own, out, active, gate, sem, *sums):
+def finish_kernel(pair, near, returned, active_in, own, out, active, sem, *sums):
     copies = fetch([(active_in, active)], sem)
     for ref in sums:
         ref[...] = jnp.zeros_like(ref)
@@ -916,26 +924,20 @@
     def peer_step(i, _):
         for s in range(SLOTS):
             for j in range(2):
-                c = pair[2 * i + j, s]
+                cell = pl.ds(pl.multiple_of(pair[2 * i + j, s] * CELL, CELL), MOVING)
                 for h in range(2):
                     at = (h * SLOTS + s) * MOVING
-                    sums[2 * j + h][c] += returned[2 * i + j, at : at + MOVING]
+                    sums[2 * j + h][cell, :] += returned[2 * i + j, at : at + MOVING]
         return 0
 
     lax.fori_loop(0, PEERS // 2, peer_step, 0)
     copies[0].wait()
     full = planes_of(own, [4], 0, CELLS, CELL)[0] > 0.0
-    gate[...] = jnp.where(full, active[...].astype(F32), 0.0)
-
-    def cell_step(c, _):
-        one = pl.ds(c, 1)
-        open_to = gate[one, :]
-        total = both(lambda h: sums[h][c] + sums[2 + h][c])
-        for k in range(4):
-            out[k, one, :] = (near[k, one, :] + total[k : k + 1]) * open_to
-        return 0
-
-    lax.fori_loop(0, CELLS, cell_step, 0, unroll=8)
+    gate = jnp.where(full, active[...].astype(F32), 0.0)
+    for k in range(4):
+        at = pl.ds(k, CELLS, stride=CELL)
+        total = both(lambda h: sums[h][at, :] + sums[2 + h][at, :])
+        out[k] = (near[k] + total) * gate
 
 
 def finish(pair, near, returned, active, own):
@@ -946,10 +948,9 @@
         out_shape=jax.ShapeDtypeStruct((4, CELLS, WIDTH), F32),
         scratch_shapes=[
             pltpu.VMEM((CELLS, WIDTH), jnp.int32),
-            pltpu.VMEM((CELLS, WIDTH), F32),
             pltpu.SemaphoreType.DMA((1,)),
         ]
-        + [pltpu.VMEM((CELLS, MOVING, 128), F32)] * 4,
+        + [pltpu.VMEM((CELLS * CELL, 128), F32)] * 4,
         compiler_params=params(),
     )(pair, near, returned, active, own)
 

time: 139 us -> 138 us (level); the launches traced: 138 us -> 135 us
  starting transfers between devices: 36.3 us -> 33.3 us
  Pallas kernels: 93.6 us -> 95.7 us
  waiting for transfers between devices: 5.3 us -> 3.26 us
    all_to_all x4, starting transfers between devices: 31.1 us -> 28.1 us  [to_peers(): return lax.all_to_all(block, 'dev', split_axis=0, concat_axis=0, tiled=True)]
    all_to_all x4, waiting for transfers between devices: 5.29 us -> 3.25 us  [to_peers(): return lax.all_to_all(block, 'dev', split_axis=0, concat_axis=0, tiled=True)]
  transfers between devices with their start and end apart: 8 -> 8, of which waited for: 3 -> 2; matrix products, arithmetic and copies ran while one was open for 0% -> 0% of each run, Pallas kernels for 49% -> 51%
where the time goes in v9:
time: 138 us; the launch traced here: 135 us
  Pallas kernels  95.7 us (69%)
  starting transfers between devices  33.3 us (24%)
  waiting for transfers between devices  3.26 us (2%)
  local copies, waits for them, and re-layouts  2.04 us (1%)
    all_to_all x4, starting transfers between devices, to_peers(): return lax.all_to_all(block, 'dev', split_axis=0, concat_axis=0, tiled=True)  28.1 us
    pallas_call x2, Pallas kernels, local_force(): pl.pallas_call(functools.partial(local_force_kernel, part), in_specs=[SM]...  28.1 us
    pallas_call x2, Pallas kernels, local_density(): pl.pallas_call(functools.partial(local_density_kernel, part), in_specs=in...  26.2 us
    pallas_call x1, Pallas kernels, cross_force(): pl.pallas_call(cross_force_kernel, in_specs=[SM, SM] + [VM] * 6 + [ANYWHE...  18.7 us
    pallas_call x1, Pallas kernels, cross_density(): pl.pallas_call(cross_density_kernel, in_specs=[SM, SM] + [VM] * 4, out_sp...  14.3 us
    ppermute x2, starting transfers between devices, with_neighbours(): lax.ppermute(rows[..., :FACE * size, :], 'region', down)  5.13 us
    pallas_call x1, Pallas kernels, prepare(): pl.pallas_call(prepare_kernel, in_specs=[SM] * 2 + [ANYWHERE] * 4, out_sp...  3.66 us
    all_to_all x4, waiting for transfers between devices, to_peers(): return lax.all_to_all(block, 'dev', split_axis=0, concat_axis=0, tiled=True)  3.25 us
  transfers between devices with their start and end apart: 8, of which 2 were waited for; matrix products, arithmetic and copies ran while one was open for 0% of the time, Pallas kernels for 51%

profile of v9, /device:TPU:0, one launch (start us, length us, event | category | flops | bytes accessed | tf_op | source)
XLA Modules:
  0.0 135.3 jit_solution(823797500020692065)
XLA Ops:
  0.6 3.7 %shard_map.113 = (f32[2,520,128]{2,1,0:T(8,128)}, f32[16,160,128]{2,1,0:T(8,128)}) custom-call(s32[64]{0:T(128)} %refs_0_.1, s32[16,16]{1,0:T(8,128)} %bitcast.2, f32[3,64,256]{2,1,0:T(8,128)} %pos_in.1, f32[3,64,256]{2,1,0:T(8,128)} %vel_in.1, f32[64,256]{1,0:T(8,128)} %smooth_in.1, f32[64,256]{1,0:T(8,128)} %mass_in.1), custom_call_target="tpu_custom_call" | custom-call | tf_op jit(solution)/shard_map/pallas_call | solution.py:248
  4.3 0.0 copy-start.7
  4.3 0.0 copy-start.8
  4.3 0.0 copy-start.9
  4.3 8.1 %all-to-all-start = ((f32[16,160,128]{2,1,0:T(8,128)}), f32[16,160,128]{2,1,0:T(8,128)S(1)}, u32[]{:S(2)}, u32[]{:S(2)}) async-start(f32[16,160,128]{2,1,0:T(8,128)} %get-tuple-element.19), calls=%async_computation | async-start | bytes 2621440 | tf_op jit(solution)/shard_map/all_to_all | solution.py:959
  12.5 2.2 %collective-permute-start.1 = (f32[2,32,128]{2,1,0:T(8,128)S(1)}, f32[2,32,128]{2,1,0:T(8,128)S(1)}, u32[]{:S(2)}, u32[]{:S(2)}) collective-permute-start(f32[2,32,128]{2,1,0:T(8,128)S(1)} %get-tuple-element.28), channel_id=1, source_target_pairs={{0,112},{16,0},{32,16},{48,32},{64,48},{80,64},{96,80},{112,96},{1... | collective-permute-start | bytes 98312 | tf_op jit(solution)/shard_map/ppermute | solution.py:969
  14.7 17.5 %shard_map.114 = (f32[64,256]{1,0:T(8,128)S(1)}, f32[2,520,128]{2,1,0:T(8,128)S(1)}, f32[2,520,128]{2,1,0:T(8,128)S(1)}, s32[612]{0:T(1024)S(1)}) custom-call(s32[64]{0:T(128)S(1)} %copy-done.8, s32[1,16]{1,0:T(1,128)S(1)} %copy-done.7, s32[16,16]{1,0:T(8,128)S(1)} %bitcast.5, f32[2,520,128]{2,1,0:T(8,128)S(1)} %copy-done), custom_call_target="tpu_custom_call" | custom-call | flops 251658240 | bytes 2097152 | tf_op jit(solution)/shard_map/pallas_call | solution.py:479
  32.2 1.0 all-to-all-done.listed
  33.3 14.3 %shard_map.115 = (f32[64,256]{1,0:T(8,128)S(1)}, f32[16,16,256]{2,1,0:T(8,128)}) custom-call(s32[1,16]{1,0:T(1,128)S(1)} %copy-done.7, s32[612]{0:T(1024)S(1)} %get-tuple-element.16.plan.refs_0_, f32[2,520,128]{2,1,0:T(8,128)S(1)} %copy-done, f32[2,520,128]{2,1,0:T(8,128)S(1)} %get-tuple-element.17.first.refs_2_, f32[16,160,128]{2,1,0:T(8,128)S(1)} %all-to-all-done.listed, ...), custom_call_target="tpu_custom_call" | custom-call | flops 314572800 | bytes 2097152 | tf_op jit(solution)/shard_map/pallas_call | solution.py:545
  47.6 5.8 %all-to-all-start.1 = ((f32[16,16,256]{2,1,0:T(8,128)}), f32[16,16,256]{2,1,0:T(8,128)S(1)}, u32[]{:S(2)}, u32[]{:S(2)}) async-start(f32[16,16,256]{2,1,0:T(8,128)} %get-tuple-element.22), calls=%async_computation.1 | async-start | bytes 524288 | tf_op jit(solution)/shard_map/all_to_all | solution.py:959
  53.4 8.7 %shard_map.116.near = f32[64,256]{1,0:T(8,128)S(1)} custom-call(s32[612]{0:T(1024)S(1)} %get-tuple-element.16.plan.refs_0_, f32[2,520,128]{2,1,0:T(8,128)S(1)} %copy-done, f32[2,520,128]{2,1,0:T(8,128)S(1)} %get-tuple-element.17.first.refs_2_, f32[2,520,128]{2,1,0:T(8,128)S(1)} %get-tuple-element.18.refs_3_.second, ...), custom_call_target="tpu_custom_call" | custom-call | flops 251658240 | bytes 2097152 | tf_op jit(solution)/shard_map/pallas_call | solution.py:479
  62.2 2.5 %shard_map.117 = (f32[64,256]{1,0:T(8,128)}, f32[64,256]{1,0:T(8,128)S(1)}, f32[16,128,128]{2,1,0:T(8,128)S(1)}) custom-call(s32[16,16]{1,0:T(8,128)S(1)} %bitcast.3, f32[64,256]{1,0:T(8,128)S(1)} %shard_map.116.near, f32[16,16,256]{2,1,0:T(8,128)S(1)} %all-to-all-done.1.returned, f32[64,256]{1,0:T(8,128)S(1)} %copy-done.5, f32[2,520,128]{2,1,0:T(8,128)S(1)} %copy-done), custom_call_target="tpu_custom_call" | custom-call | tf_op jit(solution)/shard_map/pallas_call | solution.py:605
  64.7 1.0 copy-done.2
  65.7 7.2 %all-to-all-start.2 = ((f32[16,128,128]{2,1,0:T(8,128)}), f32[16,128,128]{2,1,0:T(8,128)S(1)}, u32[]{:S(2)}, u32[]{:S(2)}) async-start(f32[16,128,128]{2,1,0:T(8,128)} %copy-done.2), calls=%async_computation.2 | async-start | bytes 2097152 | tf_op jit(solution)/shard_map/all_to_all | solution.py:959
  72.8 0.0 collective-permute-start.2
  72.8 2.9 %collective-permute-start.3 = (f32[4,256]{1,0:T(4,128)S(1)}, f32[4,256]{1,0:T(4,128)S(1)}, u32[]{:S(2)}, u32[]{:S(2)}) collective-permute-start(f32[4,256]{1,0:T(4,128)S(1)} %get-tuple-element.31), channel_id=1, source_target_pairs={{0,112},{16,0},{32,16},{48,32},{64,48},{80,64},{96,80},{112,96},{1... | collective-permute-start | bytes 12296 | tf_op jit(solution)/shard_map/ppermute | solution.py:969
  75.8 15.7 %shard_map.118.carried = f32[4,64,256]{2,1,0:T(8,128)S(1)} custom-call(s32[612]{0:T(1024)S(1)} %get-tuple-element.16.plan.refs_0_, f32[2,520,128]{2,1,0:T(8,128)S(1)} %copy-done, f32[2,520,128]{2,1,0:T(8,128)S(1)} %get-tuple-element.17.first.refs_2_, f32[2,520,128]{2,1,0:T(8,128)S(1)} %get-tuple-element.18.refs_3_.second, f32[64,256]{1,0:T(8,128)S(1)} %get-tuple-element.24.term), custom_call_target="tpu_custom_call" | custom-call | flops 335544320 | bytes 2097152 | tf_op jit(solution)/shard_map/pallas_call | solution.py:819
  91.6 18.7 %shard_map.119 = (f32[4,64,256]{2,1,0:T(8,128)S(1)}, f32[16,128,128]{2,1,0:T(8,128)S(1)}) custom-call(s32[1,16]{1,0:T(1,128)S(1)} %copy-done.7, s32[612]{0:T(1024)S(1)} %get-tuple-element.16.plan.refs_0_, f32[2,520,128]{2,1,0:T(8,128)S(1)} %copy-done, f32[2,520,128]{2,1,0:T(8,128)S(1)} %get-tuple-element.17.first.refs_2_, ...), custom_call_target="tpu_custom_call" | custom-call | flops 419430400 | bytes 2097152 | tf_op jit(solution)/shard_map/pallas_call | solution.py:896
  110.3 1.0 copy-done.3
  111.3 7.0 %all-to-all-start.3 = ((f32[16,128,128]{2,1,0:T(8,128)}), f32[16,128,128]{2,1,0:T(8,128)S(1)}, u32[]{:S(2)}, u32[]{:S(2)}) async-start(f32[16,128,128]{2,1,0:T(8,128)} %copy-done.3), calls=%async_computation.3 | async-start | bytes 2097152 | tf_op jit(solution)/shard_map/all_to_all | solution.py:959
  118.3 0.0 copy-start.6
  118.3 12.3 %shard_map.120.near = f32[4,64,256]{2,1,0:T(8,128)S(1)} custom-call(s32[612]{0:T(1024)S(1)} %get-tuple-element.16.plan.refs_0_, f32[2,520,128]{2,1,0:T(8,128)S(1)} %copy-done, f32[2,520,128]{2,1,0:T(8,128)S(1)} %get-tuple-element.17.first.refs_2_, f32[2,520,128]{2,1,0:T(8,128)S(1)} %get-tuple-element.18.refs_3_.second, ...), custom_call_target="tpu_custom_call" | custom-call | flops 335544320 | bytes 2097152 | tf_op jit(solution)/shard_map/pallas_call | solution.py:819
  130.6 2.2 %all-to-all-done.3.returned = f32[16,128,128]{2,1,0:T(8,128)S(1)} async-done(((f32[16,128,128]{2,1,0:T(8,128)}), f32[16,128,128]{2,1,0:T(8,128)S(1)}, u32[]{:S(2)}, u32[]{:S(2)}) %all-to-all-start.3) | async-done | bytes 1048608 | tf_op jit(solution)/shard_map/all_to_all | solution.py:959
  132.9 2.3 %shard_map.121 = f32[4,64,256]{2,1,0:T(8,128)} custom-call(s32[16,16]{1,0:T(8,128)S(1)} %bitcast.4, f32[4,64,256]{2,1,0:T(8,128)S(1)} %shard_map.120.near, f32[16,128,128]{2,1,0:T(8,128)S(1)} %all-to-all-done.3.returned, s32[64,256]{1,0:T(8,128)S(1)} %copy-done.6, f32[2,520,128]{2,1,0:T(8,128)S(1)} %copy-done), custom_call_target="tpu_custom_call" | custom-call | tf_op jit(solution)/shard_map/pallas_call | solution.py:944
  (26 shorter events, 0.1 us)
Async XLA Ops:
  4.3 8.2 %copy-start = (f32[2,520,128]{2,1,0:T(8,128)S(1)}, f32[2,520,128]{2,1,0:T(8,128)}, u32[]{:S(2)}) copy-start(f32[2,520,128]{2,1,0:T(8,128)} %get-tuple-element.15.refs_3_.own.refs_1_) | copy-start | bytes 1597444
  4.3 10.4 %copy-start.7 = (s32[1,16]{1,0:T(1,128)S(1)}, s32[1,16]{1,0:T(1,128)}, u32[]{:S(2)}) copy-start(s32[1,16]{1,0:T(1,128)} %fill.3) | copy-start | bytes 196
  4.3 10.4 %copy-start.8 = (s32[64]{0:T(128)S(1)}, s32[64]{0:T(128)}, u32[]{:S(2)}) copy-start(s32[64]{0:T(128)} %refs_0_.1) | copy-start | bytes 772
  4.3 10.4 %copy-start.9 = (s32[1,16,16]{2,1,0:T(8,128)S(1)}, s32[1,16,16]{2,1,0:T(8,128)}, u32[]{:S(2)}) copy-start(s32[1,16,16]{2,1,0:T(8,128)} %param.17) | copy-start | bytes 3076
  4.3 28.9 %all-to-all-start = ((f32[16,160,128]{2,1,0:T(8,128)}), f32[16,160,128]{2,1,0:T(8,128)S(1)}, u32[]{:S(2)}, u32[]{:S(2)}) async-start(f32[16,160,128]{2,1,0:T(8,128)} %get-tuple-element.19), calls=%async_computation | async-start | bytes 2621440 | tf_op jit(solution)/shard_map/all_to_all | solution.py:959
  12.5 40.9 %collective-permute-start.1 = (f32[2,32,128]{2,1,0:T(8,128)S(1)}, f32[2,32,128]{2,1,0:T(8,128)S(1)}, u32[]{:S(2)}, u32[]{:S(2)}) collective-permute-start(f32[2,32,128]{2,1,0:T(8,128)S(1)} %get-tuple-element.28), channel_id=1, source_target_pairs={{0,112},{16,0},{32,16},{48,32},{64,48},{80,64},{96,80},{112,96},{1... | collective-permute-start | bytes 98312 | tf_op jit(solution)/shard_map/ppermute | solution.py:969
  14.7 38.7 %collective-permute-start = (f32[2,32,128]{2,1,0:T(8,128)S(1)}, f32[2,32,128]{2,1,0:T(8,128)S(1)}, u32[]{:S(2)}, u32[]{:S(2)}) collective-permute-start(f32[2,32,128]{2,1,0:T(8,128)S(1)} %get-tuple-element.29), channel_id=1, source_target_pairs={{0,16},{16,32},{32,48},{48,64},{64,80},{80,96},{96,112},{112,0},{1... | collective-permute-start | bytes 98312 | tf_op jit(solution)/shard_map/ppermute | solution.py:968
  33.3 14.3 %copy-start.1 = (f32[16,160,128]{2,1,0:T(8,128)}, f32[16,160,128]{2,1,0:T(8,128)S(1)}, u32[]{:S(2)}) copy-start(f32[16,160,128]{2,1,0:T(8,128)S(1)} %all-to-all-done.listed) | copy-start | bytes 3932164
  47.6 14.6 %copy-start.4 = (s32[1,16,16]{2,1,0:T(8,128)S(1)}, s32[1,16,16]{2,1,0:T(8,128)}, u32[]{:S(2)}) copy-start(s32[1,16,16]{2,1,0:T(8,128)} %param.19) | copy-start | bytes 3076
  47.6 14.6 %copy-start.5 = (f32[64,256]{1,0:T(8,128)S(1)}, f32[64,256]{1,0:T(8,128)}, u32[]{:S(2)}) copy-start(f32[64,256]{1,0:T(8,128)} %energy_in.1) | copy-start | bytes 196612
  47.6 14.6 %all-to-all-start.1 = ((f32[16,16,256]{2,1,0:T(8,128)}), f32[16,16,256]{2,1,0:T(8,128)S(1)}, u32[]{:S(2)}, u32[]{:S(2)}) async-start(f32[16,16,256]{2,1,0:T(8,128)} %get-tuple-element.22), calls=%async_computation.1 | async-start | bytes 524288 | tf_op jit(solution)/shard_map/all_to_all | solution.py:959
  64.7 1.0 copy-start.2
  65.7 25.9 %all-to-all-start.2 = ((f32[16,128,128]{2,1,0:T(8,128)}), f32[16,128,128]{2,1,0:T(8,128)S(1)}, u32[]{:S(2)}, u32[]{:S(2)}) async-start(f32[16,128,128]{2,1,0:T(8,128)} %copy-done.2), calls=%async_computation.2 | async-start | bytes 2097152 | tf_op jit(solution)/shard_map/all_to_all | solution.py:959
  72.8 18.7 %collective-permute-start.2 = (f32[4,256]{1,0:T(4,128)S(1)}, f32[4,256]{1,0:T(4,128)S(1)}, u32[]{:S(2)}, u32[]{:S(2)}) collective-permute-start(f32[4,256]{1,0:T(4,128)S(1)} %get-tuple-element.30), channel_id=1, source_target_pairs={{0,16},{16,32},{32,48},{48,64},{64,80},{80,96},{96,112},{112,0},{1... | collective-permute-start | bytes 12296 | tf_op jit(solution)/shard_map/ppermute | solution.py:968
  72.8 18.7 %collective-permute-start.3 = (f32[4,256]{1,0:T(4,128)S(1)}, f32[4,256]{1,0:T(4,128)S(1)}, u32[]{:S(2)}, u32[]{:S(2)}) collective-permute-start(f32[4,256]{1,0:T(4,128)S(1)} %get-tuple-element.31), channel_id=1, source_target_pairs={{0,112},{16,0},{32,16},{48,32},{64,48},{80,64},{96,80},{112,96},{1... | collective-permute-start | bytes 12296 | tf_op jit(solution)/shard_map/ppermute | solution.py:969
  110.3 1.0 copy-start.3
  111.3 21.6 %all-to-all-start.3 = ((f32[16,128,128]{2,1,0:T(8,128)}), f32[16,128,128]{2,1,0:T(8,128)S(1)}, u32[]{:S(2)}, u32[]{:S(2)}) async-start(f32[16,128,128]{2,1,0:T(8,128)} %copy-done.3), calls=%async_computation.3 | async-start | bytes 2097152 | tf_op jit(solution)/shard_map/all_to_all | solution.py:959
  118.3 14.5 %copy-start.6 = (s32[64,256]{1,0:T(8,128)S(1)}, s32[64,256]{1,0:T(8,128)}, u32[]{:S(2)}) copy-start(s32[64,256]{1,0:T(8,128)} %active_in.1) | copy-start | bytes 196612

commit v10 on v9

--- a/solution.py
+++ b/solution.py
@@ -30,7 +30,7 @@
 SM = pl.BlockSpec(memory_space=pltpu.SMEM)
 ROWS = 5
 MOVING = 4
-SPLITS = (44, 40)
+SPLITS = (44, 36)
 SIZES = (160, 192, 224, 256)
 KINDS = len(SIZES)
 UNIT = 4

time: 138 us -> 137 us (level)
  starting transfers between devices: 33.3 us -> 36.4 us
  Pallas kernels: 95.7 us -> 93.4 us
    all_to_all x4, starting transfers between devices: 28.1 us -> 31.3 us  [to_peers(): return lax.all_to_all(block, 'dev', split_axis=0, concat_axis=0, tiled=True)]
  transfers between devices with their start and end apart: 8 -> 8, of which waited for: 2 -> 3; matrix products, arithmetic and copies ran while one was open for 0% -> 0% of each run, Pallas kernels for 51% -> 50%
where the time goes in v10:
time: 137 us; the launch traced here: 136 us
  Pallas kernels  93.4 us (68%)
  starting transfers between devices  36.4 us (27%)
  waiting for transfers between devices  2.61 us (2%)
  local copies, waits for them, and re-layouts  2.04 us (1%)
    all_to_all x4, starting transfers between devices, to_peers(): return lax.all_to_all(block, 'dev', split_axis=0, concat_axis=0, tiled=True)  31.3 us
    pallas_call x2, Pallas kernels, local_force(): pl.pallas_call(functools.partial(local_force_kernel, part), in_specs=[SM]...  28.1 us
    pallas_call x2, Pallas kernels, local_density(): pl.pallas_call(functools.partial(local_density_kernel, part), in_specs=in...  26.1 us
    pallas_call x1, Pallas kernels, cross_force(): pl.pallas_call(cross_force_kernel, in_specs=[SM, SM] + [VM] * 6 + [ANYWHE...  17.5 us
    pallas_call x1, Pallas kernels, cross_density(): pl.pallas_call(cross_density_kernel, in_specs=[SM, SM] + [VM] * 4, out_sp...  13.2 us
    ppermute x2, starting transfers between devices, with_neighbours(): lax.ppermute(rows[..., :FACE * size, :], 'region', down)  5.13 us
    pallas_call x1, Pallas kernels, prepare(): pl.pallas_call(prepare_kernel, in_specs=[SM] * 2 + [ANYWHERE] * 4, out_sp...  3.66 us
  transfers between devices with their start and end apart: 8, of which 3 were waited for; matrix products, arithmetic and copies ran while one was open for 0% of the time, Pallas kernels for 50%

profile of v10, /device:TPU:0, one launch (start us, length us, event | category | flops | bytes accessed | tf_op | source)
XLA Modules:
  0.0 135.6 jit_solution(10428600413112340200)
XLA Ops:
  0.6 3.7 %shard_map.113 = (f32[2,520,128]{2,1,0:T(8,128)}, f32[16,160,128]{2,1,0:T(8,128)}) custom-call(s32[64]{0:T(128)} %refs_0_.1, s32[16,16]{1,0:T(8,128)} %bitcast.2, f32[3,64,256]{2,1,0:T(8,128)} %pos_in.1, f32[3,64,256]{2,1,0:T(8,128)} %vel_in.1, f32[64,256]{1,0:T(8,128)} %smooth_in.1, f32[64,256]{1,0:T(8,128)} %mass_in.1), custom_call_target="tpu_custom_call" | custom-call | tf_op jit(solution)/shard_map/pallas_call | solution.py:248
  4.3 0.0 copy-start.8
  4.3 0.0 copy-start.9
  4.3 8.1 %all-to-all-start = ((f32[16,160,128]{2,1,0:T(8,128)}), f32[16,160,128]{2,1,0:T(8,128)S(1)}, u32[]{:S(2)}, u32[]{:S(2)}) async-start(f32[16,160,128]{2,1,0:T(8,128)} %get-tuple-element.19), calls=%async_computation | async-start | bytes 2621440 | tf_op jit(solution)/shard_map/all_to_all | solution.py:959
  12.5 2.2 %collective-permute-start.1 = (f32[2,32,128]{2,1,0:T(8,128)S(1)}, f32[2,32,128]{2,1,0:T(8,128)S(1)}, u32[]{:S(2)}, u32[]{:S(2)}) collective-permute-start(f32[2,32,128]{2,1,0:T(8,128)S(1)} %get-tuple-element.28), channel_id=1, source_target_pairs={{0,112},{16,0},{32,16},{48,32},{64,48},{80,64},{96,80},{112,96},{1... | collective-permute-start | bytes 98312 | tf_op jit(solution)/shard_map/ppermute | solution.py:969
  14.7 17.6 %shard_map.114 = (f32[64,256]{1,0:T(8,128)S(1)}, f32[2,520,128]{2,1,0:T(8,128)S(1)}, f32[2,520,128]{2,1,0:T(8,128)S(1)}, s32[612]{0:T(1024)S(1)}) custom-call(s32[64]{0:T(128)S(1)} %copy-done.8, s32[1,16]{1,0:T(1,128)S(1)} %copy-done.7, s32[16,16]{1,0:T(8,128)S(1)} %bitcast.5, f32[2,520,128]{2,1,0:T(8,128)S(1)} %copy-done), custom_call_target="tpu_custom_call" | custom-call | flops 251658240 | bytes 2097152 | tf_op jit(solution)/shard_map/pallas_call | solution.py:479
  32.3 1.0 all-to-all-done.listed
  33.3 13.2 %shard_map.115 = (f32[64,256]{1,0:T(8,128)S(1)}, f32[16,16,256]{2,1,0:T(8,128)}) custom-call(s32[1,16]{1,0:T(1,128)S(1)} %copy-done.7, s32[612]{0:T(1024)S(1)} %get-tuple-element.16.plan.refs_0_, f32[2,520,128]{2,1,0:T(8,128)S(1)} %copy-done, f32[2,520,128]{2,1,0:T(8,128)S(1)} %get-tuple-element.17.first.refs_2_, f32[16,160,128]{2,1,0:T(8,128)S(1)} %all-to-all-done.listed, ...), custom_call_target="tpu_custom_call" | custom-call | flops 314572800 | bytes 2097152 | tf_op jit(solution)/shard_map/pallas_call | solution.py:545
  46.5 7.5 %all-to-all-start.1 = ((f32[16,16,256]{2,1,0:T(8,128)}), f32[16,16,256]{2,1,0:T(8,128)S(1)}, u32[]{:S(2)}, u32[]{:S(2)}) async-start(f32[16,16,256]{2,1,0:T(8,128)} %get-tuple-element.22), calls=%async_computation.1 | async-start | bytes 524288 | tf_op jit(solution)/shard_map/all_to_all | solution.py:959
  54.0 8.5 %shard_map.116.near = f32[64,256]{1,0:T(8,128)S(1)} custom-call(s32[612]{0:T(1024)S(1)} %get-tuple-element.16.plan.refs_0_, f32[2,520,128]{2,1,0:T(8,128)S(1)} %copy-done, f32[2,520,128]{2,1,0:T(8,128)S(1)} %get-tuple-element.17.first.refs_2_, f32[2,520,128]{2,1,0:T(8,128)S(1)} %get-tuple-element.18.refs_3_.second, ...), custom_call_target="tpu_custom_call" | custom-call | flops 251658240 | bytes 2097152 | tf_op jit(solution)/shard_map/pallas_call | solution.py:479
  62.5 0.1 all-to-all-done.1.returned
  62.6 2.5 %shard_map.117 = (f32[64,256]{1,0:T(8,128)}, f32[64,256]{1,0:T(8,128)S(1)}, f32[16,128,128]{2,1,0:T(8,128)S(1)}) custom-call(s32[16,16]{1,0:T(8,128)S(1)} %bitcast.3, f32[64,256]{1,0:T(8,128)S(1)} %shard_map.116.near, f32[16,16,256]{2,1,0:T(8,128)S(1)} %all-to-all-done.1.returned, f32[64,256]{1,0:T(8,128)S(1)} %copy-done.5, f32[2,520,128]{2,1,0:T(8,128)S(1)} %copy-done), custom_call_target="tpu_custom_call" | custom-call | tf_op jit(solution)/shard_map/pallas_call | solution.py:605
  65.1 1.0 copy-done.2
  66.1 7.3 %all-to-all-start.2 = ((f32[16,128,128]{2,1,0:T(8,128)}), f32[16,128,128]{2,1,0:T(8,128)S(1)}, u32[]{:S(2)}, u32[]{:S(2)}) async-start(f32[16,128,128]{2,1,0:T(8,128)} %copy-done.2), calls=%async_computation.2 | async-start | bytes 2097152 | tf_op jit(solution)/shard_map/all_to_all | solution.py:959
  73.4 0.0 collective-permute-start.2
  73.4 2.9 %collective-permute-start.3 = (f32[4,256]{1,0:T(4,128)S(1)}, f32[4,256]{1,0:T(4,128)S(1)}, u32[]{:S(2)}, u32[]{:S(2)}) collective-permute-start(f32[4,256]{1,0:T(4,128)S(1)} %get-tuple-element.31), channel_id=1, source_target_pairs={{0,112},{16,0},{32,16},{48,32},{64,48},{80,64},{96,80},{112,96},{1... | collective-permute-start | bytes 12296 | tf_op jit(solution)/shard_map/ppermute | solution.py:969
  76.4 14.6 %shard_map.118.carried = f32[4,64,256]{2,1,0:T(8,128)S(1)} custom-call(s32[612]{0:T(1024)S(1)} %get-tuple-element.16.plan.refs_0_, f32[2,520,128]{2,1,0:T(8,128)S(1)} %copy-done, f32[2,520,128]{2,1,0:T(8,128)S(1)} %get-tuple-element.17.first.refs_2_, f32[2,520,128]{2,1,0:T(8,128)S(1)} %get-tuple-element.18.refs_3_.second, f32[64,256]{1,0:T(8,128)S(1)} %get-tuple-element.24.term), custom_call_target="tpu_custom_call" | custom-call | flops 335544320 | bytes 2097152 | tf_op jit(solution)/shard_map/pallas_call | solution.py:819
  91.1 17.5 %shard_map.119 = (f32[4,64,256]{2,1,0:T(8,128)S(1)}, f32[16,128,128]{2,1,0:T(8,128)S(1)}) custom-call(s32[1,16]{1,0:T(1,128)S(1)} %copy-done.7, s32[612]{0:T(1024)S(1)} %get-tuple-element.16.plan.refs_0_, f32[2,520,128]{2,1,0:T(8,128)S(1)} %copy-done, f32[2,520,128]{2,1,0:T(8,128)S(1)} %get-tuple-element.17.first.refs_2_, ...), custom_call_target="tpu_custom_call" | custom-call | flops 419430400 | bytes 2097152 | tf_op jit(solution)/shard_map/pallas_call | solution.py:896
  108.6 1.0 copy-done.3
  109.6 8.4 %all-to-all-start.3 = ((f32[16,128,128]{2,1,0:T(8,128)}), f32[16,128,128]{2,1,0:T(8,128)S(1)}, u32[]{:S(2)}, u32[]{:S(2)}) async-start(f32[16,128,128]{2,1,0:T(8,128)} %copy-done.3), calls=%async_computation.3 | async-start | bytes 2097152 | tf_op jit(solution)/shard_map/all_to_all | solution.py:959
  118.0 0.0 copy-start.6
  118.1 13.5 %shard_map.120.near = f32[4,64,256]{2,1,0:T(8,128)S(1)} custom-call(s32[612]{0:T(1024)S(1)} %get-tuple-element.16.plan.refs_0_, f32[2,520,128]{2,1,0:T(8,128)S(1)} %copy-done, f32[2,520,128]{2,1,0:T(8,128)S(1)} %get-tuple-element.17.first.refs_2_, f32[2,520,128]{2,1,0:T(8,128)S(1)} %get-tuple-element.18.refs_3_.second, ...), custom_call_target="tpu_custom_call" | custom-call | flops 335544320 | bytes 2097152 | tf_op jit(solution)/shard_map/pallas_call | solution.py:819
  131.6 1.5 %all-to-all-done.3.returned = f32[16,128,128]{2,1,0:T(8,128)S(1)} async-done(((f32[16,128,128]{2,1,0:T(8,128)}), f32[16,128,128]{2,1,0:T(8,128)S(1)}, u32[]{:S(2)}, u32[]{:S(2)}) %all-to-all-start.3) | async-done | bytes 1048608 | tf_op jit(solution)/shard_map/all_to_all | solution.py:959
  133.1 2.3 %shard_map.121 = f32[4,64,256]{2,1,0:T(8,128)} custom-call(s32[16,16]{1,0:T(8,128)S(1)} %bitcast.4, f32[4,64,256]{2,1,0:T(8,128)S(1)} %shard_map.120.near, f32[16,128,128]{2,1,0:T(8,128)S(1)} %all-to-all-done.3.returned, s32[64,256]{1,0:T(8,128)S(1)} %copy-done.6, f32[2,520,128]{2,1,0:T(8,128)S(1)} %copy-done), custom_call_target="tpu_custom_call" | custom-call | tf_op jit(solution)/shard_map/pallas_call | solution.py:944
  (26 shorter events, 0.1 us)
Async XLA Ops:
  4.3 8.2 %copy-start = (f32[2,520,128]{2,1,0:T(8,128)S(1)}, f32[2,520,128]{2,1,0:T(8,128)}, u32[]{:S(2)}) copy-start(f32[2,520,128]{2,1,0:T(8,128)} %get-tuple-element.15.refs_3_.own.refs_1_) | copy-start | bytes 1597444
  4.3 10.4 %copy-start.7 = (s32[1,16]{1,0:T(1,128)S(1)}, s32[1,16]{1,0:T(1,128)}, u32[]{:S(2)}) copy-start(s32[1,16]{1,0:T(1,128)} %fill.3) | copy-start | bytes 196
  4.3 10.4 %copy-start.8 = (s32[64]{0:T(128)S(1)}, s32[64]{0:T(128)}, u32[]{:S(2)}) copy-start(s32[64]{0:T(128)} %refs_0_.1) | copy-start | bytes 772
  4.3 10.3 %copy-start.9 = (s32[1,16,16]{2,1,0:T(8,128)S(1)}, s32[1,16,16]{2,1,0:T(8,128)}, u32[]{:S(2)}) copy-start(s32[1,16,16]{2,1,0:T(8,128)} %param.17) | copy-start | bytes 3076
  4.3 28.9 %all-to-all-start = ((f32[16,160,128]{2,1,0:T(8,128)}), f32[16,160,128]{2,1,0:T(8,128)S(1)}, u32[]{:S(2)}, u32[]{:S(2)}) async-start(f32[16,160,128]{2,1,0:T(8,128)} %get-tuple-element.19), calls=%async_computation | async-start | bytes 2621440 | tf_op jit(solution)/shard_map/all_to_all | solution.py:959
  12.5 41.5 %collective-permute-start.1 = (f32[2,32,128]{2,1,0:T(8,128)S(1)}, f32[2,32,128]{2,1,0:T(8,128)S(1)}, u32[]{:S(2)}, u32[]{:S(2)}) collective-permute-start(f32[2,32,128]{2,1,0:T(8,128)S(1)} %get-tuple-element.28), channel_id=1, source_target_pairs={{0,112},{16,0},{32,16},{48,32},{64,48},{80,64},{96,80},{112,96},{1... | collective-permute-start | bytes 98312 | tf_op jit(solution)/shard_map/ppermute | solution.py:969
  14.7 39.3 %collective-permute-start = (f32[2,32,128]{2,1,0:T(8,128)S(1)}, f32[2,32,128]{2,1,0:T(8,128)S(1)}, u32[]{:S(2)}, u32[]{:S(2)}) collective-permute-start(f32[2,32,128]{2,1,0:T(8,128)S(1)} %get-tuple-element.29), channel_id=1, source_target_pairs={{0,16},{16,32},{32,48},{48,64},{64,80},{80,96},{96,112},{112,0},{1... | collective-permute-start | bytes 98312 | tf_op jit(solution)/shard_map/ppermute | solution.py:968
  33.3 13.2 %copy-start.1 = (f32[16,160,128]{2,1,0:T(8,128)}, f32[16,160,128]{2,1,0:T(8,128)S(1)}, u32[]{:S(2)}) copy-start(f32[16,160,128]{2,1,0:T(8,128)S(1)} %all-to-all-done.listed) | copy-start | bytes 3932164
  46.5 16.2 %copy-start.4 = (s32[1,16,16]{2,1,0:T(8,128)S(1)}, s32[1,16,16]{2,1,0:T(8,128)}, u32[]{:S(2)}) copy-start(s32[1,16,16]{2,1,0:T(8,128)} %param.19) | copy-start | bytes 3076
  46.5 16.2 %copy-start.5 = (f32[64,256]{1,0:T(8,128)S(1)}, f32[64,256]{1,0:T(8,128)}, u32[]{:S(2)}) copy-start(f32[64,256]{1,0:T(8,128)} %energy_in.1) | copy-start | bytes 196612
  46.5 16.2 %all-to-all-start.1 = ((f32[16,16,256]{2,1,0:T(8,128)}), f32[16,16,256]{2,1,0:T(8,128)S(1)}, u32[]{:S(2)}, u32[]{:S(2)}) async-start(f32[16,16,256]{2,1,0:T(8,128)} %get-tuple-element.22), calls=%async_computation.1 | async-start | bytes 524288 | tf_op jit(solution)/shard_map/all_to_all | solution.py:959
  65.1 1.0 copy-start.2
  66.1 25.0 %all-to-all-start.2 = ((f32[16,128,128]{2,1,0:T(8,128)}), f32[16,128,128]{2,1,0:T(8,128)S(1)}, u32[]{:S(2)}, u32[]{:S(2)}) async-start(f32[16,128,128]{2,1,0:T(8,128)} %copy-done.2), calls=%async_computation.2 | async-start | bytes 2097152 | tf_op jit(solution)/shard_map/all_to_all | solution.py:959
  73.4 17.6 %collective-permute-start.2 = (f32[4,256]{1,0:T(4,128)S(1)}, f32[4,256]{1,0:T(4,128)S(1)}, u32[]{:S(2)}, u32[]{:S(2)}) collective-permute-start(f32[4,256]{1,0:T(4,128)S(1)} %get-tuple-element.30), channel_id=1, source_target_pairs={{0,16},{16,32},{32,48},{48,64},{64,80},{80,96},{96,112},{112,0},{1... | collective-permute-start | bytes 12296 | tf_op jit(solution)/shard_map/ppermute | solution.py:968
  73.4 17.6 %collective-permute-start.3 = (f32[4,256]{1,0:T(4,128)S(1)}, f32[4,256]{1,0:T(4,128)S(1)}, u32[]{:S(2)}, u32[]{:S(2)}) collective-permute-start(f32[4,256]{1,0:T(4,128)S(1)} %get-tuple-element.31), channel_id=1, source_target_pairs={{0,112},{16,0},{32,16},{48,32},{64,48},{80,64},{96,80},{112,96},{1... | collective-permute-start | bytes 12296 | tf_op jit(solution)/shard_map/ppermute | solution.py:969
  108.6 1.0 copy-start.3
  109.6 23.4 %all-to-all-start.3 = ((f32[16,128,128]{2,1,0:T(8,128)}), f32[16,128,128]{2,1,0:T(8,128)S(1)}, u32[]{:S(2)}, u32[]{:S(2)}) async-start(f32[16,128,128]{2,1,0:T(8,128)} %copy-done.3), calls=%async_computation.3 | async-start | bytes 2097152 | tf_op jit(solution)/shard_map/all_to_all | solution.py:959
  118.0 15.0 %copy-start.6 = (s32[64,256]{1,0:T(8,128)S(1)}, s32[64,256]{1,0:T(8,128)}, u32[]{:S(2)}) copy-start(s32[64,256]{1,0:T(8,128)} %active_in.1) | copy-start | bytes 196612
